TPU v7x, 32 devices: a whole 2x2x4 slice. The times are simulated.
32 devices in a mesh: freq: 8 (over y, x, core), slab: 4 (over z).
Axes of the slice: x: 2, y: 2, z: 4, core: 2. Of those that a mesh axis runs over, the one named last changes fastest.
Arguments:
- fine_model: bfloat16 [512, 2048], P(('freq', 'slab')), may hold values from 0.5 to 2
- resample: bfloat16 [8, 512, 512], P('freq', 'slab'), may hold values from -0.25 to 0.25
- lateral: bfloat16 [2048, 2048], replicated, may hold values from -0.0625 to 0.0625
- shift: float32 [8], P('freq'), may hold values from 0.5 to 4
- source: float32 [8, 512, 2048], P('freq', 'slab'), may hold values from -6 to 6
- receiver: float32 [8, 512, 2048], P('freq', 'slab'), may hold values from -6 to 6
Outputs:
- image: float32 [512, 2048], P(('freq', 'slab'))
All inputs are finite; a program needn't handle non-finite values.
Results may differ from a plain program's by a relative error of at most 0.0029.
Values may be sent and summed in bfloat16 or wider, within the bound.
No kernel may reach another device: no remote copies, remote signals or barrier semaphores. Data moves between devices by JAX's collectives and lax.ppermute only.
A program may use at most 128 MiB of HBM per device.

v0:
```python
import jax
import jax.numpy as jnp
from jax import lax
from jax.sharding import PartitionSpec as P

SWEEPS = 8


def with_halo(value, sides, width):
    for axis, dim in sides:
        size, length = (lax.axis_size(axis), value.shape[dim])
        up = [(i, (i + 1) % size) for i in range(size - 1)]
        down = [(j, i) for i, j in up]
        last = lax.slice_in_dim(value, length - width, length, axis=dim)
        initial = lax.slice_in_dim(value, 0, width, axis=dim)
        before = lax.ppermute(last, axis, up)
        after = lax.ppermute(initial, axis, down)
        value = jnp.concatenate([before, value, after], axis=dim)
    return value


def shards(fine_model, resample, lateral, shift, source, receiver):
    oper = resample[0]
    columns = oper
    coarse = jnp.dot(
        columns,
        lax.all_gather(fine_model, ("freq", "slab"), axis=0, tiled=True),
        preferred_element_type=jnp.float32,
    )
    diag = 4.0 + shift[0] * coarse * coarse
    src = source[0]
    field = jnp.zeros(src.shape, jnp.float32)
    for sweep in range(SWEEPS):
        padded = with_halo(field, (("slab", 0),), 1)
        beside = padded[2:] + padded[:-2]
        side = jnp.dot(field.astype(jnp.bfloat16), lateral, preferred_element_type=jnp.float32)
        field = (src + 0.5 * beside + side) / diag
    partial_img = (field * receiver[0]).astype(jnp.bfloat16)
    columns = oper
    return lax.psum_scatter(
        lax.dot_general(
            columns, partial_img, (((0,), (0,)), ((), ())), preferred_element_type=jnp.float32
        ),
        ("freq", "slab"),
        scatter_dimension=0,
        tiled=True,
    )


def solution(mesh):
    in_specs = (
        P(("freq", "slab"), None),
        P("freq", "slab", None),
        P(),
        P("freq"),
        P("freq", "slab", None),
        P("freq", "slab", None),
    )
    out_specs = P(("freq", "slab"), None)
    return jax.shard_map(shards, mesh=mesh, in_specs=in_specs, out_specs=out_specs, check_vma=False)
```

profile of v0, /device:TPU:0, one launch (start us, length us, event | category | flops | bytes accessed | tf_op | source)
XLA Modules:
  0.0 308.7 jit_solution(4635475144457342962)
XLA Ops:
  6.5 0.0 copy-start
  6.5 0.0 all-gather.2.cloned.1.call-start
  6.5 0.7 all-gather.2.cloned.1.call-update
  7.3 0.0 reduce-scatter.4.cloned.1.call-start
  7.3 4.9 %collective-permute-start.1 = (f32[1,2048]{1,0:T(1,128)S(1)}, f32[1,2048]{1,0:T(1,128)S(1)}, u32[]{:S(2)}, u32[]{:S(2)}) collective-permute-start(f32[1,2048]{1,0:T(1,128)S(1)} %broadcast.12), channel_id=1, source_target_pairs={{0,1},{1,2},{2,3},{4,5},{5,6},{6,7},{8,9},{9,10},{10,11},{12,13},{... | collective-permute-start | bytes 24584 | tf_op jit(solution)/shard_map/ppermute | solution.py:16
  12.3 1.3 collective-permute-start
  14.2 55.3 %all-gather.2.cloned.1.call-done = bf16[512,2048]{1,0:T(8,128)(2,1)} async-done(((bf16[16,2048]{1,0:T(8,128)(2,1)}), bf16[512,2048]{1,0:T(8,128)(2,1)}) %all-gather.2.cloned.1.call-update) | async-done | bytes 2097168 | tf_op jit(solution)/shard_map/all_gather | solution.py:27
  69.5 0.0 copy-done
  69.5 0.0 slice-start
  69.5 2.2 fusion.5
  71.7 0.0 slice-start.1
  71.7 0.0 copy-start.2
  71.7 0.0 collective-permute-done.1
  71.7 0.0 collective-permute-done
  71.7 5.1 %fusion.4 = f32[128,2048]{1,0:T(8,128)S(1)} fusion(f32[128,2048]{1,0:T(8,128)S(1)} %fusion.5, f32[1,2048]{1,0:T(1,128)S(1)} %collective-permute-done, f32[1,2048]{1,0:T(1,128)S(1)} %collective-permute-done.1, f32[1,128,2048]{2,1,0:T(8,128)} %param.10, bf16[2048,2048]{1,0:T(8,128)(2,1)} %param.8), kind=kOutput, calls=%fused_computation.8 | convolution fusion | flops 1075052544 | bytes 11550720 | tf_op jit(solution)/shard_map/dot_general | solution.py:36
  76.9 1.3 collective-permute-start.2
  78.2 4.5 %collective-permute-start.3 = (f32[1,2048]{1,0:T(1,128)S(1)}, f32[1,2048]{1,0:T(1,128)S(1)}, u32[]{:S(2)}, u32[]{:S(2)}) collective-permute-start(f32[1,2048]{1,0:T(1,128)S(1)} %get-tuple-element.18), channel_id=1, source_target_pairs={{0,1},{1,2},{2,3},{4,5},{5,6},{6,7},{8,9},{9,10},{10,11},{12,13},{... | collective-permute-start | bytes 24584 | tf_op jit(solution)/shard_map/ppermute | solution.py:16
  82.7 0.0 collective-permute-done.2
  82.8 1.3 collective-permute-done.3
  84.1 0.0 slice-done
  84.1 0.0 slice-done.1
  84.1 0.0 copy-done.2
  84.1 1.6 fusion.41
  85.7 1.3 collective-permute-start.4
  87.0 4.8 %collective-permute-start.5 = (f32[1,2048]{1,0:T(1,128)S(1)}, f32[1,2048]{1,0:T(1,128)S(1)}, u32[]{:S(2)}, u32[]{:S(2)}) collective-permute-start(f32[1,2048]{1,0:T(1,128)S(1)} %get-tuple-element.16), channel_id=1, source_target_pairs={{0,1},{1,2},{2,3},{4,5},{5,6},{6,7},{8,9},{9,10},{10,11},{12,13},{... | collective-permute-start | bytes 24584 | tf_op jit(solution)/shard_map/ppermute | solution.py:16
  91.9 0.0 collective-permute-done.4
  91.9 1.3 collective-permute-done.5
  93.2 1.6 fusion.36
  94.8 1.3 collective-permute-start.6
  96.1 4.8 %collective-permute-start.7 = (f32[1,2048]{1,0:T(1,128)S(1)}, f32[1,2048]{1,0:T(1,128)S(1)}, u32[]{:S(2)}, u32[]{:S(2)}) collective-permute-start(f32[1,2048]{1,0:T(1,128)S(1)} %get-tuple-element.14), channel_id=1, source_target_pairs={{0,1},{1,2},{2,3},{4,5},{5,6},{6,7},{8,9},{9,10},{10,11},{12,13},{... | collective-permute-start | bytes 24584 | tf_op jit(solution)/shard_map/ppermute | solution.py:16
  101.0 0.0 collective-permute-done.6
  101.0 1.3 collective-permute-done.7
  102.3 1.6 fusion.31
  103.9 1.3 collective-permute-start.8
  105.2 4.8 %collective-permute-start.9 = (f32[1,2048]{1,0:T(1,128)S(1)}, f32[1,2048]{1,0:T(1,128)S(1)}, u32[]{:S(2)}, u32[]{:S(2)}) collective-permute-start(f32[1,2048]{1,0:T(1,128)S(1)} %get-tuple-element.12), channel_id=1, source_target_pairs={{0,1},{1,2},{2,3},{4,5},{5,6},{6,7},{8,9},{9,10},{10,11},{12,13},{... | collective-permute-start | bytes 24584 | tf_op jit(solution)/shard_map/ppermute | solution.py:16
  110.1 0.0 collective-permute-done.8
  110.1 1.3 collective-permute-done.9
  111.4 1.6 fusion.26
  113.1 1.3 collective-permute-start.10
  114.4 4.8 %collective-permute-start.11 = (f32[1,2048]{1,0:T(1,128)S(1)}, f32[1,2048]{1,0:T(1,128)S(1)}, u32[]{:S(2)}, u32[]{:S(2)}) collective-permute-start(f32[1,2048]{1,0:T(1,128)S(1)} %get-tuple-element.10), channel_id=1, source_target_pairs={{0,1},{1,2},{2,3},{4,5},{5,6},{6,7},{8,9},{9,10},{10,11},{12,13},{... | collective-permute-start | bytes 24584 | tf_op jit(solution)/shard_map/ppermute | solution.py:16
  119.2 0.0 collective-permute-done.10
  119.2 1.3 collective-permute-done.11
  120.5 1.6 fusion.21
  122.2 1.3 collective-permute-start.12
  123.5 0.0 copy-start.1
  123.5 5.1 %collective-permute-start.13 = (f32[1,2048]{1,0:T(1,128)S(1)}, f32[1,2048]{1,0:T(1,128)S(1)}, u32[]{:S(2)}, u32[]{:S(2)}) collective-permute-start(f32[1,2048]{1,0:T(1,128)S(1)} %get-tuple-element.8), channel_id=1, source_target_pairs={{0,1},{1,2},{2,3},{4,5},{5,6},{6,7},{8,9},{9,10},{10,11},{12,13},{... | collective-permute-start | bytes 24584 | tf_op jit(solution)/shard_map/ppermute | solution.py:16
  128.6 0.0 collective-permute-done.12
  128.6 1.2 collective-permute-done.13
  129.8 1.6 fusion.16
  131.4 1.3 collective-permute-start.14
  132.7 4.8 %collective-permute-start.15 = (f32[1,2048]{1,0:T(1,128)S(1)}, f32[1,2048]{1,0:T(1,128)S(1)}, u32[]{:S(2)}, u32[]{:S(2)}) collective-permute-start(f32[1,2048]{1,0:T(1,128)S(1)} %get-tuple-element.6), channel_id=1, source_target_pairs={{0,1},{1,2},{2,3},{4,5},{5,6},{6,7},{8,9},{9,10},{10,11},{12,13},{... | collective-permute-start | bytes 24584 | tf_op jit(solution)/shard_map/ppermute | solution.py:16
  137.5 0.0 collective-permute-done.14
  137.5 1.3 collective-permute-done.15
  138.9 0.0 copy-done.1
  138.9 7.7 %convolution_bitcast_fusion = f32[512,2048]{0,1:T(8,128)} fusion(f32[1,128,2048]{2,1,0:T(8,128)S(1)} %copy-done.1, f32[128,2048]{1,0:T(8,128)S(1)} %fusion.5, f32[128,2048]{1,0:T(8,128)S(1)} %fusion.16, f32[1,2048]{1,0:T(1,128)S(1)} %collective-permute-done.15, f32[1,2048]{1,0:T(1,128)S(1)} %collective-permute-done.14, f32[1,128,2048]{2,1,0:T(8,128)} %param.10, ...), kind=kOutput, calls=%fused_computation | convolution fusion | flops 1344798720 | bytes 16924672 | tf_op jit(solution)/shard_map/dot_general | solution.py:41
  146.6 5.4 %copy.9 = f32[512,2048]{1,0:T(8,128)} copy(f32[512,2048]{0,1:T(8,128)} %convolution_bitcast_fusion) | data formatting | bytes 8388608
  152.0 0.0 reduce-scatter.4.cloned.1.call-update
  152.1 149.8 %reduce-scatter.4.cloned.1.call-done = f32[16,2048]{1,0:T(8,128)} async-done(((f32[512,2048]{1,0:T(8,128)}), f32[16,2048]{1,0:T(8,128)}) %reduce-scatter.4.cloned.1.call-update) | async-done | bytes 131088 | tf_op jit(solution)/shard_map/reduce_scatter | solution.py:40
  (9 shorter events, 0.1 us)
Async XLA Ops:
  6.5 63.0 %copy-start = (bf16[1,128,512]{2,1,0:T(8,128)(2,1)S(1)}, bf16[1,128,512]{2,1,0:T(8,128)(2,1)}, u32[]{:S(2)}) copy-start(bf16[1,128,512]{2,1,0:T(8,128)(2,1)} %param.7) | copy-start | bytes 393220
  6.5 63.0 %all-gather.2.cloned.1.call-start = ((), (), s32[]{:S(2)}) async-start(), calls=%async_computation.1 | async-start | bytes 2162688 | tf_op jit(solution)/shard_map/all_gather | solution.py:27
  7.3 294.6 %reduce-scatter.4.cloned.1.call-start = ((), (), s32[]{:S(2)}) async-start(), calls=%async_computation.2 | async-start | bytes 4325376 | tf_op jit(solution)/shard_map/reduce_scatter | solution.py:40
  7.3 64.4 %collective-permute-start.1 = (f32[1,2048]{1,0:T(1,128)S(1)}, f32[1,2048]{1,0:T(1,128)S(1)}, u32[]{:S(2)}, u32[]{:S(2)}) collective-permute-start(f32[1,2048]{1,0:T(1,128)S(1)} %broadcast.12), channel_id=1, source_target_pairs={{0,1},{1,2},{2,3},{4,5},{5,6},{6,7},{8,9},{9,10},{10,11},{12,13},{... | collective-permute-start | bytes 24584 | tf_op jit(solution)/shard_map/ppermute | solution.py:16
  12.3 59.5 %collective-permute-start = (f32[1,2048]{1,0:T(1,128)S(1)}, f32[1,2048]{1,0:T(1,128)S(1)}, u32[]{:S(2)}, u32[]{:S(2)}) collective-permute-start(f32[1,2048]{1,0:T(1,128)S(1)} %broadcast.12), channel_id=1, source_target_pairs={{1,0},{2,1},{3,2},{5,4},{6,5},{7,6},{9,8},{10,9},{11,10},{13,12},{... | collective-permute-start | bytes 24584 | tf_op jit(solution)/shard_map/ppermute | solution.py:17
  69.5 14.6 %slice-start = ((s8[8388608]{0:T(1024)(128)(4,1)}), s8[4194304]{0:T(1024)(128)(4,1)S(1)}, s32[]{:S(2)}) async-start(s8[8388608]{0:T(1024)(128)(4,1)} %bitcast.38), calls=%async_computation.3 | async-start | bytes 8388608
  71.7 12.4 %slice-start.1 = ((s8[8388608]{0:T(1024)(128)(4,1)}), s8[4194304]{0:T(1024)(128)(4,1)S(1)}, s32[]{:S(2)}) async-start(s8[8388608]{0:T(1024)(128)(4,1)} %bitcast.38), calls=%async_computation.4 | async-start | bytes 8388608
  71.7 12.4 %copy-start.2 = (f32[1,128,2048]{2,1,0:T(8,128)S(1)}, f32[1,128,2048]{2,1,0:T(8,128)}, u32[]{:S(2)}) copy-start(f32[1,128,2048]{2,1,0:T(8,128)} %param.10) | copy-start | bytes 3145732
  76.9 5.9 %collective-permute-start.2 = (f32[1,2048]{1,0:T(1,128)S(1)}, f32[1,2048]{1,0:T(1,128)S(1)}, u32[]{:S(2)}, u32[]{:S(2)}) collective-permute-start(f32[1,2048]{1,0:T(1,128)S(1)} %get-tuple-element.17), channel_id=1, source_target_pairs={{1,0},{2,1},{3,2},{5,4},{6,5},{7,6},{9,8},{10,9},{11,10},{13,12},{... | collective-permute-start | bytes 24584 | tf_op jit(solution)/shard_map/ppermute | solution.py:17
  78.2 5.9 %collective-permute-start.3 = (f32[1,2048]{1,0:T(1,128)S(1)}, f32[1,2048]{1,0:T(1,128)S(1)}, u32[]{:S(2)}, u32[]{:S(2)}) collective-permute-start(f32[1,2048]{1,0:T(1,128)S(1)} %get-tuple-element.18), channel_id=1, source_target_pairs={{0,1},{1,2},{2,3},{4,5},{5,6},{6,7},{8,9},{9,10},{10,11},{12,13},{... | collective-permute-start | bytes 24584 | tf_op jit(solution)/shard_map/ppermute | solution.py:16
  85.7 6.1 %collective-permute-start.4 = (f32[1,2048]{1,0:T(1,128)S(1)}, f32[1,2048]{1,0:T(1,128)S(1)}, u32[]{:S(2)}, u32[]{:S(2)}) collective-permute-start(f32[1,2048]{1,0:T(1,128)S(1)} %get-tuple-element.15), channel_id=1, source_target_pairs={{1,0},{2,1},{3,2},{5,4},{6,5},{7,6},{9,8},{10,9},{11,10},{13,12},{... | collective-permute-start | bytes 24584 | tf_op jit(solution)/shard_map/ppermute | solution.py:17
  87.0 6.2 %collective-permute-start.5 = (f32[1,2048]{1,0:T(1,128)S(1)}, f32[1,2048]{1,0:T(1,128)S(1)}, u32[]{:S(2)}, u32[]{:S(2)}) collective-permute-start(f32[1,2048]{1,0:T(1,128)S(1)} %get-tuple-element.16), channel_id=1, source_target_pairs={{0,1},{1,2},{2,3},{4,5},{5,6},{6,7},{8,9},{9,10},{10,11},{12,13},{... | collective-permute-start | bytes 24584 | tf_op jit(solution)/shard_map/ppermute | solution.py:16
  94.8 6.1 %collective-permute-start.6 = (f32[1,2048]{1,0:T(1,128)S(1)}, f32[1,2048]{1,0:T(1,128)S(1)}, u32[]{:S(2)}, u32[]{:S(2)}) collective-permute-start(f32[1,2048]{1,0:T(1,128)S(1)} %get-tuple-element.13), channel_id=1, source_target_pairs={{1,0},{2,1},{3,2},{5,4},{6,5},{7,6},{9,8},{10,9},{11,10},{13,12},{... | collective-permute-start | bytes 24584 | tf_op jit(solution)/shard_map/ppermute | solution.py:17
  96.1 6.2 %collective-permute-start.7 = (f32[1,2048]{1,0:T(1,128)S(1)}, f32[1,2048]{1,0:T(1,128)S(1)}, u32[]{:S(2)}, u32[]{:S(2)}) collective-permute-start(f32[1,2048]{1,0:T(1,128)S(1)} %get-tuple-element.14), channel_id=1, source_target_pairs={{0,1},{1,2},{2,3},{4,5},{5,6},{6,7},{8,9},{9,10},{10,11},{12,13},{... | collective-permute-start | bytes 24584 | tf_op jit(solution)/shard_map/ppermute | solution.py:16
  103.9 6.1 %collective-permute-start.8 = (f32[1,2048]{1,0:T(1,128)S(1)}, f32[1,2048]{1,0:T(1,128)S(1)}, u32[]{:S(2)}, u32[]{:S(2)}) collective-permute-start(f32[1,2048]{1,0:T(1,128)S(1)} %get-tuple-element.11), channel_id=1, source_target_pairs={{1,0},{2,1},{3,2},{5,4},{6,5},{7,6},{9,8},{10,9},{11,10},{13,12},{... | collective-permute-start | bytes 24584 | tf_op jit(solution)/shard_map/ppermute | solution.py:17
  105.2 6.2 %collective-permute-start.9 = (f32[1,2048]{1,0:T(1,128)S(1)}, f32[1,2048]{1,0:T(1,128)S(1)}, u32[]{:S(2)}, u32[]{:S(2)}) collective-permute-start(f32[1,2048]{1,0:T(1,128)S(1)} %get-tuple-element.12), channel_id=1, source_target_pairs={{0,1},{1,2},{2,3},{4,5},{5,6},{6,7},{8,9},{9,10},{10,11},{12,13},{... | collective-permute-start | bytes 24584 | tf_op jit(solution)/shard_map/ppermute | solution.py:16
  113.1 6.1 %collective-permute-start.10 = (f32[1,2048]{1,0:T(1,128)S(1)}, f32[1,2048]{1,0:T(1,128)S(1)}, u32[]{:S(2)}, u32[]{:S(2)}) collective-permute-start(f32[1,2048]{1,0:T(1,128)S(1)} %get-tuple-element.9), channel_id=1, source_target_pairs={{1,0},{2,1},{3,2},{5,4},{6,5},{7,6},{9,8},{10,9},{11,10},{13,12},{... | collective-permute-start | bytes 24584 | tf_op jit(solution)/shard_map/ppermute | solution.py:17
  114.4 6.2 %collective-permute-start.11 = (f32[1,2048]{1,0:T(1,128)S(1)}, f32[1,2048]{1,0:T(1,128)S(1)}, u32[]{:S(2)}, u32[]{:S(2)}) collective-permute-start(f32[1,2048]{1,0:T(1,128)S(1)} %get-tuple-element.10), channel_id=1, source_target_pairs={{0,1},{1,2},{2,3},{4,5},{5,6},{6,7},{8,9},{9,10},{10,11},{12,13},{... | collective-permute-start | bytes 24584 | tf_op jit(solution)/shard_map/ppermute | solution.py:16
  122.2 6.5 %collective-permute-start.12 = (f32[1,2048]{1,0:T(1,128)S(1)}, f32[1,2048]{1,0:T(1,128)S(1)}, u32[]{:S(2)}, u32[]{:S(2)}) collective-permute-start(f32[1,2048]{1,0:T(1,128)S(1)} %get-tuple-element.7), channel_id=1, source_target_pairs={{1,0},{2,1},{3,2},{5,4},{6,5},{7,6},{9,8},{10,9},{11,10},{13,12},{... | collective-permute-start | bytes 24584 | tf_op jit(solution)/shard_map/ppermute | solution.py:17
  123.5 15.4 %copy-start.1 = (f32[1,128,2048]{2,1,0:T(8,128)S(1)}, f32[1,128,2048]{2,1,0:T(8,128)}, u32[]{:S(2)}) copy-start(f32[1,128,2048]{2,1,0:T(8,128)} %param.11) | copy-start | bytes 3145732
  123.5 6.3 %collective-permute-start.13 = (f32[1,2048]{1,0:T(1,128)S(1)}, f32[1,2048]{1,0:T(1,128)S(1)}, u32[]{:S(2)}, u32[]{:S(2)}) collective-permute-start(f32[1,2048]{1,0:T(1,128)S(1)} %get-tuple-element.8), channel_id=1, source_target_pairs={{0,1},{1,2},{2,3},{4,5},{5,6},{6,7},{8,9},{9,10},{10,11},{12,13},{... | collective-permute-start | bytes 24584 | tf_op jit(solution)/shard_map/ppermute | solution.py:16
  131.4 6.1 %collective-permute-start.14 = (f32[1,2048]{1,0:T(1,128)S(1)}, f32[1,2048]{1,0:T(1,128)S(1)}, u32[]{:S(2)}, u32[]{:S(2)}) collective-permute-start(f32[1,2048]{1,0:T(1,128)S(1)} %get-tuple-element.5), channel_id=1, source_target_pairs={{1,0},{2,1},{3,2},{5,4},{6,5},{7,6},{9,8},{10,9},{11,10},{13,12},{... | collective-permute-start | bytes 24584 | tf_op jit(solution)/shard_map/ppermute | solution.py:17
  132.7 6.2 %collective-permute-start.15 = (f32[1,2048]{1,0:T(1,128)S(1)}, f32[1,2048]{1,0:T(1,128)S(1)}, u32[]{:S(2)}, u32[]{:S(2)}) collective-permute-start(f32[1,2048]{1,0:T(1,128)S(1)} %get-tuple-element.6), channel_id=1, source_target_pairs={{0,1},{1,2},{2,3},{4,5},{5,6},{6,7},{8,9},{9,10},{10,11},{12,13},{... | collective-permute-start | bytes 24584 | tf_op jit(solution)/shard_map/ppermute | solution.py:16
Sparse Core Ops, SparseCore 0:
  10.3 59.1 all-gather.1
  152.2 149.6 reduce-scatter.3
where the time goes:
time: 309 us
  waiting for transfers between devices  215 us (70%)
  starting transfers between devices  49.1 us (16%)
  matrix products  24.6 us (8%)
  between operations  14.4 us (5%)
  local copies, waits for them, and re-layouts  5.56 us (2%)
    reduce_scatter x1, waiting for transfers between devices, shards(): lax.psum_scatter(lax.dot_general(columns, partial_img, (((0,), (0,)), (()...  150 us
    all_gather x1, waiting for transfers between devices, shards(): lax.all_gather(fine_model, ('freq', 'slab'), axis=0, tiled=True)  55.3 us
    ppermute x8, starting transfers between devices, with_halo(): before = lax.ppermute(last, axis, up)  38.7 us
    dot_general x7, matrix products, shards(): jnp.dot(field.astype(jnp.bfloat16), lateral, preferred_element_type=jnp.f...  14.7 us
    ppermute x8, starting transfers between devices, with_halo(): after = lax.ppermute(initial, axis, down)  10.3 us
    ppermute x8, waiting for transfers between devices, with_halo(): before = lax.ppermute(last, axis, up)  9.19 us
    dot_general x1, matrix products, shards(): lax.dot_general(columns, partial_img, (((0,), (0,)), ((), ())), preferred...  7.73 us
  transfers between devices with their start and end apart: 18, of which 9 were waited for; matrix products, arithmetic and copies ran while one was open for 1% of the time, Pallas kernels for 0%

commit v1 on v0

v1 whole, which is shorter than its diff:
```python
import functools

import jax
import jax.numpy as jnp
from jax import lax
from jax.experimental import pallas as pl
from jax.experimental.pallas import tpu as pltpu
from jax.sharding import PartitionSpec as P

SWEEPS = 8
HALO = 8
TILE = 256
MIB = 1 << 20
VMEM = pl.BlockSpec(memory_space=pltpu.VMEM)
SMEM = pl.BlockSpec(memory_space=pltpu.SMEM)


def xor_permute(value, axis, mask):
    size = lax.axis_size(axis)
    return lax.ppermute(value, axis, [(i, i ^ mask) for i in range(size)])


def solve_kernel(n_freq, n_slab, where, factor, *refs):
    blocks = refs[:n_freq]
    oper, oper_up, oper_down, src, src_up, src_down, rec, lateral, out = refs[n_freq : n_freq + 9]
    fine, rows, source, inverse, field, field_lo = refs[n_freq + 9 :]
    freq, slab = where[0], where[1]
    depth = src.shape[0]
    width = src.shape[1]
    tall = depth + 2 * HALO
    tile = blocks[0].shape[0] // n_slab
    for g in range(n_freq):
        for j in range(n_slab):
            at = ((freq ^ g) * n_slab + (slab ^ j)) * tile
            fine[pl.ds(pl.multiple_of(at, tile), tile), :] = blocks[g][j * tile : (j + 1) * tile, :]
    rows[0:HALO, :] = oper_up[...]
    rows[HALO : HALO + depth, :] = oper[...].astype(jnp.float32)
    rows[HALO + depth : tall, :] = oper_down[...]
    source[0:HALO, :] = src_up[...]
    source[HALO : HALO + depth, :] = src[...]
    source[HALO + depth : tall, :] = src_down[...]
    basis = rows[...].astype(jnp.bfloat16)
    at = lax.broadcasted_iota(jnp.int32, (tall, TILE), 0) - HALO + slab * depth
    inside = jnp.logical_and(at >= 0, at < n_slab * depth)
    for n in range(0, width, TILE):
        cols = slice(n, n + TILE)
        coarse = jnp.dot(basis, fine[:, cols], preferred_element_type=jnp.float32)
        damped = jnp.where(inside, 1.0 / (4.0 + factor[0] * coarse * coarse), 0.0)
        inverse[:, cols] = damped
        first = source[:, cols] * damped
        field[0, :, cols] = first
        field_lo[0, :, cols] = first.astype(jnp.bfloat16)
    for sweep in range(1, SWEEPS):
        old, new = (sweep - 1) % 2, sweep % 2
        for n in range(0, width, TILE):
            cols = slice(n, n + TILE)
            side = jnp.dot(field_lo[old], lateral[:, cols], preferred_element_type=jnp.float32)
            before = field[old, :, cols]
            beside = pltpu.roll(before, 1, 0) + pltpu.roll(before, tall - 1, 0)
            after = (source[:, cols] + 0.5 * beside + side) * inverse[:, cols]
            if sweep < SWEEPS - 1:
                field[new, :, cols] = after
                field_lo[new, :, cols] = after.astype(jnp.bfloat16)
            else:
                mine = after[HALO : HALO + depth, :]
                out[:, cols] = (mine * rec[:, cols]).astype(jnp.bfloat16)


def back_kernel(n_chips, where, oper, oper_other, part, part_other, keep, *sends):
    freq = where[0]
    core, chip = lax.rem(freq, 2), lax.div(freq, 2)
    half = oper.shape[1] // (2 * n_chips)

    def columns(ref):
        picked = []
        for m in range(n_chips):
            at = pl.multiple_of((chip ^ m) * (2 * half), 2 * half)
            pair = ref[:, pl.ds(at, 2 * half)].astype(jnp.float32)
            picked.append(jnp.where(core == 0, pair[:, :half], pair[:, half:]))
        return jnp.concatenate(picked, axis=1).astype(jnp.bfloat16)

    mine, other = columns(oper), columns(oper_other)
    width = part.shape[1]
    for n in range(0, width, TILE):
        cols = slice(n, n + TILE)
        over = (((0,), (0,)), ((), ()))
        total = lax.dot_general(mine, part[:, cols], over, preferred_element_type=jnp.float32)
        total += lax.dot_general(other, part_other[:, cols], over, preferred_element_type=jnp.float32)
        keep[:, cols] = total[:half]
        for m in range(1, n_chips):
            sends[m - 1][:, cols] = total[m * half : (m + 1) * half].astype(jnp.bfloat16)


def plane_kernel(n_chips, n_slab, where, keep, *refs):
    slab = where[1]
    gets, own, sends = refs[: n_chips - 1], refs[n_chips - 1], refs[n_chips:]
    tile = keep.shape[0] // n_slab
    for j in range(n_slab):
        at = pl.ds(pl.multiple_of((slab ^ j) * tile, tile), tile)
        total = keep[at, :]
        for got in gets:
            total += got[at, :].astype(jnp.float32)
        if j == 0:
            own[...] = total
        else:
            sends[j - 1][...] = total.astype(jnp.bfloat16)


def shards(fine_model, resample, lateral, shift, source, receiver):
    n_freq, n_slab = lax.axis_size("freq"), lax.axis_size("slab")
    n_chips = n_freq // 2
    oper, src, rec = resample[0], source[0], receiver[0]
    depth, width = src.shape
    n_fine = oper.shape[1]
    tall = depth + 2 * HALO
    where = jnp.stack([lax.axis_index("freq"), lax.axis_index("slab")]).astype(jnp.int32)
    f32, bf16 = jnp.float32, jnp.bfloat16

    line = [fine_model] + [xor_permute(fine_model, "slab", m) for m in range(1, n_slab)]
    line = jnp.concatenate(line, axis=0)
    oper_other = xor_permute(oper, "freq", 1)

    edges = jnp.concatenate([src[:HALO], oper[:HALO].astype(f32)], axis=1)
    edges_last = jnp.concatenate([src[depth - HALO :], oper[depth - HALO :].astype(f32)], axis=1)
    line, edges, edges_last = lax.optimization_barrier((line, edges, edges_last))
    plane = [line] + [xor_permute(line, "freq", 2 * m) for m in range(1, n_chips)]
    up = [(i, i + 1) for i in range(n_slab - 1)]
    above = lax.ppermute(edges_last, "slab", up)
    below = lax.ppermute(edges, "slab", [(j, i) for i, j in up])
    blocks = []
    for block in plane:
        blocks += [block, xor_permute(block, "freq", 1)]

    part = pl.pallas_call(
        functools.partial(solve_kernel, n_freq, n_slab),
        out_shape=jax.ShapeDtypeStruct((depth, width), bf16),
        in_specs=[SMEM, SMEM] + [VMEM] * (n_freq + 8),
        out_specs=VMEM,
        scratch_shapes=[
            pltpu.VMEM((n_fine, width), bf16),
            pltpu.VMEM((tall, n_fine), f32),
            pltpu.VMEM((tall, width), f32),
            pltpu.VMEM((tall, width), f32),
            pltpu.VMEM((2, tall, width), f32),
            pltpu.VMEM((2, tall, width), bf16),
        ],
        compiler_params=pltpu.CompilerParams(vmem_limit_bytes=48 * MIB),
        name="solve",
    )(
        where, shift, *blocks, oper, above[:, width:], below[:, width:], src, above[:, :width], below[:, :width],
        rec, lateral,
    )

    part_other = xor_permute(part, "freq", 1)
    rows = n_fine // n_freq
    keep, *sends = pl.pallas_call(
        functools.partial(back_kernel, n_chips),
        out_shape=[jax.ShapeDtypeStruct((rows, width), f32)]
        + [jax.ShapeDtypeStruct((rows, width), bf16)] * (n_chips - 1),
        in_specs=[SMEM] + [VMEM] * 4,
        out_specs=[VMEM] * n_chips,
        compiler_params=pltpu.CompilerParams(vmem_limit_bytes=32 * MIB),
        name="back",
    )(where, oper, oper_other, part, part_other)
    gets = [xor_permute(send, "freq", 2 * (m + 1)) for m, send in enumerate(sends)]

    tile = rows // n_slab
    own, *sends = pl.pallas_call(
        functools.partial(plane_kernel, n_chips, n_slab),
        out_shape=[jax.ShapeDtypeStruct((tile, width), f32)]
        + [jax.ShapeDtypeStruct((tile, width), bf16)] * (n_slab - 1),
        in_specs=[SMEM] + [VMEM] * n_chips,
        out_specs=[VMEM] * n_slab,
        compiler_params=pltpu.CompilerParams(vmem_limit_bytes=32 * MIB),
        name="plane",
    )(where, keep, *gets)
    for m, send in enumerate(sends):
        own = own + xor_permute(send, "slab", m + 1).astype(f32)
    return own


def solution(mesh):
    in_specs = (
        P(("freq", "slab"), None),
        P("freq", "slab", None),
        P(),
        P("freq"),
        P("freq", "slab", None),
        P("freq", "slab", None),
    )
    out_specs = P(("freq", "slab"), None)
    return jax.shard_map(shards, mesh=mesh, in_specs=in_specs, out_specs=out_specs, check_vma=False)
```

time: 309 us -> 85.2 us (0.28)
  waiting for transfers between devices: 215 us -> 38.9 us
  starting transfers between devices: 49.1 us -> 22.5 us
  matrix products: 24.6 us -> 0 us
  Pallas kernels: 0 us -> 16 us
  between operations: 14.4 us -> 0.78 us
    reduce_scatter x1 -> x0, waiting for transfers between devices: 150 us -> none  [shards(): lax.psum_scatter(lax.dot_general(columns, partial_img, (((0,), (0,)), (()...]
    all_gather x1 -> x0, waiting for transfers between devices: 55.3 us -> none  [shards(): lax.all_gather(fine_model, ('freq', 'slab'), axis=0, tiled=True)]
    ppermute x16 -> x20, waiting for transfers between devices: 9.21 us -> 38.9 us  [the longest x18 32.2 us: xor_permute(): return lax.ppermute(value, axis, [(i, i ^ mask) for i in range(size)])]
    ppermute x16 -> x20, starting transfers between devices: 49 us -> 22.5 us  [the longest x18 18.7 us: xor_permute(): return lax.ppermute(value, axis, [(i, i ^ mask) for i in range(size)])]
    dot_general x9 -> x0, matrix products: 24.6 us -> none  [the longest x7 14.7 us: shards(): jnp.dot(field.astype(jnp.bfloat16), lateral, preferred_element_type=jnp.f...]
    pallas_call x0 -> x3, Pallas kernels: none -> 16 us  [the longest x1 13.9 us: shards(): pl.pallas_call(functools.partial(solve_kernel, n_freq, n_slab), out_shape...]
  transfers between devices with their start and end apart: 18 -> 20, of which waited for: 9 -> 12; matrix products, arithmetic and copies ran while one was open for 1% -> 2% of each run, Pallas kernels for 0% -> 0%
where the time goes in v1:
time: 85.2 us; the launch traced here: 84.8 us
  waiting for transfers between devices  38.9 us (46%)
  starting transfers between devices  22.5 us (26%)
  Pallas kernels  16 us (19%)
  local copies, waits for them, and re-layouts  4.24 us (5%)
  other arithmetic  2.35 us (3%)
    ppermute x18, waiting for transfers between devices, xor_permute(): return lax.ppermute(value, axis, [(i, i ^ mask) for i in range(size)])  32.2 us
    ppermute x18, starting transfers between devices, xor_permute(): return lax.ppermute(value, axis, [(i, i ^ mask) for i in range(size)])  18.7 us
    pallas_call x1, Pallas kernels, shards(): pl.pallas_call(functools.partial(solve_kernel, n_freq, n_slab), out_shape...  13.9 us
    ppermute x1, waiting for transfers between devices, shards(): below = lax.ppermute(edges, 'slab', [(j, i) for i, j in up])  5.32 us
    unnamed x6, local copies, waits for them, and re-layouts  3.35 us
    ppermute x1, starting transfers between devices, shards(): above = lax.ppermute(edges_last, 'slab', up)  2.59 us
  transfers between devices with their start and end apart: 20, of which 12 were waited for; matrix products, arithmetic and copies ran while one was open for 2% of the time, Pallas kernels for 0%

profile of v1, /device:TPU:0, one launch (start us, length us, event | category | flops | bytes accessed | tf_op | source)
XLA Modules:
  0.0 84.8 jit_solution(4293439818691799769)
XLA Ops:
  0.0 3.0 %collective-permute-start.1 = (bf16[16,2048]{1,0:T(8,128)(2,1)}, bf16[16,2048]{1,0:T(8,128)(2,1)S(1)}, u32[]{:S(2)}, u32[]{:S(2)}) collective-permute-start(bf16[16,2048]{1,0:T(8,128)(2,1)} %param.6), channel_id=1, source_target_pairs={{0,1},{1,0},{2,3},{3,2},{4,5},{5,4},{6,7},{7,6},{8,9},{9,8},{10,11... | collective-permute-start | bytes 196616 | tf_op jit(solution)/shard_map/ppermute | solution.py:20
  3.0 2.6 %collective-permute-start.2 = (bf16[16,2048]{1,0:T(8,128)(2,1)}, bf16[16,2048]{1,0:T(8,128)(2,1)S(1)}, u32[]{:S(2)}, u32[]{:S(2)}) collective-permute-start(bf16[16,2048]{1,0:T(8,128)(2,1)} %param.6), channel_id=1, source_target_pairs={{0,2},{1,3},{2,0},{3,1},{4,6},{5,7},{6,4},{7,5},{8,10},{9,11},{10,... | collective-permute-start | bytes 196616 | tf_op jit(solution)/shard_map/ppermute | solution.py:20
  5.6 0.0 collective-permute-start.3
  5.6 0.9 %slice_bitcast_fusion = (f32[8,2048]{1,0:T(8,128)S(1)}, f32[8,2048]{1,0:T(8,128)S(1)}) fusion(f32[1,128,2048]{2,1,0:T(8,128)} %param.10), kind=kLoop, calls=%fused_computation.4 | loop fusion | bytes 262144 | tf_op jit(solution)/shard_map/slice | solution.py:124
  6.5 0.7 bitcast_convert_fusion
  7.2 0.0 collective-permute-done.1
  7.2 3.3 %collective-permute-done.2 = bf16[16,2048]{1,0:T(8,128)(2,1)S(1)} collective-permute-done((bf16[16,2048]{1,0:T(8,128)(2,1)}, bf16[16,2048]{1,0:T(8,128)(2,1)S(1)}, u32[]{:S(2)}, u32[]{:S(2)}) %collective-permute-start.2) | collective-permute-done | bytes 65568 | tf_op jit(solution)/shard_map/ppermute | solution.py:20
  10.5 1.4 %collective-permute-done.3 = bf16[16,2048]{1,0:T(8,128)(2,1)S(1)} collective-permute-done((bf16[16,2048]{1,0:T(8,128)(2,1)}, bf16[16,2048]{1,0:T(8,128)(2,1)S(1)}, u32[]{:S(2)}, u32[]{:S(2)}) %collective-permute-start.3) | collective-permute-done | bytes 65568 | tf_op jit(solution)/shard_map/ppermute | solution.py:20
  11.9 0.9 %pad_maximum_fusion.refs_0_ = bf16[64,2048]{1,0:T(8,128)(2,1)S(1)} fusion(bf16[16,2048]{1,0:T(8,128)(2,1)S(1)} %collective-permute-done.3, bf16[16,2048]{1,0:T(8,128)(2,1)S(1)} %collective-permute-done.2, bf16[16,2048]{1,0:T(8,128)(2,1)S(1)} %collective-permute-done.1, bf16[16,2048]{1,0:T(8,128)(2,1)} %param.6), kind=kLoop, calls=%fused_computation | loop fusion | flops 1048576 | bytes 524288 | tf_op jit(solution)/shard_map/concatenate | solution.py:120
  12.8 2.5 %collective-permute-start.9 = (bf16[64,2048]{1,0:T(8,128)(2,1)S(1)}, bf16[64,2048]{1,0:T(8,128)(2,1)S(1)}, u32[]{:S(2)}, u32[]{:S(2)}) collective-permute-start(bf16[64,2048]{1,0:T(8,128)(2,1)S(1)} %pad_maximum_fusion.refs_0_), channel_id=1, source_target_pairs={{0,24},{4,28},{8,16},{12,20},{16,8},{20,12},{24,0},{28,4},{1,25},{... | collective-permute-start | bytes 786440 | tf_op jit(solution)/shard_map/ppermute | solution.py:20
  15.3 0.5 collective-permute-start.5
  15.8 0.5 collective-permute-start.7
  16.3 0.0 collective-permute-start.4
  16.3 6.6 %collective-permute-done.9.refs_6_ = bf16[64,2048]{1,0:T(8,128)(2,1)S(1)} collective-permute-done((bf16[64,2048]{1,0:T(8,128)(2,1)S(1)}, bf16[64,2048]{1,0:T(8,128)(2,1)S(1)}, u32[]{:S(2)}, u32[]{:S(2)}) %collective-permute-start.9) | collective-permute-done | bytes 262176 | tf_op jit(solution)/shard_map/ppermute | solution.py:20
  23.0 0.0 collective-permute-start.10
  23.0 2.9 %collective-permute-done.5.refs_2_ = bf16[64,2048]{1,0:T(8,128)(2,1)S(1)} collective-permute-done((bf16[64,2048]{1,0:T(8,128)(2,1)S(1)}, bf16[64,2048]{1,0:T(8,128)(2,1)S(1)}, u32[]{:S(2)}, u32[]{:S(2)}) %collective-permute-start.5) | collective-permute-done | bytes 262176 | tf_op jit(solution)/shard_map/ppermute | solution.py:20
  25.9 0.0 collective-permute-start.6
  25.9 0.0 collective-permute-done.7.refs_4_
  25.9 0.5 collective-permute-start.8
  26.4 2.6 %collective-permute-start.11 = (f32[8,2560]{1,0:T(8,128)S(1)}, f32[8,2560]{1,0:T(8,128)S(1)}, u32[]{:S(2)}, u32[]{:S(2)}) collective-permute-start(f32[8,2560]{1,0:T(8,128)S(1)} %get-tuple-element.17), channel_id=1, source_target_pairs={{0,1},{1,2},{2,3},{4,5},{5,6},{6,7},{8,9},{9,10},{10,11},{12,13},{... | collective-permute-start | bytes 245768 | tf_op jit(solution)/shard_map/ppermute | solution.py:128
  29.6 1.4 %collective-permute-done.11 = f32[8,2560]{1,0:T(8,128)S(1)} collective-permute-done((f32[8,2560]{1,0:T(8,128)S(1)}, f32[8,2560]{1,0:T(8,128)S(1)}, u32[]{:S(2)}, u32[]{:S(2)}) %collective-permute-start.11) | collective-permute-done | bytes 81952 | tf_op jit(solution)/shard_map/ppermute | solution.py:128
  31.0 1.3 %collective-permute-start.12 = (f32[8,2560]{1,0:T(8,128)S(1)}, f32[8,2560]{1,0:T(8,128)S(1)}, u32[]{:S(2)}, u32[]{:S(2)}) collective-permute-start(f32[8,2560]{1,0:T(8,128)S(1)} %get-tuple-element.18), channel_id=1, source_target_pairs={{1,0},{2,1},{3,2},{5,4},{6,5},{7,6},{9,8},{10,9},{11,10},{13,12},{... | collective-permute-start | bytes 245768 | tf_op jit(solution)/shard_map/ppermute | solution.py:129
  32.3 0.1 pad_add_fusion.where
  32.4 5.3 %collective-permute-done.12 = f32[8,2560]{1,0:T(8,128)S(1)} collective-permute-done((f32[8,2560]{1,0:T(8,128)S(1)}, f32[8,2560]{1,0:T(8,128)S(1)}, u32[]{:S(2)}, u32[]{:S(2)}) %collective-permute-start.12) | collective-permute-done | bytes 81952 | tf_op jit(solution)/shard_map/ppermute | solution.py:129
  37.7 0.0 collective-permute-done.4.refs_1_
  37.7 0.0 collective-permute-done.10.refs_7_
  37.7 0.0 collective-permute-done.6.refs_3_
  37.8 0.0 collective-permute-done.8.refs_5_
  37.8 0.0 copy-start
  37.8 1.2 %copy-done = f32[1,128,2048]{2,1,0:T(8,128)S(1)} copy-done((f32[1,128,2048]{2,1,0:T(8,128)S(1)}, f32[1,128,2048]{2,1,0:T(8,128)}, u32[]{:S(2)}) %copy-start) | copy-done | bytes 1048600
  39.0 0.0 copy-start.1
  39.0 1.2 %copy-done.1 = f32[1,128,2048]{2,1,0:T(8,128)S(1)} copy-done((f32[1,128,2048]{2,1,0:T(8,128)S(1)}, f32[1,128,2048]{2,1,0:T(8,128)}, u32[]{:S(2)}) %copy-start.1) | copy-done | bytes 1048600
  40.2 0.0 copy-start.2
  40.2 0.9 %copy-done.2 = bf16[1,128,512]{2,1,0:T(8,128)(2,1)S(1)} copy-done((bf16[1,128,512]{2,1,0:T(8,128)(2,1)S(1)}, bf16[1,128,512]{2,1,0:T(8,128)(2,1)}, u32[]{:S(2)}) %copy-start.2) | copy-done | bytes 131096
  41.1 13.9 %solve.1.part = bf16[128,2048]{1,0:T(8,128)(2,1)S(1)} custom-call(s32[2]{0:T(128)S(1)} %pad_add_fusion.where, f32[1]{0:T(128)S(6)} %copy.7.factor, bf16[64,2048]{1,0:T(8,128)(2,1)S(1)} %pad_maximum_fusion.refs_0_, bf16[64,2048]{1,0:T(8,128)(2,1)S(1)} %collective-permute-done.4.refs_1_, bf16[64,2048]{1,0:T(8,128)(2,1)S(1)} %collective-permute-done.5.refs_2_, ...), custom_call_target="tpu_custom_call" | custom-call | tf_op jit(solution)/shard_map/solve/pallas_call | solution.py:134
  55.0 0.1 collective-permute-start.13
  55.1 0.5 collective-permute-start
  55.6 1.6 %collective-permute-done.oper_other = bf16[128,512]{1,0:T(8,128)(2,1)S(1)} collective-permute-done((bf16[128,512]{1,0:T(8,128)(2,1)S(1)}, bf16[128,512]{1,0:T(8,128)(2,1)S(1)}, u32[]{:S(2)}, u32[]{:S(2)}) %collective-permute-start) | collective-permute-done | bytes 131104 | tf_op jit(solution)/shard_map/ppermute | solution.py:20
  57.2 0.0 collective-permute-done.13.part_other
  57.2 1.4 %back.1 = (f32[64,2048]{1,0:T(8,128)S(1)}, bf16[64,2048]{1,0:T(8,128)(2,1)S(1)}, bf16[64,2048]{1,0:T(8,128)(2,1)S(1)}, bf16[64,2048]{1,0:T(8,128)(2,1)S(1)}) custom-call(s32[2]{0:T(128)S(1)} %pad_add_fusion.where, bf16[128,512]{1,0:T(8,128)(2,1)S(1)} %bitcast.19, bf16[128,512]{1,0:T(8,128)(2,1)S(1)} %collective-permute-done.oper_other, ...), custom_call_target="tpu_custom_call" | custom-call | tf_op jit(solution)/shard_map/back/pallas_call | solution.py:156
  58.6 1.6 %collective-permute-start.14 = (bf16[64,2048]{1,0:T(8,128)(2,1)S(1)}, bf16[64,2048]{1,0:T(8,128)(2,1)S(1)}, u32[]{:S(2)}, u32[]{:S(2)}) collective-permute-start(bf16[64,2048]{1,0:T(8,128)(2,1)S(1)} %get-tuple-element.20), channel_id=1, source_target_pairs={{0,8},{4,12},{8,0},{12,4},{16,24},{20,28},{24,16},{28,20},{1,9},{5... | collective-permute-start | bytes 786440 | tf_op jit(solution)/shard_map/ppermute | solution.py:20
  60.2 1.3 %collective-permute-start.15 = (bf16[64,2048]{1,0:T(8,128)(2,1)S(1)}, bf16[64,2048]{1,0:T(8,128)(2,1)S(1)}, u32[]{:S(2)}, u32[]{:S(2)}) collective-permute-start(bf16[64,2048]{1,0:T(8,128)(2,1)S(1)} %get-tuple-element.21), channel_id=1, source_target_pairs={{0,16},{4,20},{8,24},{12,28},{16,0},{20,4},{24,8},{28,12},{1,17},{... | collective-permute-start | bytes 786440 | tf_op jit(solution)/shard_map/ppermute | solution.py:20
  61.5 0.7 collective-permute-start.16
  62.2 5.7 %collective-permute-done.14.refs_0_ = bf16[64,2048]{1,0:T(8,128)(2,1)S(1)} collective-permute-done((bf16[64,2048]{1,0:T(8,128)(2,1)S(1)}, bf16[64,2048]{1,0:T(8,128)(2,1)S(1)}, u32[]{:S(2)}, u32[]{:S(2)}) %collective-permute-start.14) | collective-permute-done | bytes 262176 | tf_op jit(solution)/shard_map/ppermute | solution.py:20
  67.8 6.0 %collective-permute-done.15.refs_1_ = bf16[64,2048]{1,0:T(8,128)(2,1)S(1)} collective-permute-done((bf16[64,2048]{1,0:T(8,128)(2,1)S(1)}, bf16[64,2048]{1,0:T(8,128)(2,1)S(1)}, u32[]{:S(2)}, u32[]{:S(2)}) %collective-permute-start.15) | collective-permute-done | bytes 262176 | tf_op jit(solution)/shard_map/ppermute | solution.py:20
  73.9 0.0 collective-permute-done.16.refs_2_
  73.9 0.7 plane.1
  74.5 2.1 %collective-permute-start.17 = (bf16[16,2048]{1,0:T(8,128)(2,1)S(1)}, bf16[16,2048]{1,0:T(8,128)(2,1)S(1)}, u32[]{:S(2)}, u32[]{:S(2)}) collective-permute-start(bf16[16,2048]{1,0:T(8,128)(2,1)S(1)} %get-tuple-element.24), channel_id=1, source_target_pairs={{0,1},{1,0},{2,3},{3,2},{4,5},{5,4},{6,7},{7,6},{8,9},{9,8},{10,11... | collective-permute-start | bytes 196616 | tf_op jit(solution)/shard_map/ppermute | solution.py:20
  76.6 1.4 %collective-permute-start.18 = (bf16[16,2048]{1,0:T(8,128)(2,1)S(1)}, bf16[16,2048]{1,0:T(8,128)(2,1)S(1)}, u32[]{:S(2)}, u32[]{:S(2)}) collective-permute-start(bf16[16,2048]{1,0:T(8,128)(2,1)S(1)} %get-tuple-element.25), channel_id=1, source_target_pairs={{0,2},{1,3},{2,0},{3,1},{4,6},{5,7},{6,4},{7,5},{8,10},{9,11},{10,... | collective-permute-start | bytes 196616 | tf_op jit(solution)/shard_map/ppermute | solution.py:20
  78.0 1.4 %collective-permute-start.19 = (bf16[16,2048]{1,0:T(8,128)(2,1)S(1)}, bf16[16,2048]{1,0:T(8,128)(2,1)S(1)}, u32[]{:S(2)}, u32[]{:S(2)}) collective-permute-start(bf16[16,2048]{1,0:T(8,128)(2,1)S(1)} %get-tuple-element.26), channel_id=1, source_target_pairs={{0,3},{1,2},{2,1},{3,0},{4,7},{5,6},{6,5},{7,4},{8,11},{9,10},{10,... | collective-permute-start | bytes 196616 | tf_op jit(solution)/shard_map/ppermute | solution.py:20
  79.4 0.2 collective-permute-done.17
  79.6 3.6 %collective-permute-done.18 = bf16[16,2048]{1,0:T(8,128)(2,1)S(1)} collective-permute-done((bf16[16,2048]{1,0:T(8,128)(2,1)S(1)}, bf16[16,2048]{1,0:T(8,128)(2,1)S(1)}, u32[]{:S(2)}, u32[]{:S(2)}) %collective-permute-start.18) | collective-permute-done | bytes 65568 | tf_op jit(solution)/shard_map/ppermute | solution.py:20
  83.2 1.0 %collective-permute-done.19 = bf16[16,2048]{1,0:T(8,128)(2,1)S(1)} collective-permute-done((bf16[16,2048]{1,0:T(8,128)(2,1)S(1)}, bf16[16,2048]{1,0:T(8,128)(2,1)S(1)}, u32[]{:S(2)}, u32[]{:S(2)}) %collective-permute-start.19) | collective-permute-done | bytes 65568 | tf_op jit(solution)/shard_map/ppermute | solution.py:20
  84.1 0.7 convert_add_fusion
  (5 shorter events, 0.0 us)
Async XLA Ops:
  0.0 7.2 %collective-permute-start.1 = (bf16[16,2048]{1,0:T(8,128)(2,1)}, bf16[16,2048]{1,0:T(8,128)(2,1)S(1)}, u32[]{:S(2)}, u32[]{:S(2)}) collective-permute-start(bf16[16,2048]{1,0:T(8,128)(2,1)} %param.6), channel_id=1, source_target_pairs={{0,1},{1,0},{2,3},{3,2},{4,5},{5,4},{6,7},{7,6},{8,9},{9,8},{10,11... | collective-permute-start | bytes 196616 | tf_op jit(solution)/shard_map/ppermute | solution.py:20
  3.0 7.5 %collective-permute-start.2 = (bf16[16,2048]{1,0:T(8,128)(2,1)}, bf16[16,2048]{1,0:T(8,128)(2,1)S(1)}, u32[]{:S(2)}, u32[]{:S(2)}) collective-permute-start(bf16[16,2048]{1,0:T(8,128)(2,1)} %param.6), channel_id=1, source_target_pairs={{0,2},{1,3},{2,0},{3,1},{4,6},{5,7},{6,4},{7,5},{8,10},{9,11},{10,... | collective-permute-start | bytes 196616 | tf_op jit(solution)/shard_map/ppermute | solution.py:20
  5.6 6.3 %collective-permute-start.3 = (bf16[16,2048]{1,0:T(8,128)(2,1)}, bf16[16,2048]{1,0:T(8,128)(2,1)S(1)}, u32[]{:S(2)}, u32[]{:S(2)}) collective-permute-start(bf16[16,2048]{1,0:T(8,128)(2,1)} %param.6), channel_id=1, source_target_pairs={{0,3},{1,2},{2,1},{3,0},{4,7},{5,6},{6,5},{7,4},{8,11},{9,10},{10,... | collective-permute-start | bytes 196616 | tf_op jit(solution)/shard_map/ppermute | solution.py:20
  12.8 10.2 %collective-permute-start.9 = (bf16[64,2048]{1,0:T(8,128)(2,1)S(1)}, bf16[64,2048]{1,0:T(8,128)(2,1)S(1)}, u32[]{:S(2)}, u32[]{:S(2)}) collective-permute-start(bf16[64,2048]{1,0:T(8,128)(2,1)S(1)} %pad_maximum_fusion.refs_0_), channel_id=1, source_target_pairs={{0,24},{4,28},{8,16},{12,20},{16,8},{20,12},{24,0},{28,4},{1,25},{... | collective-permute-start | bytes 786440 | tf_op jit(solution)/shard_map/ppermute | solution.py:20
  15.3 10.6 %collective-permute-start.5 = (bf16[64,2048]{1,0:T(8,128)(2,1)S(1)}, bf16[64,2048]{1,0:T(8,128)(2,1)S(1)}, u32[]{:S(2)}, u32[]{:S(2)}) collective-permute-start(bf16[64,2048]{1,0:T(8,128)(2,1)S(1)} %pad_maximum_fusion.refs_0_), channel_id=1, source_target_pairs={{0,8},{4,12},{8,0},{12,4},{16,24},{20,28},{24,16},{28,20},{1,9},{5... | collective-permute-start | bytes 786440 | tf_op jit(solution)/shard_map/ppermute | solution.py:20
  15.8 10.0 %collective-permute-start.7 = (bf16[64,2048]{1,0:T(8,128)(2,1)S(1)}, bf16[64,2048]{1,0:T(8,128)(2,1)S(1)}, u32[]{:S(2)}, u32[]{:S(2)}) collective-permute-start(bf16[64,2048]{1,0:T(8,128)(2,1)S(1)} %pad_maximum_fusion.refs_0_), channel_id=1, source_target_pairs={{0,16},{4,20},{8,24},{12,28},{16,0},{20,4},{24,8},{28,12},{1,17},{... | collective-permute-start | bytes 786440 | tf_op jit(solution)/shard_map/ppermute | solution.py:20
  16.3 21.4 %collective-permute-start.4 = (bf16[64,2048]{1,0:T(8,128)(2,1)S(1)}, bf16[64,2048]{1,0:T(8,128)(2,1)S(1)}, u32[]{:S(2)}, u32[]{:S(2)}) collective-permute-start(bf16[64,2048]{1,0:T(8,128)(2,1)S(1)} %pad_maximum_fusion.refs_0_), channel_id=1, source_target_pairs={{0,4},{4,0},{8,12},{12,8},{16,20},{20,16},{24,28},{28,24},{1,5},{5... | collective-permute-start | bytes 786440 | tf_op jit(solution)/shard_map/ppermute | solution.py:20
  23.0 14.8 %collective-permute-start.10 = (bf16[64,2048]{1,0:T(8,128)(2,1)S(1)}, bf16[64,2048]{1,0:T(8,128)(2,1)S(1)}, u32[]{:S(2)}, u32[]{:S(2)}) collective-permute-start(bf16[64,2048]{1,0:T(8,128)(2,1)S(1)} %collective-permute-done.9.refs_6_), channel_id=1, source_target_pairs={{0,4},{4,0},{8,12},{12,8},{16,20},{20,16},{24,28},{28,24},{1,5},{5... | collective-permute-start | bytes 786440 | tf_op jit(solution)/shard_map/ppermute | solution.py:20
  25.9 11.9 %collective-permute-start.6 = (bf16[64,2048]{1,0:T(8,128)(2,1)S(1)}, bf16[64,2048]{1,0:T(8,128)(2,1)S(1)}, u32[]{:S(2)}, u32[]{:S(2)}) collective-permute-start(bf16[64,2048]{1,0:T(8,128)(2,1)S(1)} %collective-permute-done.5.refs_2_), channel_id=1, source_target_pairs={{0,4},{4,0},{8,12},{12,8},{16,20},{20,16},{24,28},{28,24},{1,5},{5... | collective-permute-start | bytes 786440 | tf_op jit(solution)/shard_map/ppermute | solution.py:20
  25.9 11.9 %collective-permute-start.8 = (bf16[64,2048]{1,0:T(8,128)(2,1)S(1)}, bf16[64,2048]{1,0:T(8,128)(2,1)S(1)}, u32[]{:S(2)}, u32[]{:S(2)}) collective-permute-start(bf16[64,2048]{1,0:T(8,128)(2,1)S(1)} %collective-permute-done.7.refs_4_), channel_id=1, source_target_pairs={{0,4},{4,0},{8,12},{12,8},{16,20},{20,16},{24,28},{28,24},{1,5},{5... | collective-permute-start | bytes 786440 | tf_op jit(solution)/shard_map/ppermute | solution.py:20
  26.4 4.6 %collective-permute-start.11 = (f32[8,2560]{1,0:T(8,128)S(1)}, f32[8,2560]{1,0:T(8,128)S(1)}, u32[]{:S(2)}, u32[]{:S(2)}) collective-permute-start(f32[8,2560]{1,0:T(8,128)S(1)} %get-tuple-element.17), channel_id=1, source_target_pairs={{0,1},{1,2},{2,3},{4,5},{5,6},{6,7},{8,9},{9,10},{10,11},{12,13},{... | collective-permute-start | bytes 245768 | tf_op jit(solution)/shard_map/ppermute | solution.py:128
  31.0 6.7 %collective-permute-start.12 = (f32[8,2560]{1,0:T(8,128)S(1)}, f32[8,2560]{1,0:T(8,128)S(1)}, u32[]{:S(2)}, u32[]{:S(2)}) collective-permute-start(f32[8,2560]{1,0:T(8,128)S(1)} %get-tuple-element.18), channel_id=1, source_target_pairs={{1,0},{2,1},{3,2},{5,4},{6,5},{7,6},{9,8},{10,9},{11,10},{13,12},{... | collective-permute-start | bytes 245768 | tf_op jit(solution)/shard_map/ppermute | solution.py:129
  37.8 1.2 %copy-start = (f32[1,128,2048]{2,1,0:T(8,128)S(1)}, f32[1,128,2048]{2,1,0:T(8,128)}, u32[]{:S(2)}) copy-start(f32[1,128,2048]{2,1,0:T(8,128)} %param.10) | copy-start | bytes 3145732
  39.0 1.2 %copy-start.1 = (f32[1,128,2048]{2,1,0:T(8,128)S(1)}, f32[1,128,2048]{2,1,0:T(8,128)}, u32[]{:S(2)}) copy-start(f32[1,128,2048]{2,1,0:T(8,128)} %param.11) | copy-start | bytes 3145732
  40.2 0.9 %copy-start.2 = (bf16[1,128,512]{2,1,0:T(8,128)(2,1)S(1)}, bf16[1,128,512]{2,1,0:T(8,128)(2,1)}, u32[]{:S(2)}) copy-start(bf16[1,128,512]{2,1,0:T(8,128)(2,1)} %param.7) | copy-start | bytes 393220
  55.0 2.2 %collective-permute-start.13 = (bf16[128,2048]{1,0:T(8,128)(2,1)S(1)}, bf16[128,2048]{1,0:T(8,128)(2,1)S(1)}, u32[]{:S(2)}, u32[]{:S(2)}) collective-permute-start(bf16[128,2048]{1,0:T(8,128)(2,1)S(1)} %solve.1.part), channel_id=1, source_target_pairs={{0,4},{4,0},{8,12},{12,8},{16,20},{20,16},{24,28},{28,24},{1,5},{5... | collective-permute-start | bytes 1572872 | tf_op jit(solution)/shard_map/ppermute | solution.py:20
  55.1 2.1 %collective-permute-start = (bf16[128,512]{1,0:T(8,128)(2,1)S(1)}, bf16[128,512]{1,0:T(8,128)(2,1)S(1)}, u32[]{:S(2)}, u32[]{:S(2)}) collective-permute-start(bf16[128,512]{1,0:T(8,128)(2,1)S(1)} %bitcast.18), channel_id=1, source_target_pairs={{0,4},{4,0},{8,12},{12,8},{16,20},{20,16},{24,28},{28,24},{1,5},{5... | collective-permute-start | bytes 393224 | tf_op jit(solution)/shard_map/ppermute | solution.py:20
  58.6 9.2 %collective-permute-start.14 = (bf16[64,2048]{1,0:T(8,128)(2,1)S(1)}, bf16[64,2048]{1,0:T(8,128)(2,1)S(1)}, u32[]{:S(2)}, u32[]{:S(2)}) collective-permute-start(bf16[64,2048]{1,0:T(8,128)(2,1)S(1)} %get-tuple-element.20), channel_id=1, source_target_pairs={{0,8},{4,12},{8,0},{12,4},{16,24},{20,28},{24,16},{28,20},{1,9},{5... | collective-permute-start | bytes 786440 | tf_op jit(solution)/shard_map/ppermute | solution.py:20
  60.2 13.7 %collective-permute-start.15 = (bf16[64,2048]{1,0:T(8,128)(2,1)S(1)}, bf16[64,2048]{1,0:T(8,128)(2,1)S(1)}, u32[]{:S(2)}, u32[]{:S(2)}) collective-permute-start(bf16[64,2048]{1,0:T(8,128)(2,1)S(1)} %get-tuple-element.21), channel_id=1, source_target_pairs={{0,16},{4,20},{8,24},{12,28},{16,0},{20,4},{24,8},{28,12},{1,17},{... | collective-permute-start | bytes 786440 | tf_op jit(solution)/shard_map/ppermute | solution.py:20
  61.5 12.4 %collective-permute-start.16 = (bf16[64,2048]{1,0:T(8,128)(2,1)S(1)}, bf16[64,2048]{1,0:T(8,128)(2,1)S(1)}, u32[]{:S(2)}, u32[]{:S(2)}) collective-permute-start(bf16[64,2048]{1,0:T(8,128)(2,1)S(1)} %get-tuple-element.22), channel_id=1, source_target_pairs={{0,24},{4,28},{8,16},{12,20},{16,8},{20,12},{24,0},{28,4},{1,25},{... | collective-permute-start | bytes 786440 | tf_op jit(solution)/shard_map/ppermute | solution.py:20
  74.5 5.0 %collective-permute-start.17 = (bf16[16,2048]{1,0:T(8,128)(2,1)S(1)}, bf16[16,2048]{1,0:T(8,128)(2,1)S(1)}, u32[]{:S(2)}, u32[]{:S(2)}) collective-permute-start(bf16[16,2048]{1,0:T(8,128)(2,1)S(1)} %get-tuple-element.24), channel_id=1, source_target_pairs={{0,1},{1,0},{2,3},{3,2},{4,5},{5,4},{6,7},{7,6},{8,9},{9,8},{10,11... | collective-permute-start | bytes 196616 | tf_op jit(solution)/shard_map/ppermute | solution.py:20
  76.6 6.5 %collective-permute-start.18 = (bf16[16,2048]{1,0:T(8,128)(2,1)S(1)}, bf16[16,2048]{1,0:T(8,128)(2,1)S(1)}, u32[]{:S(2)}, u32[]{:S(2)}) collective-permute-start(bf16[16,2048]{1,0:T(8,128)(2,1)S(1)} %get-tuple-element.25), channel_id=1, source_target_pairs={{0,2},{1,3},{2,0},{3,1},{4,6},{5,7},{6,4},{7,5},{8,10},{9,11},{10,... | collective-permute-start | bytes 196616 | tf_op jit(solution)/shard_map/ppermute | solution.py:20
  78.0 6.1 %collective-permute-start.19 = (bf16[16,2048]{1,0:T(8,128)(2,1)S(1)}, bf16[16,2048]{1,0:T(8,128)(2,1)S(1)}, u32[]{:S(2)}, u32[]{:S(2)}) collective-permute-start(bf16[16,2048]{1,0:T(8,128)(2,1)S(1)} %get-tuple-element.26), channel_id=1, source_target_pairs={{0,3},{1,2},{2,1},{3,0},{4,7},{5,6},{6,5},{7,4},{8,11},{9,10},{10,... | collective-permute-start | bytes 196616 | tf_op jit(solution)/shard_map/ppermute | solution.py:20

commit v2 on v1

--- a/solution.py
+++ b/solution.py
@@ -66,6 +66,28 @@
                 out[:, cols] = (mine * rec[:, cols]).astype(jnp.bfloat16)
 
 
+def stage_kernel(*refs):
+    count = (len(refs) - 1) // 2
+    copies = [pltpu.make_async_copy(refs[i], refs[count + i], refs[-1].at[i]) for i in range(count)]
+    for copy in copies:
+        copy.start()
+    for copy in copies:
+        copy.wait()
+
+
+def stage(*arrays):
+    return pl.pallas_call(
+        stage_kernel,
+        out_shape=[pltpu.VMEM(a.shape, a.dtype) for a in arrays],
+        in_specs=[pl.BlockSpec(memory_space=pl.ANY)] * len(arrays),
+        out_specs=[VMEM] * len(arrays),
+        scratch_shapes=[pltpu.SemaphoreType.DMA((len(arrays),))],
+        compiler_params=pltpu.CompilerParams(vmem_limit_bytes=48 * MIB),
+        cost_estimate=pl.CostEstimate(flops=0, transcendentals=0, bytes_accessed=2 * sum(a.size * a.dtype.itemsize for a in arrays)),
+        name="stage",
+    )(*arrays)
+
+
 def back_kernel(n_chips, where, oper, oper_other, part, part_other, keep, *sends):
     freq = where[0]
     core, chip = lax.rem(freq, 2), lax.div(freq, 2)
@@ -116,17 +138,21 @@
     where = jnp.stack([lax.axis_index("freq"), lax.axis_index("slab")]).astype(jnp.int32)
     f32, bf16 = jnp.float32, jnp.bfloat16
 
-    line = [fine_model] + [xor_permute(fine_model, "slab", m) for m in range(1, n_slab)]
-    line = jnp.concatenate(line, axis=0)
+    line = [xor_permute(fine_model, "slab", m) for m in range(n_slab - 1, 0, -1)]
+    line = jnp.concatenate([fine_model] + line[::-1], axis=0)
     oper_other = xor_permute(oper, "freq", 1)
 
     edges = jnp.concatenate([src[:HALO], oper[:HALO].astype(f32)], axis=1)
     edges_last = jnp.concatenate([src[depth - HALO :], oper[depth - HALO :].astype(f32)], axis=1)
-    line, edges, edges_last = lax.optimization_barrier((line, edges, edges_last))
     plane = [line] + [xor_permute(line, "freq", 2 * m) for m in range(1, n_chips)]
-    up = [(i, i + 1) for i in range(n_slab - 1)]
-    above = lax.ppermute(edges_last, "slab", up)
-    below = lax.ppermute(edges, "slab", [(j, i) for i, j in up])
+    odd = lax.rem(lax.axis_index("slab"), 2) == 1
+    near = lax.ppermute(jnp.where(odd, edges, edges_last), "slab", [(i, i ^ 1) for i in range(n_slab)])
+    mid = [(i, i + 1) for i in range(1, n_slab - 1, 2)]
+    far = lax.ppermute(jnp.where(odd, edges_last, edges), "slab", mid + [(j, i) for i, j in mid])
+    lateral, src, rec, oper = stage(lateral, src, rec, oper)
+    near, far, plane[1] = lax.optimization_barrier((near, far, plane[1]))
+    above = jnp.where(odd, near, far)
+    below = jnp.where(odd, far, near)
     blocks = []
     for block in plane:
         blocks += [block, xor_permute(block, "freq", 1)]
@@ -144,7 +170,7 @@
             pltpu.VMEM((2, tall, width), f32),
             pltpu.VMEM((2, tall, width), bf16),
         ],
-        compiler_params=pltpu.CompilerParams(vmem_limit_bytes=48 * MIB),
+        compiler_params=pltpu.CompilerParams(vmem_limit_bytes=12 * MIB),
         name="solve",
     )(
         where, shift, *blocks, oper, above[:, width:], below[:, width:], src, above[:, :width], below[:, :width],
@@ -159,10 +185,10 @@
         + [jax.ShapeDtypeStruct((rows, width), bf16)] * (n_chips - 1),
         in_specs=[SMEM] + [VMEM] * 4,
         out_specs=[VMEM] * n_chips,
-        compiler_params=pltpu.CompilerParams(vmem_limit_bytes=32 * MIB),
+        compiler_params=pltpu.CompilerParams(vmem_limit_bytes=10 * MIB),
         name="back",
     )(where, oper, oper_other, part, part_other)
-    gets = [xor_permute(send, "freq", 2 * (m + 1)) for m, send in enumerate(sends)]
+    gets = [xor_permute(sends[m - 1], "freq", 2 * m) for m in range(n_chips - 1, 0, -1)]
 
     tile = rows // n_slab
     own, *sends = pl.pallas_call(
@@ -171,11 +197,12 @@
         + [jax.ShapeDtypeStruct((tile, width), bf16)] * (n_slab - 1),
         in_specs=[SMEM] + [VMEM] * n_chips,
         out_specs=[VMEM] * n_slab,
-        compiler_params=pltpu.CompilerParams(vmem_limit_bytes=32 * MIB),
+        compiler_params=pltpu.CompilerParams(vmem_limit_bytes=10 * MIB),
         name="plane",
     )(where, keep, *gets)
-    for m, send in enumerate(sends):
-        own = own + xor_permute(send, "slab", m + 1).astype(f32)
+    gets = [xor_permute(sends[m - 1], "slab", m) for m in range(n_slab - 1, 0, -1)]
+    for got in gets:
+        own = own + got.astype(f32)
     return own
 
 

time: 85.2 us -> 66.7 us (0.78)
  waiting for transfers between devices: 38.9 us -> 26.3 us
  starting transfers between devices: 22.5 us -> 19.2 us
  local copies, waits for them, and re-layouts: 4.24 us -> 1.83 us
    ppermute x2, waiting for transfers between devices: 6.7 us -> 0.01 us  [the longest x1 0.01 us: shards(): lax.ppermute(jnp.where(odd, edges, edges_last), 'slab', [(i, i ^ 1) for i...]
    ppermute x18, waiting for transfers between devices: 32.2 us -> 26.3 us  [xor_permute(): return lax.ppermute(value, axis, [(i, i ^ mask) for i in range(size)])]
    pallas_call x0 -> x1, Pallas kernels: none -> 3.95 us  [stage(): pl.pallas_call(stage_kernel, out_shape=[pltpu.VMEM(a.shape, a.dtype) for...]
    pallas_call x1, Pallas kernels: 13.9 us -> 10.6 us  [shards(): pl.pallas_call(functools.partial(solve_kernel, n_freq, n_slab), out_shape...]
    ppermute x2, starting transfers between devices: 3.87 us -> 0.74 us  [the longest x1 0.67 us: shards(): lax.ppermute(jnp.where(odd, edges_last, edges), 'slab', mid + [(j, i) for...]
    unnamed x6 -> x5, local copies, waits for them, and re-layouts: 3.35 us -> 0.93 us
    concatenate x2 -> x0, other arithmetic: 0.87 us -> none  [the longest x1 0.86 us: shards(): line = jnp.concatenate(line, axis=0)]
  transfers between devices with their start and end apart: 20 -> 20, of which waited for: 12 -> 12; matrix products, arithmetic and copies ran while one was open for 2% -> 4% of each run, Pallas kernels for 0% -> 6%
where the time goes in v2:
time: 66.7 us; the launch traced here: 66.4 us
  waiting for transfers between devices  26.3 us (39%)
  starting transfers between devices  19.2 us (29%)
  Pallas kernels  16.7 us (25%)
  local copies, waits for them, and re-layouts  1.83 us (3%)
  other arithmetic  1.51 us (2%)
  between operations  0.8 us (1%)
    ppermute x18, waiting for transfers between devices, xor_permute(): return lax.ppermute(value, axis, [(i, i ^ mask) for i in range(size)])  26.3 us
    ppermute x18, starting transfers between devices, xor_permute(): return lax.ppermute(value, axis, [(i, i ^ mask) for i in range(size)])  18.5 us
    pallas_call x1, Pallas kernels, shards(): pl.pallas_call(functools.partial(solve_kernel, n_freq, n_slab), out_shape...  10.6 us
    pallas_call x1, Pallas kernels, stage(): pl.pallas_call(stage_kernel, out_shape=[pltpu.VMEM(a.shape, a.dtype) for...  3.95 us
    pallas_call x1, Pallas kernels, shards(): pl.pallas_call(functools.partial(back_kernel, n_chips), out_shape=[jax.Sh...  1.43 us
  transfers between devices with their start and end apart: 20, of which 12 were waited for; matrix products, arithmetic and copies ran while one was open for 4% of the time, Pallas kernels for 6%

profile of v2, /device:TPU:0, one launch (start us, length us, event | category | flops | bytes accessed | tf_op | source)
XLA Modules:
  0.0 66.4 jit_solution(11494870073857447754)
XLA Ops:
  0.0 3.0 %collective-permute-start.1 = (bf16[16,2048]{1,0:T(8,128)(2,1)}, bf16[16,2048]{1,0:T(8,128)(2,1)S(1)}, u32[]{:S(2)}, u32[]{:S(2)}) collective-permute-start(bf16[16,2048]{1,0:T(8,128)(2,1)} %param.6), channel_id=1, source_target_pairs={{0,1},{1,0},{2,3},{3,2},{4,5},{5,4},{6,7},{7,6},{8,9},{9,8},{10,11... | collective-permute-start | bytes 196616 | tf_op jit(solution)/shard_map/ppermute | solution.py:20
  3.0 2.6 %collective-permute-start.2 = (bf16[16,2048]{1,0:T(8,128)(2,1)}, bf16[16,2048]{1,0:T(8,128)(2,1)S(1)}, u32[]{:S(2)}, u32[]{:S(2)}) collective-permute-start(bf16[16,2048]{1,0:T(8,128)(2,1)} %param.6), channel_id=1, source_target_pairs={{0,2},{1,3},{2,0},{3,1},{4,6},{5,7},{6,4},{7,5},{8,10},{9,11},{10,... | collective-permute-start | bytes 196616 | tf_op jit(solution)/shard_map/ppermute | solution.py:20
  5.6 0.0 collective-permute-start.3
  5.6 0.9 %constant_dynamic-update-slice_fusion.3 = bf16[64,2048]{1,0:T(8,128)(2,1)S(1)} fusion(bf16[16,2048]{1,0:T(8,128)(2,1)} %param.6), kind=kLoop, calls=%fused_computation.12 | loop fusion | bytes 131072
  6.5 0.9 %slice_bitcast_fusion.1 = (f32[8,2048]{1,0:T(8,128)S(1)}, f32[8,2048]{1,0:T(8,128)S(1)}) fusion(f32[1,128,2048]{2,1,0:T(8,128)} %param.10), kind=kLoop, calls=%fused_computation.6 | loop fusion | bytes 262144 | tf_op jit(solution)/shard_map/slice | solution.py:145
  7.4 0.7 %bitcast_convert_fusion.1 = (f32[8,512]{1,0:T(8,128)S(1)}, f32[8,512]{1,0:T(8,128)S(1)}) fusion(bf16[1,128,512]{2,1,0:T(8,128)(2,1)} %param.7), kind=kLoop, calls=%fused_computation.14 | loop fusion | flops 8192 | bytes 49152 | tf_op jit(solution)/shard_map/convert_element_type | solution.py:145
  8.1 0.0 collective-permute-done.1
  8.1 2.4 %collective-permute-done.2 = bf16[16,2048]{1,0:T(8,128)(2,1)S(1)} collective-permute-done((bf16[16,2048]{1,0:T(8,128)(2,1)}, bf16[16,2048]{1,0:T(8,128)(2,1)S(1)}, u32[]{:S(2)}, u32[]{:S(2)}) %collective-permute-start.2) | collective-permute-done | bytes 65568 | tf_op jit(solution)/shard_map/ppermute | solution.py:20
  10.5 1.4 %collective-permute-done.3 = bf16[16,2048]{1,0:T(8,128)(2,1)S(1)} collective-permute-done((bf16[16,2048]{1,0:T(8,128)(2,1)}, bf16[16,2048]{1,0:T(8,128)(2,1)S(1)}, u32[]{:S(2)}, u32[]{:S(2)}) %collective-permute-start.3) | collective-permute-done | bytes 65568 | tf_op jit(solution)/shard_map/ppermute | solution.py:20
  11.9 1.5 %collective-permute-start.7 = (bf16[64,2048]{1,0:T(8,128)(2,1)S(1)}, bf16[64,2048]{1,0:T(8,128)(2,1)S(1)}, u32[]{:S(2)}, u32[]{:S(2)}) collective-permute-start(bf16[64,2048]{1,0:T(8,128)(2,1)S(1)} %constant_dynamic-update-slice_fusion.refs_0_), channel_id=1, source_target_pairs={{0,8},{4,12},{8,0},{12,4},{16,24},{20,28},{24,16},{28,20},{1,9},{5... | collective-permute-start | bytes 786440 | tf_op jit(solution)/shard_map/ppermute | solution.py:20
  13.4 1.5 %collective-permute-start.9 = (bf16[64,2048]{1,0:T(8,128)(2,1)S(1)}, bf16[64,2048]{1,0:T(8,128)(2,1)S(1)}, u32[]{:S(2)}, u32[]{:S(2)}) collective-permute-start(bf16[64,2048]{1,0:T(8,128)(2,1)S(1)} %constant_dynamic-update-slice_fusion.refs_0_), channel_id=1, source_target_pairs={{0,16},{4,20},{8,24},{12,28},{16,0},{20,4},{24,8},{28,12},{1,17},{... | collective-permute-start | bytes 786440 | tf_op jit(solution)/shard_map/ppermute | solution.py:20
  14.9 0.5 collective-permute-start.11
  15.4 0.1 collective-permute-start.5
  15.5 0.7 %collective-permute-start.6 = (f32[8,2560]{1,0:T(8,128)S(1)}, f32[8,2560]{1,0:T(8,128)S(1)}, u32[]{:S(2)}, u32[]{:S(2)}) collective-permute-start(f32[8,2560]{1,0:T(8,128)S(1)} %get-tuple-element.39), channel_id=1, source_target_pairs={{1,2},{2,1},{5,6},{6,5},{9,10},{10,9},{13,14},{14,13},{17,18},{18,... | collective-permute-start | bytes 245768 | tf_op jit(solution)/shard_map/ppermute | solution.py:151
  16.8 4.0 %stage.1 = (bf16[2048,2048]{1,0:T(8,128)(2,1)S(1)}, f32[128,2048]{1,0:T(8,128)S(1)}, f32[128,2048]{1,0:T(8,128)S(1)}, bf16[128,512]{1,0:T(8,128)(2,1)S(1)}) custom-call(bf16[2048,2048]{1,0:T(8,128)(2,1)} %refs_0_.1, f32[128,2048]{1,0:T(8,128)} %bitcast.15, f32[128,2048]{1,0:T(8,128)} %bitcast.16, bf16[128,512]{1,0:T(8,128)(2,1)} %bitcast.17), custom_call_target="tpu_custom_call" | custom-call | bytes 21233664 | tf_op jit(solution)/shard_map/stage/pallas_call | solution.py:79
  20.8 0.0 copy-start
  20.8 0.1 pad_add_fusion.where
  20.9 0.0 collective-permute-done.5
  20.9 0.0 collective-permute-start.4
  20.9 0.0 collective-permute-done.6
  20.9 0.2 collective-permute-done.7.refs_2_
  21.1 0.3 collective-permute-start.8
  21.4 3.7 %collective-permute-done.9.refs_4_ = bf16[64,2048]{1,0:T(8,128)(2,1)S(1)} collective-permute-done((bf16[64,2048]{1,0:T(8,128)(2,1)S(1)}, bf16[64,2048]{1,0:T(8,128)(2,1)S(1)}, u32[]{:S(2)}, u32[]{:S(2)}) %collective-permute-start.9) | collective-permute-done | bytes 262176 | tf_op jit(solution)/shard_map/ppermute | solution.py:20
  25.2 0.0 collective-permute-start.10
  25.2 0.0 collective-permute-done.11.refs_6_
  25.2 0.5 collective-permute-start.12
  25.7 0.0 collective-permute-done.4.refs_1_
  25.8 0.0 collective-permute-done.8.refs_3_
  25.8 0.9 %collective-permute-done.10.refs_5_ = bf16[64,2048]{1,0:T(8,128)(2,1)S(1)} collective-permute-done((bf16[64,2048]{1,0:T(8,128)(2,1)S(1)}, bf16[64,2048]{1,0:T(8,128)(2,1)S(1)}, u32[]{:S(2)}, u32[]{:S(2)}) %collective-permute-start.10) | collective-permute-done | bytes 262176 | tf_op jit(solution)/shard_map/ppermute | solution.py:20
  26.7 0.4 collective-permute-done.12.refs_7_
  27.1 10.6 %solve.1.part = bf16[128,2048]{1,0:T(8,128)(2,1)S(1)} custom-call(s32[2]{0:T(128)S(1)} %pad_add_fusion.where, f32[1]{0:T(128)S(6)} %copy.10.factor, bf16[64,2048]{1,0:T(8,128)(2,1)S(1)} %constant_dynamic-update-slice_fusion.refs_0_, bf16[64,2048]{1,0:T(8,128)(2,1)S(1)} %collective-permute-done.4.refs_1_, ...), custom_call_target="tpu_custom_call" | custom-call | tf_op jit(solution)/shard_map/solve/pallas_call | solution.py:160
  37.7 0.2 collective-permute-start.13
  37.9 0.0 copy-done
  37.9 0.4 collective-permute-start
  38.3 1.6 %collective-permute-done.oper_other = bf16[128,512]{1,0:T(8,128)(2,1)S(1)} collective-permute-done((bf16[128,512]{1,0:T(8,128)(2,1)S(1)}, bf16[128,512]{1,0:T(8,128)(2,1)S(1)}, u32[]{:S(2)}, u32[]{:S(2)}) %collective-permute-start) | collective-permute-done | bytes 131104 | tf_op jit(solution)/shard_map/ppermute | solution.py:20
  39.9 0.0 collective-permute-done.13.part_other
  39.9 1.4 %back.1 = (f32[64,2048]{1,0:T(8,128)S(1)}, bf16[64,2048]{1,0:T(8,128)(2,1)S(1)}, bf16[64,2048]{1,0:T(8,128)(2,1)S(1)}, bf16[64,2048]{1,0:T(8,128)(2,1)S(1)}) custom-call(s32[2]{0:T(128)S(1)} %pad_add_fusion.where, bf16[128,512]{1,0:T(8,128)(2,1)S(1)} %get-tuple-element.20.refs_8_.oper, bf16[128,512]{1,0:T(8,128)(2,1)S(1)} %collective-permute-done.oper_other, ...), custom_call_target="tpu_custom_call" | custom-call | tf_op jit(solution)/shard_map/back/pallas_call | solution.py:182
  41.3 1.6 %collective-permute-start.14 = (bf16[64,2048]{1,0:T(8,128)(2,1)S(1)}, bf16[64,2048]{1,0:T(8,128)(2,1)S(1)}, u32[]{:S(2)}, u32[]{:S(2)}) collective-permute-start(bf16[64,2048]{1,0:T(8,128)(2,1)S(1)} %get-tuple-element.28), channel_id=1, source_target_pairs={{0,24},{4,28},{8,16},{12,20},{16,8},{20,12},{24,0},{28,4},{1,25},{... | collective-permute-start | bytes 786440 | tf_op jit(solution)/shard_map/ppermute | solution.py:20
  42.9 0.8 %collective-permute-start.15 = (bf16[64,2048]{1,0:T(8,128)(2,1)S(1)}, bf16[64,2048]{1,0:T(8,128)(2,1)S(1)}, u32[]{:S(2)}, u32[]{:S(2)}) collective-permute-start(bf16[64,2048]{1,0:T(8,128)(2,1)S(1)} %get-tuple-element.29), channel_id=1, source_target_pairs={{0,16},{4,20},{8,24},{12,28},{16,0},{20,4},{24,8},{28,12},{1,17},{... | collective-permute-start | bytes 786440 | tf_op jit(solution)/shard_map/ppermute | solution.py:20
  43.7 1.2 %collective-permute-start.16 = (bf16[64,2048]{1,0:T(8,128)(2,1)S(1)}, bf16[64,2048]{1,0:T(8,128)(2,1)S(1)}, u32[]{:S(2)}, u32[]{:S(2)}) collective-permute-start(bf16[64,2048]{1,0:T(8,128)(2,1)S(1)} %get-tuple-element.30), channel_id=1, source_target_pairs={{0,8},{4,12},{8,0},{12,4},{16,24},{20,28},{24,16},{28,20},{1,9},{5... | collective-permute-start | bytes 786440 | tf_op jit(solution)/shard_map/ppermute | solution.py:20
  44.9 6.6 %collective-permute-done.14.refs_0_ = bf16[64,2048]{1,0:T(8,128)(2,1)S(1)} collective-permute-done((bf16[64,2048]{1,0:T(8,128)(2,1)S(1)}, bf16[64,2048]{1,0:T(8,128)(2,1)S(1)}, u32[]{:S(2)}, u32[]{:S(2)}) %collective-permute-start.14) | collective-permute-done | bytes 262176 | tf_op jit(solution)/shard_map/ppermute | solution.py:20
  51.5 4.8 %collective-permute-done.15.refs_1_ = bf16[64,2048]{1,0:T(8,128)(2,1)S(1)} collective-permute-done((bf16[64,2048]{1,0:T(8,128)(2,1)S(1)}, bf16[64,2048]{1,0:T(8,128)(2,1)S(1)}, u32[]{:S(2)}, u32[]{:S(2)}) %collective-permute-start.15) | collective-permute-done | bytes 262176 | tf_op jit(solution)/shard_map/ppermute | solution.py:20
  56.3 0.1 collective-permute-done.16.refs_2_
  56.4 0.7 plane.1
  57.0 1.1 %collective-permute-start.17 = (bf16[16,2048]{1,0:T(8,128)(2,1)S(1)}, bf16[16,2048]{1,0:T(8,128)(2,1)S(1)}, u32[]{:S(2)}, u32[]{:S(2)}) collective-permute-start(bf16[16,2048]{1,0:T(8,128)(2,1)S(1)} %get-tuple-element.32), channel_id=1, source_target_pairs={{0,3},{1,2},{2,1},{3,0},{4,7},{5,6},{6,5},{7,4},{8,11},{9,10},{10,... | collective-permute-start | bytes 196616 | tf_op jit(solution)/shard_map/ppermute | solution.py:20
  58.1 1.2 %collective-permute-start.18 = (bf16[16,2048]{1,0:T(8,128)(2,1)S(1)}, bf16[16,2048]{1,0:T(8,128)(2,1)S(1)}, u32[]{:S(2)}, u32[]{:S(2)}) collective-permute-start(bf16[16,2048]{1,0:T(8,128)(2,1)S(1)} %get-tuple-element.33), channel_id=1, source_target_pairs={{0,2},{1,3},{2,0},{3,1},{4,6},{5,7},{6,4},{7,5},{8,10},{9,11},{10,... | collective-permute-start | bytes 196616 | tf_op jit(solution)/shard_map/ppermute | solution.py:20
  59.2 2.2 %collective-permute-start.19 = (bf16[16,2048]{1,0:T(8,128)(2,1)S(1)}, bf16[16,2048]{1,0:T(8,128)(2,1)S(1)}, u32[]{:S(2)}, u32[]{:S(2)}) collective-permute-start(bf16[16,2048]{1,0:T(8,128)(2,1)S(1)} %get-tuple-element.34), channel_id=1, source_target_pairs={{0,1},{1,0},{2,3},{3,2},{4,5},{5,4},{6,7},{7,6},{8,9},{9,8},{10,11... | collective-permute-start | bytes 196616 | tf_op jit(solution)/shard_map/ppermute | solution.py:20
  61.5 2.4 %collective-permute-done.17 = bf16[16,2048]{1,0:T(8,128)(2,1)S(1)} collective-permute-done((bf16[16,2048]{1,0:T(8,128)(2,1)S(1)}, bf16[16,2048]{1,0:T(8,128)(2,1)S(1)}, u32[]{:S(2)}, u32[]{:S(2)}) %collective-permute-start.17) | collective-permute-done | bytes 65568 | tf_op jit(solution)/shard_map/ppermute | solution.py:20
  63.9 1.8 %collective-permute-done.18 = bf16[16,2048]{1,0:T(8,128)(2,1)S(1)} collective-permute-done((bf16[16,2048]{1,0:T(8,128)(2,1)S(1)}, bf16[16,2048]{1,0:T(8,128)(2,1)S(1)}, u32[]{:S(2)}, u32[]{:S(2)}) %collective-permute-start.18) | collective-permute-done | bytes 65568 | tf_op jit(solution)/shard_map/ppermute | solution.py:20
  65.7 0.0 collective-permute-done.19
  65.7 0.7 %convert_add_fusion = f32[16,2048]{1,0:T(8,128)} fusion(bf16[16,2048]{1,0:T(8,128)(2,1)S(1)} %collective-permute-done.19, bf16[16,2048]{1,0:T(8,128)(2,1)S(1)} %collective-permute-done.18, f32[16,2048]{1,0:T(8,128)S(1)} %get-tuple-element.31, bf16[16,2048]{1,0:T(8,128)(2,1)S(1)} %collective-permute-done.17), kind=kLoop, calls=%fused_computation | loop fusion | flops 196608 | bytes 458752 | tf_op jit(solution)/shard_map/add | solution.py:205
  (9 shorter events, 0.1 us)
Async XLA Ops:
  0.0 8.1 %collective-permute-start.1 = (bf16[16,2048]{1,0:T(8,128)(2,1)}, bf16[16,2048]{1,0:T(8,128)(2,1)S(1)}, u32[]{:S(2)}, u32[]{:S(2)}) collective-permute-start(bf16[16,2048]{1,0:T(8,128)(2,1)} %param.6), channel_id=1, source_target_pairs={{0,1},{1,0},{2,3},{3,2},{4,5},{5,4},{6,7},{7,6},{8,9},{9,8},{10,11... | collective-permute-start | bytes 196616 | tf_op jit(solution)/shard_map/ppermute | solution.py:20
  3.0 7.5 %collective-permute-start.2 = (bf16[16,2048]{1,0:T(8,128)(2,1)}, bf16[16,2048]{1,0:T(8,128)(2,1)S(1)}, u32[]{:S(2)}, u32[]{:S(2)}) collective-permute-start(bf16[16,2048]{1,0:T(8,128)(2,1)} %param.6), channel_id=1, source_target_pairs={{0,2},{1,3},{2,0},{3,1},{4,6},{5,7},{6,4},{7,5},{8,10},{9,11},{10,... | collective-permute-start | bytes 196616 | tf_op jit(solution)/shard_map/ppermute | solution.py:20
  5.6 6.3 %collective-permute-start.3 = (bf16[16,2048]{1,0:T(8,128)(2,1)}, bf16[16,2048]{1,0:T(8,128)(2,1)S(1)}, u32[]{:S(2)}, u32[]{:S(2)}) collective-permute-start(bf16[16,2048]{1,0:T(8,128)(2,1)} %param.6), channel_id=1, source_target_pairs={{0,3},{1,2},{2,1},{3,0},{4,7},{5,6},{6,5},{7,4},{8,11},{9,10},{10,... | collective-permute-start | bytes 196616 | tf_op jit(solution)/shard_map/ppermute | solution.py:20
  11.9 9.2 %collective-permute-start.7 = (bf16[64,2048]{1,0:T(8,128)(2,1)S(1)}, bf16[64,2048]{1,0:T(8,128)(2,1)S(1)}, u32[]{:S(2)}, u32[]{:S(2)}) collective-permute-start(bf16[64,2048]{1,0:T(8,128)(2,1)S(1)} %constant_dynamic-update-slice_fusion.refs_0_), channel_id=1, source_target_pairs={{0,8},{4,12},{8,0},{12,4},{16,24},{20,28},{24,16},{28,20},{1,9},{5... | collective-permute-start | bytes 786440 | tf_op jit(solution)/shard_map/ppermute | solution.py:20
  13.4 11.7 %collective-permute-start.9 = (bf16[64,2048]{1,0:T(8,128)(2,1)S(1)}, bf16[64,2048]{1,0:T(8,128)(2,1)S(1)}, u32[]{:S(2)}, u32[]{:S(2)}) collective-permute-start(bf16[64,2048]{1,0:T(8,128)(2,1)S(1)} %constant_dynamic-update-slice_fusion.refs_0_), channel_id=1, source_target_pairs={{0,16},{4,20},{8,24},{12,28},{16,0},{20,4},{24,8},{28,12},{1,17},{... | collective-permute-start | bytes 786440 | tf_op jit(solution)/shard_map/ppermute | solution.py:20
  14.9 10.2 %collective-permute-start.11 = (bf16[64,2048]{1,0:T(8,128)(2,1)S(1)}, bf16[64,2048]{1,0:T(8,128)(2,1)S(1)}, u32[]{:S(2)}, u32[]{:S(2)}) collective-permute-start(bf16[64,2048]{1,0:T(8,128)(2,1)S(1)} %constant_dynamic-update-slice_fusion.refs_0_), channel_id=1, source_target_pairs={{0,24},{4,28},{8,16},{12,20},{16,8},{20,12},{24,0},{28,4},{1,25},{... | collective-permute-start | bytes 786440 | tf_op jit(solution)/shard_map/ppermute | solution.py:20
  15.4 5.5 %collective-permute-start.5 = (f32[8,2560]{1,0:T(8,128)S(1)}, f32[8,2560]{1,0:T(8,128)S(1)}, u32[]{:S(2)}, u32[]{:S(2)}) collective-permute-start(f32[8,2560]{1,0:T(8,128)S(1)} %get-tuple-element.40), channel_id=1, source_target_pairs={{0,1},{1,0},{2,3},{3,2},{4,5},{5,4},{6,7},{7,6},{8,9},{9,8},{10,11... | collective-permute-start | bytes 245768 | tf_op jit(solution)/shard_map/ppermute | solution.py:149
  15.5 5.4 %collective-permute-start.6 = (f32[8,2560]{1,0:T(8,128)S(1)}, f32[8,2560]{1,0:T(8,128)S(1)}, u32[]{:S(2)}, u32[]{:S(2)}) collective-permute-start(f32[8,2560]{1,0:T(8,128)S(1)} %get-tuple-element.39), channel_id=1, source_target_pairs={{1,2},{2,1},{5,6},{6,5},{9,10},{10,9},{13,14},{14,13},{17,18},{18,... | collective-permute-start | bytes 245768 | tf_op jit(solution)/shard_map/ppermute | solution.py:151
  20.8 17.1 %copy-start = (bf16[1,128,512]{2,1,0:T(8,128)(2,1)S(1)}, bf16[1,128,512]{2,1,0:T(8,128)(2,1)}, u32[]{:S(2)}) copy-start(bf16[1,128,512]{2,1,0:T(8,128)(2,1)} %param.7) | copy-start | bytes 393220
  20.9 4.9 %collective-permute-start.4 = (bf16[64,2048]{1,0:T(8,128)(2,1)S(1)}, bf16[64,2048]{1,0:T(8,128)(2,1)S(1)}, u32[]{:S(2)}, u32[]{:S(2)}) collective-permute-start(bf16[64,2048]{1,0:T(8,128)(2,1)S(1)} %constant_dynamic-update-slice_fusion.refs_0_), channel_id=1, source_target_pairs={{0,4},{4,0},{8,12},{12,8},{16,20},{20,16},{24,28},{28,24},{1,5},{5... | collective-permute-start | bytes 786440 | tf_op jit(solution)/shard_map/ppermute | solution.py:20
  21.1 4.6 %collective-permute-start.8 = (bf16[64,2048]{1,0:T(8,128)(2,1)S(1)}, bf16[64,2048]{1,0:T(8,128)(2,1)S(1)}, u32[]{:S(2)}, u32[]{:S(2)}) collective-permute-start(bf16[64,2048]{1,0:T(8,128)(2,1)S(1)} %collective-permute-done.7.refs_2_), channel_id=1, source_target_pairs={{0,4},{4,0},{8,12},{12,8},{16,20},{20,16},{24,28},{28,24},{1,5},{5... | collective-permute-start | bytes 786440 | tf_op jit(solution)/shard_map/ppermute | solution.py:20
  25.2 1.5 %collective-permute-start.10 = (bf16[64,2048]{1,0:T(8,128)(2,1)S(1)}, bf16[64,2048]{1,0:T(8,128)(2,1)S(1)}, u32[]{:S(2)}, u32[]{:S(2)}) collective-permute-start(bf16[64,2048]{1,0:T(8,128)(2,1)S(1)} %collective-permute-done.9.refs_4_), channel_id=1, source_target_pairs={{0,4},{4,0},{8,12},{12,8},{16,20},{20,16},{24,28},{28,24},{1,5},{5... | collective-permute-start | bytes 786440 | tf_op jit(solution)/shard_map/ppermute | solution.py:20
  25.2 1.9 %collective-permute-start.12 = (bf16[64,2048]{1,0:T(8,128)(2,1)S(1)}, bf16[64,2048]{1,0:T(8,128)(2,1)S(1)}, u32[]{:S(2)}, u32[]{:S(2)}) collective-permute-start(bf16[64,2048]{1,0:T(8,128)(2,1)S(1)} %collective-permute-done.11.refs_6_), channel_id=1, source_target_pairs={{0,4},{4,0},{8,12},{12,8},{16,20},{20,16},{24,28},{28,24},{1,5},{5... | collective-permute-start | bytes 786440 | tf_op jit(solution)/shard_map/ppermute | solution.py:20
  37.7 2.2 %collective-permute-start.13 = (bf16[128,2048]{1,0:T(8,128)(2,1)S(1)}, bf16[128,2048]{1,0:T(8,128)(2,1)S(1)}, u32[]{:S(2)}, u32[]{:S(2)}) collective-permute-start(bf16[128,2048]{1,0:T(8,128)(2,1)S(1)} %solve.1.part), channel_id=1, source_target_pairs={{0,4},{4,0},{8,12},{12,8},{16,20},{20,16},{24,28},{28,24},{1,5},{5... | collective-permute-start | bytes 1572872 | tf_op jit(solution)/shard_map/ppermute | solution.py:20
  37.9 2.0 %collective-permute-start = (bf16[128,512]{1,0:T(8,128)(2,1)S(1)}, bf16[128,512]{1,0:T(8,128)(2,1)S(1)}, u32[]{:S(2)}, u32[]{:S(2)}) collective-permute-start(bf16[128,512]{1,0:T(8,128)(2,1)S(1)} %bitcast.18), channel_id=1, source_target_pairs={{0,4},{4,0},{8,12},{12,8},{16,20},{20,16},{24,28},{28,24},{1,5},{5... | collective-permute-start | bytes 393224 | tf_op jit(solution)/shard_map/ppermute | solution.py:20
  41.3 10.2 %collective-permute-start.14 = (bf16[64,2048]{1,0:T(8,128)(2,1)S(1)}, bf16[64,2048]{1,0:T(8,128)(2,1)S(1)}, u32[]{:S(2)}, u32[]{:S(2)}) collective-permute-start(bf16[64,2048]{1,0:T(8,128)(2,1)S(1)} %get-tuple-element.28), channel_id=1, source_target_pairs={{0,24},{4,28},{8,16},{12,20},{16,8},{20,12},{24,0},{28,4},{1,25},{... | collective-permute-start | bytes 786440 | tf_op jit(solution)/shard_map/ppermute | solution.py:20
  42.9 13.4 %collective-permute-start.15 = (bf16[64,2048]{1,0:T(8,128)(2,1)S(1)}, bf16[64,2048]{1,0:T(8,128)(2,1)S(1)}, u32[]{:S(2)}, u32[]{:S(2)}) collective-permute-start(bf16[64,2048]{1,0:T(8,128)(2,1)S(1)} %get-tuple-element.29), channel_id=1, source_target_pairs={{0,16},{4,20},{8,24},{12,28},{16,0},{20,4},{24,8},{28,12},{1,17},{... | collective-permute-start | bytes 786440 | tf_op jit(solution)/shard_map/ppermute | solution.py:20
  43.7 12.6 %collective-permute-start.16 = (bf16[64,2048]{1,0:T(8,128)(2,1)S(1)}, bf16[64,2048]{1,0:T(8,128)(2,1)S(1)}, u32[]{:S(2)}, u32[]{:S(2)}) collective-permute-start(bf16[64,2048]{1,0:T(8,128)(2,1)S(1)} %get-tuple-element.30), channel_id=1, source_target_pairs={{0,8},{4,12},{8,0},{12,4},{16,24},{20,28},{24,16},{28,20},{1,9},{5... | collective-permute-start | bytes 786440 | tf_op jit(solution)/shard_map/ppermute | solution.py:20
  57.0 6.8 %collective-permute-start.17 = (bf16[16,2048]{1,0:T(8,128)(2,1)S(1)}, bf16[16,2048]{1,0:T(8,128)(2,1)S(1)}, u32[]{:S(2)}, u32[]{:S(2)}) collective-permute-start(bf16[16,2048]{1,0:T(8,128)(2,1)S(1)} %get-tuple-element.32), channel_id=1, source_target_pairs={{0,3},{1,2},{2,1},{3,0},{4,7},{5,6},{6,5},{7,4},{8,11},{9,10},{10,... | collective-permute-start | bytes 196616 | tf_op jit(solution)/shard_map/ppermute | solution.py:20
  58.1 7.6 %collective-permute-start.18 = (bf16[16,2048]{1,0:T(8,128)(2,1)S(1)}, bf16[16,2048]{1,0:T(8,128)(2,1)S(1)}, u32[]{:S(2)}, u32[]{:S(2)}) collective-permute-start(bf16[16,2048]{1,0:T(8,128)(2,1)S(1)} %get-tuple-element.33), channel_id=1, source_target_pairs={{0,2},{1,3},{2,0},{3,1},{4,6},{5,7},{6,4},{7,5},{8,10},{9,11},{10,... | collective-permute-start | bytes 196616 | tf_op jit(solution)/shard_map/ppermute | solution.py:20
  59.2 6.5 %collective-permute-start.19 = (bf16[16,2048]{1,0:T(8,128)(2,1)S(1)}, bf16[16,2048]{1,0:T(8,128)(2,1)S(1)}, u32[]{:S(2)}, u32[]{:S(2)}) collective-permute-start(bf16[16,2048]{1,0:T(8,128)(2,1)S(1)} %get-tuple-element.34), channel_id=1, source_target_pairs={{0,1},{1,0},{2,3},{3,2},{4,5},{5,4},{6,7},{7,6},{8,9},{9,8},{10,11... | collective-permute-start | bytes 196616 | tf_op jit(solution)/shard_map/ppermute | solution.py:20

commit v3 on v0

v3 whole, which is shorter than its diff:
```python
import functools

import jax
import jax.numpy as jnp
from jax import lax
from jax.experimental import pallas as pl
from jax.experimental.pallas import tpu as pltpu
from jax.sharding import PartitionSpec as P

SWEEPS = 8
HALO = 8
Z_ORDER = (1, 2, 3)
XY_ORDER = (3, 2, 1)
XYB_ORDER = (3, 2, 1)
ZB_ORDER = (1, 2, 3)
XYB2_ORDER = (1, 2, 3)
TILE = 256
MIB = 1 << 20
VMEM = pl.BlockSpec(memory_space=pltpu.VMEM)
SMEM = pl.BlockSpec(memory_space=pltpu.SMEM)


def xor_permute(value, axis, mask):
    size = lax.axis_size(axis)
    return lax.ppermute(value, axis, [(i, i ^ mask) for i in range(size)])


def solve_kernel(n_blocks, n_slab, where, factor, *refs):
    blocks = refs[:n_blocks]
    oper, oper_up, oper_down, src, src_up, src_down, rec, lateral, moved = refs[n_blocks : n_blocks + 9]
    out, inverse, field, field_lo = refs[n_blocks + 9 :]
    slab = where[1]
    depth, width = src.shape
    tall = depth + 2 * HALO

    def source(cols):
        return jnp.concatenate([src_up[:, cols], src[:, cols], src_down[:, cols]], axis=0)

    rows = jnp.concatenate([oper_up[...], oper[...].astype(jnp.float32), oper_down[...]], axis=0)
    basis = jnp.dot(rows.astype(jnp.bfloat16), moved[...], preferred_element_type=jnp.float32).astype(jnp.bfloat16)
    at = lax.broadcasted_iota(jnp.int32, (tall, TILE), 0) - HALO + slab * depth
    inside = jnp.logical_and(at >= 0, at < n_slab * depth)
    for n in range(0, width, TILE):
        cols = slice(n, n + TILE)
        fine = jnp.concatenate([block[:, cols] for block in blocks], axis=0)
        coarse = jnp.dot(basis, fine, preferred_element_type=jnp.float32)
        damped = jnp.where(inside, 1.0 / (4.0 + factor[0] * coarse * coarse), 0.0)
        inverse[:, cols] = damped
        first = source(cols) * damped
        field[0, :, cols] = first
        field_lo[0, :, cols] = first.astype(jnp.bfloat16)
    for sweep in range(1, SWEEPS - 1):
        old, new = (sweep - 1) % 2, sweep % 2
        for n in range(0, width, TILE):
            cols = slice(n, n + TILE)
            side = jnp.dot(field_lo[old], lateral[:, cols], preferred_element_type=jnp.float32)
            before = field[old, :, cols]
            beside = pltpu.roll(before, 1, 0) + pltpu.roll(before, tall - 1, 0)
            after = (source(cols) + 0.5 * beside + side) * inverse[:, cols]
            field[new, :, cols] = after
            field_lo[new, :, cols] = after.astype(jnp.bfloat16)
    old = (SWEEPS - 2) % 2
    mine = slice(HALO, HALO + depth)
    for n in range(0, width, TILE):
        cols = slice(n, n + TILE)
        side = jnp.dot(field_lo[old], lateral[:, cols], preferred_element_type=jnp.float32)
        before = field[old, :, cols]
        beside = pltpu.roll(before, 1, 0) + pltpu.roll(before, tall - 1, 0)
        after = (src[:, cols] + 0.5 * beside[mine] + side[mine]) * inverse[mine, cols]
        out[:, cols] = (after * rec[:, cols]).astype(jnp.bfloat16)


def stage_kernel(order, n_freq, n_slab, tile, where, oper, oper_other, *refs):
    count = (len(refs) - 4) // 2
    moved, turned, sems, upright = refs[-4:]
    copies = [pltpu.make_async_copy(refs[i], refs[count + i], sems.at[i]) for i in range(count)]
    for copy in copies:
        copy.start()
    freq, slab = where[0], where[1]
    size = moved.shape[0]
    place = lax.broadcasted_iota(jnp.int32, (1, size), 1)
    held = jnp.zeros((1, size), jnp.int32)
    for t, (g, j) in enumerate(order):
        begin = ((freq ^ g) * n_slab + (slab ^ j)) * tile
        held = jnp.where(place >= t * tile, begin + place - t * tile, held)
    step = min(size, 128)
    for n in range(0, size, step):
        row = lax.broadcasted_iota(jnp.int32, (step, size), 0) + n
        moved[n : n + step, :] = jnp.where(row == held, 1.0, 0.0).astype(jnp.bfloat16)
    core, chip = lax.rem(freq, 2), lax.div(freq, 2)
    half = n_slab * tile
    depth = oper.shape[0]
    for m in range(n_freq // 2):
        for b, ref in enumerate((oper, oper_other)):
            at = pl.multiple_of((chip ^ m) * (2 * half), 2 * half)
            pair = ref[:, pl.ds(at, 2 * half)].astype(jnp.float32)
            mine = jnp.where(core == 0, pair[:, :half], pair[:, half:])
            upright[m, :, b * depth : (b + 1) * depth] = mine.T
    for m in range(n_freq // 2):
        for j in range(n_slab):
            at = pl.ds(pl.multiple_of((slab ^ j) * tile, tile), tile)
            begin = m * half + j * tile
            turned[begin : begin + tile, :] = upright[m, at, :].astype(jnp.bfloat16)
    for copy in copies:
        copy.wait()


def stage(where, order, n_freq, n_slab, tile, oper, oper_other, *arrays):
    size, depth = oper.shape[1], oper.shape[0]
    results = [pltpu.VMEM(a.shape, a.dtype) for a in arrays]
    results += [pltpu.VMEM((size, size), jnp.bfloat16), pltpu.VMEM((size // 2, 2 * depth), jnp.bfloat16)]
    held = sum(a.size * a.dtype.itemsize for a in arrays) + 2 * size * size + 2 * size * depth
    return pl.pallas_call(
        functools.partial(stage_kernel, order, n_freq, n_slab, tile),
        out_shape=results,
        in_specs=[SMEM, VMEM, VMEM] + [pl.BlockSpec(memory_space=pl.ANY)] * len(arrays),
        out_specs=[VMEM] * len(results),
        scratch_shapes=[
            pltpu.SemaphoreType.DMA((len(arrays),)),
            pltpu.VMEM((n_freq // 2, n_slab * tile, 2 * depth), jnp.float32),
        ],
        compiler_params=pltpu.CompilerParams(vmem_limit_bytes=58 * MIB - held),
        cost_estimate=cost(0, 2 * held),
        name="stage",
    )(where, oper, oper_other, *arrays)


def back_kernel(n_chips, tile, turned, part, part_other, keep, *sends):
    half, width = keep.shape
    far, near = sends[: n_chips - 1], sends[n_chips - 1 :]
    for n in range(0, width, TILE):
        cols = slice(n, n + TILE)
        both = jnp.concatenate([part[:, cols], part_other[:, cols]], axis=0)
        total = jnp.dot(turned[...], both, preferred_element_type=jnp.float32)
        keep[:, cols] = total[:half]
        for m in range(1, n_chips):
            rows = total[m * half : (m + 1) * half].astype(jnp.bfloat16)
            near[m - 1][:, cols] = rows[:tile]
            far[m - 1][:, cols] = rows[tile:]


def plane_kernel(n_chips, tile, keep, *refs):
    gets, sends = refs[: n_chips - 1], refs[n_chips - 1 :]
    for n in range(0, keep.shape[1], TILE):
        cols = slice(n, n + TILE)
        total = keep[tile:, cols]
        for got in gets:
            total += got[:, cols].astype(jnp.float32)
        total = total.astype(jnp.bfloat16)
        for j, send in enumerate(sends):
            send[:, cols] = total[j * tile : (j + 1) * tile]


def turns(size, order):
    return [m for m in order if m < size] + [m for m in range(1, size) if m not in order]


def cost(flops, accessed):
    return pl.CostEstimate(flops=int(flops), bytes_accessed=int(accessed), transcendentals=0)


def shards(fine_model, resample, lateral, shift, source, receiver):
    n_freq, n_slab = lax.axis_size("freq"), lax.axis_size("slab")
    n_chips = n_freq // 2
    oper, src, rec = resample[0], source[0], receiver[0]
    depth, width = src.shape
    n_fine = oper.shape[1]
    tall = depth + 2 * HALO
    where = jnp.stack([lax.axis_index("freq"), lax.axis_index("slab")]).astype(jnp.int32)
    f32, bf16 = jnp.float32, jnp.bfloat16

    line = dict((m, xor_permute(fine_model, "slab", m)) for m in turns(n_slab, Z_ORDER))
    line = [line[m] for m in range(1, n_slab)]
    edges = jnp.concatenate([src[:HALO], oper[:HALO].astype(f32)], axis=1)
    edges_last = jnp.concatenate([src[depth - HALO :], oper[depth - HALO :].astype(f32)], axis=1)
    oper_other = xor_permute(oper, "freq", 1)
    line, edges, edges_last, lateral, src, rec, oper, oper_other = lax.optimization_barrier(
        (line, edges, edges_last, lateral, src, rec, oper, oper_other)
    )
    line = jnp.concatenate([fine_model] + line, axis=0)
    plane = dict((m, xor_permute(line, "freq", 2 * m)) for m in turns(n_chips, XY_ORDER))
    plane = [line] + [plane[m] for m in range(1, n_chips)]
    odd = lax.rem(lax.axis_index("slab"), 2) == 1
    mid = [(i, i + 1) for i in range(1, n_slab - 1, 2)]
    far = lax.ppermute(jnp.where(odd, edges_last, edges), "slab", mid + [(j, i) for i, j in mid])
    near = lax.ppermute(jnp.where(odd, edges, edges_last), "slab", [(i, i ^ 1) for i in range(n_slab)])

    tile = fine_model.shape[0]
    order = [(2 * m + b, j) for m in range(n_chips) for b in range(2) for j in range(n_slab)]
    lateral, src, rec, moved, turned = stage(where, order, n_freq, n_slab, tile, oper, oper_other, lateral, src, rec)
    far, near, plane[1] = lax.optimization_barrier((far, near, plane[1]))
    above = jnp.where(odd, near, far)
    below = jnp.where(odd, far, near)
    blocks = []
    for block in plane:
        blocks += [block, xor_permute(block, "freq", 1)]

    part = pl.pallas_call(
        functools.partial(solve_kernel, len(blocks), n_slab),
        out_shape=pltpu.VMEM((depth, width), bf16),
        in_specs=[SMEM, SMEM] + [VMEM] * (len(blocks) + 9),
        out_specs=VMEM,
        scratch_shapes=[
            pltpu.VMEM((tall, width), f32),
            pltpu.VMEM((2, tall, width), f32),
            pltpu.VMEM((2, tall, width), bf16),
        ],
        compiler_params=pltpu.CompilerParams(vmem_limit_bytes=12 * MIB),
        cost_estimate=cost(2 * (SWEEPS - 1) * tall * width * width, 2 * width * width),
        name="solve",
    )(
        where, shift, *blocks, oper, above[:, width:], below[:, width:], src, above[:, :width], below[:, :width],
        rec, lateral, moved,
    )
    tile = n_fine // (n_freq * n_slab)
    keep, sends, level = back(turned, part, tile)
    gets = [xor_permute(sends[m - 1], "freq", 2 * m) for m in turns(n_chips, XYB_ORDER)]

    sends = pl.pallas_call(
        functools.partial(plane_kernel, n_chips, tile),
        out_shape=[jax.ShapeDtypeStruct((tile, width), bf16)] * (n_slab - 1),
        in_specs=[VMEM] * n_chips,
        out_specs=[VMEM] * (n_slab - 1),
        compiler_params=pltpu.CompilerParams(vmem_limit_bytes=6 * MIB),
        cost_estimate=cost(0, 4 * n_slab * tile * width * (n_chips + 1)),
        name="plane",
    )(keep, *gets)
    own = keep[:tile]
    for m in turns(n_chips, XYB2_ORDER):
        own = own + xor_permute(level[m - 1], "freq", 2 * m).astype(f32)
    for m in turns(n_slab, ZB_ORDER):
        own = own + xor_permute(sends[m - 1], "slab", m).astype(f32)
    return own


def back(turned, part, tile):
    n_chips = lax.axis_size("freq") // 2
    rows, width = turned.shape[0] // n_chips, part.shape[1]
    others = n_chips - 1
    keep, *sends = pl.pallas_call(
        functools.partial(back_kernel, n_chips, tile),
        out_shape=[jax.ShapeDtypeStruct((rows, width), jnp.float32)]
        + [jax.ShapeDtypeStruct((rows - tile, width), jnp.bfloat16)] * others
        + [jax.ShapeDtypeStruct((tile, width), jnp.bfloat16)] * others,
        in_specs=[VMEM] * 3,
        out_specs=[VMEM] * (2 * n_chips - 1),
        compiler_params=pltpu.CompilerParams(vmem_limit_bytes=6 * MIB),
        cost_estimate=cost(2 * turned.size * width, 4 * n_chips * rows * width),
        name="back",
    )(turned, part, xor_permute(part, "freq", 1))
    return keep, sends[:others], sends[others:]


def solution(mesh):
    in_specs = (
        P(("freq", "slab"), None),
        P("freq", "slab", None),
        P(),
        P("freq"),
        P("freq", "slab", None),
        P("freq", "slab", None),
    )
    out_specs = P(("freq", "slab"), None)
    return jax.shard_map(shards, mesh=mesh, in_specs=in_specs, out_specs=out_specs, check_vma=False)
```

time: 309 us -> 63.7 us (0.21)
  waiting for transfers between devices: 215 us -> 15.5 us
  matrix products: 24.6 us -> 0 us
  starting transfers between devices: 49.1 us -> 27 us
  Pallas kernels: 0 us -> 16.3 us
  between operations: 14.4 us -> 0.82 us
  local copies, waits for them, and re-layouts: 5.56 us -> 1.78 us
    reduce_scatter x1 -> x0, waiting for transfers between devices: 150 us -> none  [shards(): lax.psum_scatter(lax.dot_general(columns, partial_img, (((0,), (0,)), (()...]
    all_gather x1 -> x0, waiting for transfers between devices: 55.3 us -> none  [shards(): lax.all_gather(fine_model, ('freq', 'slab'), axis=0, tiled=True)]
    dot_general x9 -> x0, matrix products: 24.6 us -> none  [the longest x7 14.7 us: shards(): jnp.dot(field.astype(jnp.bfloat16), lateral, preferred_element_type=jnp.f...]
    ppermute x16 -> x23, starting transfers between devices: 49 us -> 27 us  [the longest x21 22.9 us: xor_permute(): return lax.ppermute(value, axis, [(i, i ^ mask) for i in range(size)])]
    pallas_call x0 -> x4, Pallas kernels: none -> 16.3 us  [the longest x1 10.6 us: shards(): pl.pallas_call(functools.partial(solve_kernel, len(blocks), n_slab), out_...]
    ppermute x16 -> x23, waiting for transfers between devices: 9.21 us -> 15.5 us  [the longest x21 15.5 us: xor_permute(): return lax.ppermute(value, axis, [(i, i ^ mask) for i in range(size)])]
    unnamed x11 -> x9, local copies, waits for them, and re-layouts: 5.46 us -> 0.87 us
  transfers between devices with their start and end apart: 18 -> 23, of which waited for: 9 -> 12; matrix products, arithmetic and copies ran while one was open for 1% -> 5% of each run, Pallas kernels for 0% -> 8%
where the time goes in v3:
time: 63.7 us; the launch traced here: 63.4 us
  starting transfers between devices  27 us (42%)
  Pallas kernels  16.3 us (26%)
  waiting for transfers between devices  15.5 us (24%)
  other arithmetic  2.05 us (3%)
  local copies, waits for them, and re-layouts  1.78 us (3%)
  between operations  0.82 us (1%)
    ppermute x21, starting transfers between devices, xor_permute(): return lax.ppermute(value, axis, [(i, i ^ mask) for i in range(size)])  22.9 us
    ppermute x21, waiting for transfers between devices, xor_permute(): return lax.ppermute(value, axis, [(i, i ^ mask) for i in range(size)])  15.5 us
    pallas_call x1, Pallas kernels, shards(): pl.pallas_call(functools.partial(solve_kernel, len(blocks), n_slab), out_...  10.6 us
    pallas_call x1, Pallas kernels, stage(): pl.pallas_call(functools.partial(stage_kernel, order, n_freq, n_slab, til...  5.06 us
    ppermute x1, starting transfers between devices, shards(): lax.ppermute(jnp.where(odd, edges, edges_last), 'slab', [(i, i ^ 1) for i...  3.43 us
  transfers between devices with their start and end apart: 23, of which 12 were waited for; matrix products, arithmetic and copies ran while one was open for 5% of the time, Pallas kernels for 8%

profile of v3, /device:TPU:0, one launch (start us, length us, event | category | flops | bytes accessed | tf_op | source)
XLA Modules:
  0.0 63.4 jit_solution(13028767275071661503)
XLA Ops:
  0.0 0.0 copy-start
  0.0 3.0 %collective-permute-start = (bf16[16,2048]{1,0:T(8,128)(2,1)}, bf16[16,2048]{1,0:T(8,128)(2,1)S(1)}, u32[]{:S(2)}, u32[]{:S(2)}) collective-permute-start(bf16[16,2048]{1,0:T(8,128)(2,1)} %param.6), channel_id=1, source_target_pairs={{0,1},{1,0},{2,3},{3,2},{4,5},{5,4},{6,7},{7,6},{8,9},{9,8},{10,11... | collective-permute-start | bytes 196616 | tf_op jit(solution)/shard_map/ppermute | solution.py:25
  3.0 2.6 %collective-permute-start.1 = (bf16[16,2048]{1,0:T(8,128)(2,1)}, bf16[16,2048]{1,0:T(8,128)(2,1)S(1)}, u32[]{:S(2)}, u32[]{:S(2)}) collective-permute-start(bf16[16,2048]{1,0:T(8,128)(2,1)} %param.6), channel_id=1, source_target_pairs={{0,2},{1,3},{2,0},{3,1},{4,6},{5,7},{6,4},{7,5},{8,10},{9,11},{10,... | collective-permute-start | bytes 196616 | tf_op jit(solution)/shard_map/ppermute | solution.py:25
  5.6 0.0 collective-permute-start.2
  5.6 0.0 collective-permute-start.3
  5.6 0.7 %bitcast_convert_fusion = (f32[8,512]{1,0:T(8,128)S(1)}, f32[8,512]{1,0:T(8,128)S(1)}) fusion(bf16[1,128,512]{2,1,0:T(8,128)(2,1)} %param.7), kind=kLoop, calls=%fused_computation.13 | loop fusion | flops 8192 | bytes 49152 | tf_op jit(solution)/shard_map/convert_element_type | solution.py:175
  6.3 0.9 %slice_bitcast_fusion = (f32[8,2048]{1,0:T(8,128)S(1)}, f32[8,2048]{1,0:T(8,128)S(1)}) fusion(f32[1,128,2048]{2,1,0:T(8,128)} %param.10), kind=kLoop, calls=%fused_computation.3 | loop fusion | bytes 262144 | tf_op jit(solution)/shard_map/slice | solution.py:175
  7.2 0.8 %constant_dynamic-update-slice_fusion.3 = bf16[64,2048]{1,0:T(8,128)(2,1)S(1)} fusion(bf16[16,2048]{1,0:T(8,128)(2,1)} %param.6), kind=kLoop, calls=%fused_computation.12 | loop fusion | bytes 131072
  8.7 0.0 collective-permute-done
  8.8 1.8 %collective-permute-done.1 = bf16[16,2048]{1,0:T(8,128)(2,1)S(1)} collective-permute-done((bf16[16,2048]{1,0:T(8,128)(2,1)}, bf16[16,2048]{1,0:T(8,128)(2,1)S(1)}, u32[]{:S(2)}, u32[]{:S(2)}) %collective-permute-start.1) | collective-permute-done | bytes 65568 | tf_op jit(solution)/shard_map/ppermute | solution.py:25
  10.5 1.4 %collective-permute-done.2 = bf16[16,2048]{1,0:T(8,128)(2,1)S(1)} collective-permute-done((bf16[16,2048]{1,0:T(8,128)(2,1)}, bf16[16,2048]{1,0:T(8,128)(2,1)S(1)}, u32[]{:S(2)}, u32[]{:S(2)}) %collective-permute-start.2) | collective-permute-done | bytes 65568 | tf_op jit(solution)/shard_map/ppermute | solution.py:25
  11.9 0.0 collective-permute-done.3.oper_other
  11.9 0.0 copy-start.2
  12.0 1.6 %collective-permute-start.7 = (bf16[64,2048]{1,0:T(8,128)(2,1)S(1)}, bf16[64,2048]{1,0:T(8,128)(2,1)S(1)}, u32[]{:S(2)}, u32[]{:S(2)}) collective-permute-start(bf16[64,2048]{1,0:T(8,128)(2,1)S(1)} %constant_dynamic-update-slice_fusion.refs_0_), channel_id=1, source_target_pairs={{0,8},{4,12},{8,0},{12,4},{16,24},{20,28},{24,16},{28,20},{1,9},{5... | collective-permute-start | bytes 786440 | tf_op jit(solution)/shard_map/ppermute | solution.py:25
  13.5 1.5 %collective-permute-start.9 = (bf16[64,2048]{1,0:T(8,128)(2,1)S(1)}, bf16[64,2048]{1,0:T(8,128)(2,1)S(1)}, u32[]{:S(2)}, u32[]{:S(2)}) collective-permute-start(bf16[64,2048]{1,0:T(8,128)(2,1)S(1)} %constant_dynamic-update-slice_fusion.refs_0_), channel_id=1, source_target_pairs={{0,16},{4,20},{8,24},{12,28},{16,0},{20,4},{24,8},{28,12},{1,17},{... | collective-permute-start | bytes 786440 | tf_op jit(solution)/shard_map/ppermute | solution.py:25
  15.0 0.5 collective-permute-start.11
  15.5 0.7 %collective-permute-start.5 = (f32[8,2560]{1,0:T(8,128)S(1)}, f32[8,2560]{1,0:T(8,128)S(1)}, u32[]{:S(2)}, u32[]{:S(2)}) collective-permute-start(f32[8,2560]{1,0:T(8,128)S(1)} %get-tuple-element.66), channel_id=1, source_target_pairs={{1,2},{2,1},{5,6},{6,5},{9,10},{10,9},{13,14},{14,13},{17,18},{18,... | collective-permute-start | bytes 245768 | tf_op jit(solution)/shard_map/ppermute | solution.py:185
  16.2 3.4 %collective-permute-start.6 = (f32[8,2560]{1,0:T(8,128)S(1)}, f32[8,2560]{1,0:T(8,128)S(1)}, u32[]{:S(2)}, u32[]{:S(2)}) collective-permute-start(f32[8,2560]{1,0:T(8,128)S(1)} %get-tuple-element.65), channel_id=1, source_target_pairs={{0,1},{1,0},{2,3},{3,2},{4,5},{5,4},{6,7},{7,6},{8,9},{9,8},{10,11... | collective-permute-start | bytes 245768 | tf_op jit(solution)/shard_map/ppermute | solution.py:186
  19.6 0.6 pad_add_fusion.where
  20.2 0.0 copy-done.2
  20.2 0.0 copy-start.1
  20.2 5.1 %stage.1 = (bf16[2048,2048]{1,0:T(8,128)(2,1)S(1)}, f32[128,2048]{1,0:T(8,128)S(1)}, f32[128,2048]{1,0:T(8,128)S(1)}, bf16[512,512]{1,0:T(8,128)(2,1)S(1)}, bf16[256,256]{1,0:T(8,128)(2,1)S(1)}) custom-call(s32[2]{0:T(128)} %pad_add_fusion.where, bf16[128,512]{1,0:T(8,128)(2,1)} %bitcast.16, bf16[128,512]{1,0:T(8,128)(2,1)} %copy-done.2, ...), custom_call_target="tpu_custom_call" | custom-call | bytes 22282240 | tf_op jit(solution)/shard_map/stage/pallas_call | solution.py:113
  25.3 0.0 collective-permute-done.5
  25.3 0.1 collective-permute-start.4
  25.4 0.0 collective-permute-done.6
  25.4 0.0 collective-permute-done.7.refs_2_
  25.4 0.5 collective-permute-start.8
  25.9 0.0 collective-permute-done.9.refs_4_
  25.9 0.1 collective-permute-start.10
  26.0 0.0 collective-permute-done.11.refs_6_
  26.0 0.4 collective-permute-start.12
  26.5 0.4 collective-permute-done.4.refs_1_
  26.9 0.4 collective-permute-done.8.refs_3_
  27.3 0.4 collective-permute-done.10.refs_5_
  27.7 0.4 collective-permute-done.12.refs_7_
  28.0 0.0 copy-done
  28.0 0.0 copy-done.1
  28.0 10.6 %solve.1.part = bf16[128,2048]{1,0:T(8,128)(2,1)S(1)} custom-call(s32[2]{0:T(128)S(1)} %copy-done.1, f32[1]{0:T(128)S(6)} %copy.10.factor, bf16[64,2048]{1,0:T(8,128)(2,1)S(1)} %constant_dynamic-update-slice_fusion.refs_0_, bf16[64,2048]{1,0:T(8,128)(2,1)S(1)} %collective-permute-done.4.refs_1_, bf16[64,2048]{1,0:T(8,128)(2,1)S(1)} %collective-permute-done.7.refs_2_, ...), custom_call_target="tpu_custom_call" | custom-call | flops 8455716864 | bytes 8388608 | tf_op jit(solution)/shard_map/solve/pallas_call | solution.py:198
  38.7 0.2 collective-permute-start.13
  38.9 1.8 %collective-permute-done.13.part_other = bf16[128,2048]{1,0:T(8,128)(2,1)S(1)} collective-permute-done((bf16[128,2048]{1,0:T(8,128)(2,1)S(1)}, bf16[128,2048]{1,0:T(8,128)(2,1)S(1)}, u32[]{:S(2)}, u32[]{:S(2)}) %collective-permute-start.13) | collective-permute-done | bytes 524320 | tf_op jit(solution)/shard_map/ppermute | solution.py:25
  40.7 0.4 back.1
  41.1 2.5 %collective-permute-start.17 = (bf16[48,2048]{1,0:T(8,128)(2,1)S(1)}, bf16[48,2048]{1,0:T(8,128)(2,1)S(1)}, u32[]{:S(2)}, u32[]{:S(2)}) collective-permute-start(bf16[48,2048]{1,0:T(8,128)(2,1)S(1)} %get-tuple-element.55), channel_id=1, source_target_pairs={{0,24},{4,28},{8,16},{12,20},{16,8},{20,12},{24,0},{28,4},{1,25},{... | collective-permute-start | bytes 589832 | tf_op jit(solution)/shard_map/ppermute | solution.py:25
  43.6 0.5 collective-permute-start.18
  44.1 0.5 collective-permute-start.19
  44.7 2.5 %collective-permute-start.16 = (bf16[16,2048]{1,0:T(8,128)(2,1)S(1)}, bf16[16,2048]{1,0:T(8,128)(2,1)S(1)}, u32[]{:S(2)}, u32[]{:S(2)}) collective-permute-start(bf16[16,2048]{1,0:T(8,128)(2,1)S(1)} %get-tuple-element.54), channel_id=1, source_target_pairs={{0,24},{4,28},{8,16},{12,20},{16,8},{20,12},{24,0},{28,4},{1,25},{... | collective-permute-start | bytes 196616 | tf_op jit(solution)/shard_map/ppermute | solution.py:25
  47.1 0.5 collective-permute-start.15
  47.6 2.2 %collective-permute-done.17.refs_0_ = bf16[48,2048]{1,0:T(8,128)(2,1)S(1)} collective-permute-done((bf16[48,2048]{1,0:T(8,128)(2,1)S(1)}, bf16[48,2048]{1,0:T(8,128)(2,1)S(1)}, u32[]{:S(2)}, u32[]{:S(2)}) %collective-permute-start.17) | collective-permute-done | bytes 196640 | tf_op jit(solution)/shard_map/ppermute | solution.py:25
  49.9 1.5 %collective-permute-start.14 = (bf16[16,2048]{1,0:T(8,128)(2,1)S(1)}, bf16[16,2048]{1,0:T(8,128)(2,1)S(1)}, u32[]{:S(2)}, u32[]{:S(2)}) collective-permute-start(bf16[16,2048]{1,0:T(8,128)(2,1)S(1)} %get-tuple-element.52), channel_id=1, source_target_pairs={{0,8},{4,12},{8,0},{12,4},{16,24},{20,28},{24,16},{28,20},{1,9},{5... | collective-permute-start | bytes 196616 | tf_op jit(solution)/shard_map/ppermute | solution.py:25
  51.4 2.7 %collective-permute-done.18.refs_1_ = bf16[48,2048]{1,0:T(8,128)(2,1)S(1)} collective-permute-done((bf16[48,2048]{1,0:T(8,128)(2,1)S(1)}, bf16[48,2048]{1,0:T(8,128)(2,1)S(1)}, u32[]{:S(2)}, u32[]{:S(2)}) %collective-permute-start.18) | collective-permute-done | bytes 196640 | tf_op jit(solution)/shard_map/ppermute | solution.py:25
  54.0 0.1 collective-permute-done.19.refs_2_
  54.1 0.1 plane.1
  54.2 2.2 %collective-permute-start.22 = (bf16[16,2048]{1,0:T(8,128)(2,1)S(1)}, bf16[16,2048]{1,0:T(8,128)(2,1)S(1)}, u32[]{:S(2)}, u32[]{:S(2)}) collective-permute-start(bf16[16,2048]{1,0:T(8,128)(2,1)S(1)} %get-tuple-element.60), channel_id=1, source_target_pairs={{0,3},{1,2},{2,1},{3,0},{4,7},{5,6},{6,5},{7,4},{8,11},{9,10},{10,... | collective-permute-start | bytes 196616 | tf_op jit(solution)/shard_map/ppermute | solution.py:25
  56.5 0.0 collective-permute-start.21
  56.5 0.0 collective-permute-done.16
  56.5 2.2 %collective-permute-start.20 = (bf16[16,2048]{1,0:T(8,128)(2,1)S(1)}, bf16[16,2048]{1,0:T(8,128)(2,1)S(1)}, u32[]{:S(2)}, u32[]{:S(2)}) collective-permute-start(bf16[16,2048]{1,0:T(8,128)(2,1)S(1)} %get-tuple-element.58), channel_id=1, source_target_pairs={{0,1},{1,0},{2,3},{3,2},{4,5},{5,4},{6,7},{7,6},{8,9},{9,8},{10,11... | collective-permute-start | bytes 196616 | tf_op jit(solution)/shard_map/ppermute | solution.py:25
  58.7 0.0 collective-permute-done.15
  58.7 0.0 collective-permute-done.14
  58.7 2.0 %collective-permute-done.22 = bf16[16,2048]{1,0:T(8,128)(2,1)S(1)} collective-permute-done((bf16[16,2048]{1,0:T(8,128)(2,1)S(1)}, bf16[16,2048]{1,0:T(8,128)(2,1)S(1)}, u32[]{:S(2)}, u32[]{:S(2)}) %collective-permute-start.22) | collective-permute-done | bytes 65568 | tf_op jit(solution)/shard_map/ppermute | solution.py:25
  60.7 2.0 %collective-permute-done.21 = bf16[16,2048]{1,0:T(8,128)(2,1)S(1)} collective-permute-done((bf16[16,2048]{1,0:T(8,128)(2,1)S(1)}, bf16[16,2048]{1,0:T(8,128)(2,1)S(1)}, u32[]{:S(2)}, u32[]{:S(2)}) %collective-permute-start.21) | collective-permute-done | bytes 65568 | tf_op jit(solution)/shard_map/ppermute | solution.py:25
  62.7 0.0 collective-permute-done.20
  62.7 0.7 %convert_add_fusion = f32[16,2048]{1,0:T(8,128)} fusion(bf16[16,2048]{1,0:T(8,128)(2,1)S(1)} %collective-permute-done.22, bf16[16,2048]{1,0:T(8,128)(2,1)S(1)} %collective-permute-done.21, bf16[16,2048]{1,0:T(8,128)(2,1)S(1)} %collective-permute-done.20, bf16[16,2048]{1,0:T(8,128)(2,1)S(1)} %collective-permute-done.16, ...), kind=kLoop, calls=%fused_computation | loop fusion | flops 393216 | bytes 655360 | tf_op jit(solution)/shard_map/add | solution.py:232
  (10 shorter events, 0.1 us)
Async XLA Ops:
  0.0 28.0 %copy-start = (bf16[1,128,512]{2,1,0:T(8,128)(2,1)S(1)}, bf16[1,128,512]{2,1,0:T(8,128)(2,1)}, u32[]{:S(2)}) copy-start(bf16[1,128,512]{2,1,0:T(8,128)(2,1)} %param.7) | copy-start | bytes 393220
  0.0 8.7 %collective-permute-start = (bf16[16,2048]{1,0:T(8,128)(2,1)}, bf16[16,2048]{1,0:T(8,128)(2,1)S(1)}, u32[]{:S(2)}, u32[]{:S(2)}) collective-permute-start(bf16[16,2048]{1,0:T(8,128)(2,1)} %param.6), channel_id=1, source_target_pairs={{0,1},{1,0},{2,3},{3,2},{4,5},{5,4},{6,7},{7,6},{8,9},{9,8},{10,11... | collective-permute-start | bytes 196616 | tf_op jit(solution)/shard_map/ppermute | solution.py:25
  3.0 7.5 %collective-permute-start.1 = (bf16[16,2048]{1,0:T(8,128)(2,1)}, bf16[16,2048]{1,0:T(8,128)(2,1)S(1)}, u32[]{:S(2)}, u32[]{:S(2)}) collective-permute-start(bf16[16,2048]{1,0:T(8,128)(2,1)} %param.6), channel_id=1, source_target_pairs={{0,2},{1,3},{2,0},{3,1},{4,6},{5,7},{6,4},{7,5},{8,10},{9,11},{10,... | collective-permute-start | bytes 196616 | tf_op jit(solution)/shard_map/ppermute | solution.py:25
  5.6 6.3 %collective-permute-start.2 = (bf16[16,2048]{1,0:T(8,128)(2,1)}, bf16[16,2048]{1,0:T(8,128)(2,1)S(1)}, u32[]{:S(2)}, u32[]{:S(2)}) collective-permute-start(bf16[16,2048]{1,0:T(8,128)(2,1)} %param.6), channel_id=1, source_target_pairs={{0,3},{1,2},{2,1},{3,0},{4,7},{5,6},{6,5},{7,4},{8,11},{9,10},{10,... | collective-permute-start | bytes 196616 | tf_op jit(solution)/shard_map/ppermute | solution.py:25
  5.6 6.3 %collective-permute-start.3 = (bf16[128,512]{1,0:T(8,128)(2,1)}, bf16[128,512]{1,0:T(8,128)(2,1)S(1)}, u32[]{:S(2)}, u32[]{:S(2)}) collective-permute-start(bf16[128,512]{1,0:T(8,128)(2,1)} %bitcast.15), channel_id=1, source_target_pairs={{0,4},{4,0},{8,12},{12,8},{16,20},{20,16},{24,28},{28,24},{1,5},{5... | collective-permute-start | bytes 393224 | tf_op jit(solution)/shard_map/ppermute | solution.py:25
  11.9 8.3 %copy-start.2 = (bf16[128,512]{1,0:T(8,128)(2,1)}, bf16[128,512]{1,0:T(8,128)(2,1)S(1)}, u32[]{:S(2)}) copy-start(bf16[128,512]{1,0:T(8,128)(2,1)S(1)} %collective-permute-done.3.oper_other) | copy-start | bytes 393220
  12.0 13.4 %collective-permute-start.7 = (bf16[64,2048]{1,0:T(8,128)(2,1)S(1)}, bf16[64,2048]{1,0:T(8,128)(2,1)S(1)}, u32[]{:S(2)}, u32[]{:S(2)}) collective-permute-start(bf16[64,2048]{1,0:T(8,128)(2,1)S(1)} %constant_dynamic-update-slice_fusion.refs_0_), channel_id=1, source_target_pairs={{0,8},{4,12},{8,0},{12,4},{16,24},{20,28},{24,16},{28,20},{1,9},{5... | collective-permute-start | bytes 786440 | tf_op jit(solution)/shard_map/ppermute | solution.py:25
  13.5 12.4 %collective-permute-start.9 = (bf16[64,2048]{1,0:T(8,128)(2,1)S(1)}, bf16[64,2048]{1,0:T(8,128)(2,1)S(1)}, u32[]{:S(2)}, u32[]{:S(2)}) collective-permute-start(bf16[64,2048]{1,0:T(8,128)(2,1)S(1)} %constant_dynamic-update-slice_fusion.refs_0_), channel_id=1, source_target_pairs={{0,16},{4,20},{8,24},{12,28},{16,0},{20,4},{24,8},{28,12},{1,17},{... | collective-permute-start | bytes 786440 | tf_op jit(solution)/shard_map/ppermute | solution.py:25
  15.0 10.9 %collective-permute-start.11 = (bf16[64,2048]{1,0:T(8,128)(2,1)S(1)}, bf16[64,2048]{1,0:T(8,128)(2,1)S(1)}, u32[]{:S(2)}, u32[]{:S(2)}) collective-permute-start(bf16[64,2048]{1,0:T(8,128)(2,1)S(1)} %constant_dynamic-update-slice_fusion.refs_0_), channel_id=1, source_target_pairs={{0,24},{4,28},{8,16},{12,20},{16,8},{20,12},{24,0},{28,4},{1,25},{... | collective-permute-start | bytes 786440 | tf_op jit(solution)/shard_map/ppermute | solution.py:25
  15.5 9.8 %collective-permute-start.5 = (f32[8,2560]{1,0:T(8,128)S(1)}, f32[8,2560]{1,0:T(8,128)S(1)}, u32[]{:S(2)}, u32[]{:S(2)}) collective-permute-start(f32[8,2560]{1,0:T(8,128)S(1)} %get-tuple-element.66), channel_id=1, source_target_pairs={{1,2},{2,1},{5,6},{6,5},{9,10},{10,9},{13,14},{14,13},{17,18},{18,... | collective-permute-start | bytes 245768 | tf_op jit(solution)/shard_map/ppermute | solution.py:185
  16.2 9.2 %collective-permute-start.6 = (f32[8,2560]{1,0:T(8,128)S(1)}, f32[8,2560]{1,0:T(8,128)S(1)}, u32[]{:S(2)}, u32[]{:S(2)}) collective-permute-start(f32[8,2560]{1,0:T(8,128)S(1)} %get-tuple-element.65), channel_id=1, source_target_pairs={{0,1},{1,0},{2,3},{3,2},{4,5},{5,4},{6,7},{7,6},{8,9},{9,8},{10,11... | collective-permute-start | bytes 245768 | tf_op jit(solution)/shard_map/ppermute | solution.py:186
  20.2 7.8 %copy-start.1 = (s32[2]{0:T(128)S(1)}, s32[2]{0:T(128)}, u32[]{:S(2)}) copy-start(s32[2]{0:T(128)} %pad_add_fusion.where) | copy-start | bytes 28
  25.3 1.6 %collective-permute-start.4 = (bf16[64,2048]{1,0:T(8,128)(2,1)S(1)}, bf16[64,2048]{1,0:T(8,128)(2,1)S(1)}, u32[]{:S(2)}, u32[]{:S(2)}) collective-permute-start(bf16[64,2048]{1,0:T(8,128)(2,1)S(1)} %constant_dynamic-update-slice_fusion.refs_0_), channel_id=1, source_target_pairs={{0,4},{4,0},{8,12},{12,8},{16,20},{20,16},{24,28},{28,24},{1,5},{5... | collective-permute-start | bytes 786440 | tf_op jit(solution)/shard_map/ppermute | solution.py:25
  25.4 1.9 %collective-permute-start.8 = (bf16[64,2048]{1,0:T(8,128)(2,1)S(1)}, bf16[64,2048]{1,0:T(8,128)(2,1)S(1)}, u32[]{:S(2)}, u32[]{:S(2)}) collective-permute-start(bf16[64,2048]{1,0:T(8,128)(2,1)S(1)} %collective-permute-done.7.refs_2_), channel_id=1, source_target_pairs={{0,4},{4,0},{8,12},{12,8},{16,20},{20,16},{24,28},{28,24},{1,5},{5... | collective-permute-start | bytes 786440 | tf_op jit(solution)/shard_map/ppermute | solution.py:25
  25.9 1.8 %collective-permute-start.10 = (bf16[64,2048]{1,0:T(8,128)(2,1)S(1)}, bf16[64,2048]{1,0:T(8,128)(2,1)S(1)}, u32[]{:S(2)}, u32[]{:S(2)}) collective-permute-start(bf16[64,2048]{1,0:T(8,128)(2,1)S(1)} %collective-permute-done.9.refs_4_), channel_id=1, source_target_pairs={{0,4},{4,0},{8,12},{12,8},{16,20},{20,16},{24,28},{28,24},{1,5},{5... | collective-permute-start | bytes 786440 | tf_op jit(solution)/shard_map/ppermute | solution.py:25
  26.0 2.0 %collective-permute-start.12 = (bf16[64,2048]{1,0:T(8,128)(2,1)S(1)}, bf16[64,2048]{1,0:T(8,128)(2,1)S(1)}, u32[]{:S(2)}, u32[]{:S(2)}) collective-permute-start(bf16[64,2048]{1,0:T(8,128)(2,1)S(1)} %collective-permute-done.11.refs_6_), channel_id=1, source_target_pairs={{0,4},{4,0},{8,12},{12,8},{16,20},{20,16},{24,28},{28,24},{1,5},{5... | collective-permute-start | bytes 786440 | tf_op jit(solution)/shard_map/ppermute | solution.py:25
  38.7 2.0 %collective-permute-start.13 = (bf16[128,2048]{1,0:T(8,128)(2,1)S(1)}, bf16[128,2048]{1,0:T(8,128)(2,1)S(1)}, u32[]{:S(2)}, u32[]{:S(2)}) collective-permute-start(bf16[128,2048]{1,0:T(8,128)(2,1)S(1)} %solve.1.part), channel_id=1, source_target_pairs={{0,4},{4,0},{8,12},{12,8},{16,20},{20,16},{24,28},{28,24},{1,5},{5... | collective-permute-start | bytes 1572872 | tf_op jit(solution)/shard_map/ppermute | solution.py:25
  41.1 8.8 %collective-permute-start.17 = (bf16[48,2048]{1,0:T(8,128)(2,1)S(1)}, bf16[48,2048]{1,0:T(8,128)(2,1)S(1)}, u32[]{:S(2)}, u32[]{:S(2)}) collective-permute-start(bf16[48,2048]{1,0:T(8,128)(2,1)S(1)} %get-tuple-element.55), channel_id=1, source_target_pairs={{0,24},{4,28},{8,16},{12,20},{16,8},{20,12},{24,0},{28,4},{1,25},{... | collective-permute-start | bytes 589832 | tf_op jit(solution)/shard_map/ppermute | solution.py:25
  43.6 10.4 %collective-permute-start.18 = (bf16[48,2048]{1,0:T(8,128)(2,1)S(1)}, bf16[48,2048]{1,0:T(8,128)(2,1)S(1)}, u32[]{:S(2)}, u32[]{:S(2)}) collective-permute-start(bf16[48,2048]{1,0:T(8,128)(2,1)S(1)} %get-tuple-element.56), channel_id=1, source_target_pairs={{0,16},{4,20},{8,24},{12,28},{16,0},{20,4},{24,8},{28,12},{1,17},{... | collective-permute-start | bytes 589832 | tf_op jit(solution)/shard_map/ppermute | solution.py:25
  44.1 10.0 %collective-permute-start.19 = (bf16[48,2048]{1,0:T(8,128)(2,1)S(1)}, bf16[48,2048]{1,0:T(8,128)(2,1)S(1)}, u32[]{:S(2)}, u32[]{:S(2)}) collective-permute-start(bf16[48,2048]{1,0:T(8,128)(2,1)S(1)} %get-tuple-element.57), channel_id=1, source_target_pairs={{0,8},{4,12},{8,0},{12,4},{16,24},{20,28},{24,16},{28,20},{1,9},{5... | collective-permute-start | bytes 589832 | tf_op jit(solution)/shard_map/ppermute | solution.py:25
  44.7 11.8 %collective-permute-start.16 = (bf16[16,2048]{1,0:T(8,128)(2,1)S(1)}, bf16[16,2048]{1,0:T(8,128)(2,1)S(1)}, u32[]{:S(2)}, u32[]{:S(2)}) collective-permute-start(bf16[16,2048]{1,0:T(8,128)(2,1)S(1)} %get-tuple-element.54), channel_id=1, source_target_pairs={{0,24},{4,28},{8,16},{12,20},{16,8},{20,12},{24,0},{28,4},{1,25},{... | collective-permute-start | bytes 196616 | tf_op jit(solution)/shard_map/ppermute | solution.py:25
  47.1 11.6 %collective-permute-start.15 = (bf16[16,2048]{1,0:T(8,128)(2,1)S(1)}, bf16[16,2048]{1,0:T(8,128)(2,1)S(1)}, u32[]{:S(2)}, u32[]{:S(2)}) collective-permute-start(bf16[16,2048]{1,0:T(8,128)(2,1)S(1)} %get-tuple-element.53), channel_id=1, source_target_pairs={{0,16},{4,20},{8,24},{12,28},{16,0},{20,4},{24,8},{28,12},{1,17},{... | collective-permute-start | bytes 196616 | tf_op jit(solution)/shard_map/ppermute | solution.py:25
  49.9 8.8 %collective-permute-start.14 = (bf16[16,2048]{1,0:T(8,128)(2,1)S(1)}, bf16[16,2048]{1,0:T(8,128)(2,1)S(1)}, u32[]{:S(2)}, u32[]{:S(2)}) collective-permute-start(bf16[16,2048]{1,0:T(8,128)(2,1)S(1)} %get-tuple-element.52), channel_id=1, source_target_pairs={{0,8},{4,12},{8,0},{12,4},{16,24},{20,28},{24,16},{28,20},{1,9},{5... | collective-permute-start | bytes 196616 | tf_op jit(solution)/shard_map/ppermute | solution.py:25
  54.2 6.5 %collective-permute-start.22 = (bf16[16,2048]{1,0:T(8,128)(2,1)S(1)}, bf16[16,2048]{1,0:T(8,128)(2,1)S(1)}, u32[]{:S(2)}, u32[]{:S(2)}) collective-permute-start(bf16[16,2048]{1,0:T(8,128)(2,1)S(1)} %get-tuple-element.60), channel_id=1, source_target_pairs={{0,3},{1,2},{2,1},{3,0},{4,7},{5,6},{6,5},{7,4},{8,11},{9,10},{10,... | collective-permute-start | bytes 196616 | tf_op jit(solution)/shard_map/ppermute | solution.py:25
  56.5 6.2 %collective-permute-start.21 = (bf16[16,2048]{1,0:T(8,128)(2,1)S(1)}, bf16[16,2048]{1,0:T(8,128)(2,1)S(1)}, u32[]{:S(2)}, u32[]{:S(2)}) collective-permute-start(bf16[16,2048]{1,0:T(8,128)(2,1)S(1)} %get-tuple-element.59), channel_id=1, source_target_pairs={{0,2},{1,3},{2,0},{3,1},{4,6},{5,7},{6,4},{7,5},{8,10},{9,11},{10,... | collective-permute-start | bytes 196616 | tf_op jit(solution)/shard_map/ppermute | solution.py:25
  56.5 6.2 %collective-permute-start.20 = (bf16[16,2048]{1,0:T(8,128)(2,1)S(1)}, bf16[16,2048]{1,0:T(8,128)(2,1)S(1)}, u32[]{:S(2)}, u32[]{:S(2)}) collective-permute-start(bf16[16,2048]{1,0:T(8,128)(2,1)S(1)} %get-tuple-element.58), channel_id=1, source_target_pairs={{0,1},{1,0},{2,3},{3,2},{4,5},{5,4},{6,7},{7,6},{8,9},{9,8},{10,11... | collective-permute-start | bytes 196616 | tf_op jit(solution)/shard_map/ppermute | solution.py:25

commit v4 on v3

--- a/solution.py
+++ b/solution.py
@@ -9,6 +9,7 @@
 
 SWEEPS = 8
 HALO = 8
+CUT = 2
 Z_ORDER = (1, 2, 3)
 XY_ORDER = (3, 2, 1)
 XYB_ORDER = (3, 2, 1)
@@ -135,20 +136,20 @@
         keep[:, cols] = total[:half]
         for m in range(1, n_chips):
             rows = total[m * half : (m + 1) * half].astype(jnp.bfloat16)
-            near[m - 1][:, cols] = rows[:tile]
-            far[m - 1][:, cols] = rows[tile:]
-
-
-def plane_kernel(n_chips, tile, keep, *refs):
-    gets, sends = refs[: n_chips - 1], refs[n_chips - 1 :]
+            near[m - 1][:, cols] = rows[: CUT * tile]
+            far[m - 1][:, cols] = rows[CUT * tile :]
+
+
+def plane_kernel(n_chips, tile, begin, n_keep, keep, *refs):
+    gets, outs = refs[: n_chips - 1], refs[n_chips - 1 :]
+    rows = gets[0].shape[0]
     for n in range(0, keep.shape[1], TILE):
         cols = slice(n, n + TILE)
-        total = keep[tile:, cols]
+        total = keep[begin : begin + rows, cols]
         for got in gets:
             total += got[:, cols].astype(jnp.float32)
-        total = total.astype(jnp.bfloat16)
-        for j, send in enumerate(sends):
-            send[:, cols] = total[j * tile : (j + 1) * tile]
+        for j, out in enumerate(outs):
+            out[:, cols] = total[j * tile : (j + 1) * tile].astype(out.dtype)
 
 
 def turns(size, order):
@@ -214,23 +215,29 @@
     )
     tile = n_fine // (n_freq * n_slab)
     keep, sends, level = back(turned, part, tile)
-    gets = [xor_permute(sends[m - 1], "freq", 2 * m) for m in turns(n_chips, XYB_ORDER)]
-
-    sends = pl.pallas_call(
-        functools.partial(plane_kernel, n_chips, tile),
-        out_shape=[jax.ShapeDtypeStruct((tile, width), bf16)] * (n_slab - 1),
-        in_specs=[VMEM] * n_chips,
-        out_specs=[VMEM] * (n_slab - 1),
+    far = [xor_permute(sends[m - 1], "freq", 2 * m) for m in turns(n_chips, XYB_ORDER)]
+    far = plane_sum(keep, far, tile, CUT, 0)
+    near = [xor_permute(level[m - 1], "freq", 2 * m) for m in turns(n_chips, XYB2_ORDER)]
+    own, *near = plane_sum(keep, near, tile, 0, 1)
+    sends = [None, *near, *far]
+    for m in turns(n_slab, ZB_ORDER):
+        own = own + xor_permute(sends[m], "slab", m).astype(f32)
+    return own
+
+
+def plane_sum(keep, gets, tile, begin, n_keep):
+    width, count = keep.shape[1], gets[0].shape[0] // tile
+    out_shape = [jax.ShapeDtypeStruct((tile, width), jnp.float32)] * n_keep
+    out_shape += [jax.ShapeDtypeStruct((tile, width), jnp.bfloat16)] * (count - n_keep)
+    return pl.pallas_call(
+        functools.partial(plane_kernel, len(gets) + 1, tile, begin * tile, n_keep),
+        out_shape=out_shape,
+        in_specs=[VMEM] * (len(gets) + 1),
+        out_specs=[VMEM] * count,
         compiler_params=pltpu.CompilerParams(vmem_limit_bytes=6 * MIB),
-        cost_estimate=cost(0, 4 * n_slab * tile * width * (n_chips + 1)),
+        cost_estimate=cost(0, 4 * count * tile * width * (len(gets) + 2)),
         name="plane",
     )(keep, *gets)
-    own = keep[:tile]
-    for m in turns(n_chips, XYB2_ORDER):
-        own = own + xor_permute(level[m - 1], "freq", 2 * m).astype(f32)
-    for m in turns(n_slab, ZB_ORDER):
-        own = own + xor_permute(sends[m - 1], "slab", m).astype(f32)
-    return own
 
 
 def back(turned, part, tile):
@@ -240,8 +247,8 @@
     keep, *sends = pl.pallas_call(
         functools.partial(back_kernel, n_chips, tile),
         out_shape=[jax.ShapeDtypeStruct((rows, width), jnp.float32)]
-        + [jax.ShapeDtypeStruct((rows - tile, width), jnp.bfloat16)] * others
-        + [jax.ShapeDtypeStruct((tile, width), jnp.bfloat16)] * others,
+        + [jax.ShapeDtypeStruct((rows - CUT * tile, width), jnp.bfloat16)] * others
+        + [jax.ShapeDtypeStruct((CUT * tile, width), jnp.bfloat16)] * others,
         in_specs=[VMEM] * 3,
         out_specs=[VMEM] * (2 * n_chips - 1),
         compiler_params=pltpu.CompilerParams(vmem_limit_bytes=6 * MIB),

time: 63.7 us -> 61.5 us (0.965)
  waiting for transfers between devices: 15.5 us -> 13.9 us
    ppermute x21, waiting for transfers between devices: 15.5 us -> 13.9 us  [xor_permute(): return lax.ppermute(value, axis, [(i, i ^ mask) for i in range(size)])]
  transfers between devices with their start and end apart: 23 -> 23, of which waited for: 12 -> 15; matrix products, arithmetic and copies ran while one was open for 5% -> 5% of each run, Pallas kernels for 8% -> 8%
where the time goes in v4:
time: 61.5 us; the launch traced here: 61.2 us
  starting transfers between devices  26.4 us (43%)
  Pallas kernels  16.3 us (27%)
  waiting for transfers between devices  13.9 us (23%)
  other arithmetic  2.09 us (3%)
  local copies, waits for them, and re-layouts  1.78 us (3%)
  between operations  0.82 us (1%)
    ppermute x21, starting transfers between devices, xor_permute(): return lax.ppermute(value, axis, [(i, i ^ mask) for i in range(size)])  22.3 us
    ppermute x21, waiting for transfers between devices, xor_permute(): return lax.ppermute(value, axis, [(i, i ^ mask) for i in range(size)])  13.9 us
    pallas_call x1, Pallas kernels, shards(): pl.pallas_call(functools.partial(solve_kernel, len(blocks), n_slab), out_...  10.7 us
    pallas_call x1, Pallas kernels, stage(): pl.pallas_call(functools.partial(stage_kernel, order, n_freq, n_slab, til...  5.06 us
    ppermute x1, starting transfers between devices, shards(): lax.ppermute(jnp.where(odd, edges, edges_last), 'slab', [(i, i ^ 1) for i...  3.43 us
  transfers between devices with their start and end apart: 23, of which 15 were waited for; matrix products, arithmetic and copies ran while one was open for 5% of the time, Pallas kernels for 8%

profile of v4, /device:TPU:0, one launch (start us, length us, event | category | flops | bytes accessed | tf_op | source)
XLA Modules:
  0.0 61.2 jit_solution(11348134791199403932)
XLA Ops:
  0.0 0.0 copy-start
  0.0 3.0 %collective-permute-start = (bf16[16,2048]{1,0:T(8,128)(2,1)}, bf16[16,2048]{1,0:T(8,128)(2,1)S(1)}, u32[]{:S(2)}, u32[]{:S(2)}) collective-permute-start(bf16[16,2048]{1,0:T(8,128)(2,1)} %param.6), channel_id=1, source_target_pairs={{0,1},{1,0},{2,3},{3,2},{4,5},{5,4},{6,7},{7,6},{8,9},{9,8},{10,11... | collective-permute-start | bytes 196616 | tf_op jit(solution)/shard_map/ppermute | solution.py:26
  3.0 2.6 %collective-permute-start.1 = (bf16[16,2048]{1,0:T(8,128)(2,1)}, bf16[16,2048]{1,0:T(8,128)(2,1)S(1)}, u32[]{:S(2)}, u32[]{:S(2)}) collective-permute-start(bf16[16,2048]{1,0:T(8,128)(2,1)} %param.6), channel_id=1, source_target_pairs={{0,2},{1,3},{2,0},{3,1},{4,6},{5,7},{6,4},{7,5},{8,10},{9,11},{10,... | collective-permute-start | bytes 196616 | tf_op jit(solution)/shard_map/ppermute | solution.py:26
  5.6 0.0 collective-permute-start.2
  5.6 0.0 collective-permute-start.3
  5.6 0.7 %bitcast_convert_fusion = (f32[8,512]{1,0:T(8,128)S(1)}, f32[8,512]{1,0:T(8,128)S(1)}) fusion(bf16[1,128,512]{2,1,0:T(8,128)(2,1)} %param.7), kind=kLoop, calls=%fused_computation.13 | loop fusion | flops 8192 | bytes 49152 | tf_op jit(solution)/shard_map/convert_element_type | solution.py:176
  6.3 0.9 %slice_bitcast_fusion = (f32[8,2048]{1,0:T(8,128)S(1)}, f32[8,2048]{1,0:T(8,128)S(1)}) fusion(f32[1,128,2048]{2,1,0:T(8,128)} %param.10), kind=kLoop, calls=%fused_computation.3 | loop fusion | bytes 262144 | tf_op jit(solution)/shard_map/slice | solution.py:176
  7.2 0.8 %constant_dynamic-update-slice_fusion.3 = bf16[64,2048]{1,0:T(8,128)(2,1)S(1)} fusion(bf16[16,2048]{1,0:T(8,128)(2,1)} %param.6), kind=kLoop, calls=%fused_computation.12 | loop fusion | bytes 131072
  8.7 0.0 collective-permute-done
  8.8 1.8 %collective-permute-done.1 = bf16[16,2048]{1,0:T(8,128)(2,1)S(1)} collective-permute-done((bf16[16,2048]{1,0:T(8,128)(2,1)}, bf16[16,2048]{1,0:T(8,128)(2,1)S(1)}, u32[]{:S(2)}, u32[]{:S(2)}) %collective-permute-start.1) | collective-permute-done | bytes 65568 | tf_op jit(solution)/shard_map/ppermute | solution.py:26
  10.5 1.4 %collective-permute-done.2 = bf16[16,2048]{1,0:T(8,128)(2,1)S(1)} collective-permute-done((bf16[16,2048]{1,0:T(8,128)(2,1)}, bf16[16,2048]{1,0:T(8,128)(2,1)S(1)}, u32[]{:S(2)}, u32[]{:S(2)}) %collective-permute-start.2) | collective-permute-done | bytes 65568 | tf_op jit(solution)/shard_map/ppermute | solution.py:26
  11.9 0.0 collective-permute-done.3.oper_other
  11.9 0.0 copy-start.2
  12.0 1.6 %collective-permute-start.7 = (bf16[64,2048]{1,0:T(8,128)(2,1)S(1)}, bf16[64,2048]{1,0:T(8,128)(2,1)S(1)}, u32[]{:S(2)}, u32[]{:S(2)}) collective-permute-start(bf16[64,2048]{1,0:T(8,128)(2,1)S(1)} %constant_dynamic-update-slice_fusion.refs_0_), channel_id=1, source_target_pairs={{0,8},{4,12},{8,0},{12,4},{16,24},{20,28},{24,16},{28,20},{1,9},{5... | collective-permute-start | bytes 786440 | tf_op jit(solution)/shard_map/ppermute | solution.py:26
  13.5 1.5 %collective-permute-start.9 = (bf16[64,2048]{1,0:T(8,128)(2,1)S(1)}, bf16[64,2048]{1,0:T(8,128)(2,1)S(1)}, u32[]{:S(2)}, u32[]{:S(2)}) collective-permute-start(bf16[64,2048]{1,0:T(8,128)(2,1)S(1)} %constant_dynamic-update-slice_fusion.refs_0_), channel_id=1, source_target_pairs={{0,16},{4,20},{8,24},{12,28},{16,0},{20,4},{24,8},{28,12},{1,17},{... | collective-permute-start | bytes 786440 | tf_op jit(solution)/shard_map/ppermute | solution.py:26
  15.0 0.5 collective-permute-start.11
  15.5 0.7 %collective-permute-start.5 = (f32[8,2560]{1,0:T(8,128)S(1)}, f32[8,2560]{1,0:T(8,128)S(1)}, u32[]{:S(2)}, u32[]{:S(2)}) collective-permute-start(f32[8,2560]{1,0:T(8,128)S(1)} %get-tuple-element.68), channel_id=1, source_target_pairs={{1,2},{2,1},{5,6},{6,5},{9,10},{10,9},{13,14},{14,13},{17,18},{18,... | collective-permute-start | bytes 245768 | tf_op jit(solution)/shard_map/ppermute | solution.py:186
  16.2 3.4 %collective-permute-start.6 = (f32[8,2560]{1,0:T(8,128)S(1)}, f32[8,2560]{1,0:T(8,128)S(1)}, u32[]{:S(2)}, u32[]{:S(2)}) collective-permute-start(f32[8,2560]{1,0:T(8,128)S(1)} %get-tuple-element.67), channel_id=1, source_target_pairs={{0,1},{1,0},{2,3},{3,2},{4,5},{5,4},{6,7},{7,6},{8,9},{9,8},{10,11... | collective-permute-start | bytes 245768 | tf_op jit(solution)/shard_map/ppermute | solution.py:187
  19.6 0.6 %pad_add_fusion.where = s32[2]{0:T(128)} fusion(s32[1]{0:T(128)} %bitcast.1, s32[1]{0:T(128)} %bitcast), kind=kLoop, calls=%fused_computation.15 | loop fusion | flops 2 | bytes 16 | tf_op jit(solution)/shard_map/stack | solution.py:170
  20.3 0.0 copy-done.2
  20.3 0.0 copy-start.1
  20.3 5.1 %stage.1 = (bf16[2048,2048]{1,0:T(8,128)(2,1)S(1)}, f32[128,2048]{1,0:T(8,128)S(1)}, f32[128,2048]{1,0:T(8,128)S(1)}, bf16[512,512]{1,0:T(8,128)(2,1)S(1)}, bf16[256,256]{1,0:T(8,128)(2,1)S(1)}) custom-call(s32[2]{0:T(128)} %pad_add_fusion.where, bf16[128,512]{1,0:T(8,128)(2,1)} %bitcast.16, bf16[128,512]{1,0:T(8,128)(2,1)} %copy-done.2, ...), custom_call_target="tpu_custom_call" | custom-call | bytes 22282240 | tf_op jit(solution)/shard_map/stage/pallas_call | solution.py:114
  25.4 0.0 collective-permute-done.5
  25.4 0.1 collective-permute-start.4
  25.5 0.0 collective-permute-done.6
  25.5 0.0 collective-permute-done.7.refs_2_
  25.5 0.5 collective-permute-start.8
  26.0 0.0 collective-permute-done.9.refs_4_
  26.0 0.1 collective-permute-start.10
  26.1 0.0 collective-permute-done.11.refs_6_
  26.1 0.4 collective-permute-start.12
  26.5 0.4 collective-permute-done.4.refs_1_
  27.0 0.4 collective-permute-done.8.refs_3_
  27.4 0.4 collective-permute-done.10.refs_5_
  27.7 0.4 collective-permute-done.12.refs_7_
  28.1 0.0 copy-done
  28.1 0.0 copy-done.1
  28.1 10.7 %solve.1.part = bf16[128,2048]{1,0:T(8,128)(2,1)S(1)} custom-call(s32[2]{0:T(128)S(1)} %copy-done.1, f32[1]{0:T(128)S(6)} %copy.10.factor, bf16[64,2048]{1,0:T(8,128)(2,1)S(1)} %constant_dynamic-update-slice_fusion.refs_0_, bf16[64,2048]{1,0:T(8,128)(2,1)S(1)} %collective-permute-done.4.refs_1_, bf16[64,2048]{1,0:T(8,128)(2,1)S(1)} %collective-permute-done.7.refs_2_, ...), custom_call_target="tpu_custom_call" | custom-call | flops 8455716864 | bytes 8388608 | tf_op jit(solution)/shard_map/solve/pallas_call | solution.py:199
  38.8 0.2 collective-permute-start.13
  39.0 1.8 %collective-permute-done.13.part_other = bf16[128,2048]{1,0:T(8,128)(2,1)S(1)} collective-permute-done((bf16[128,2048]{1,0:T(8,128)(2,1)S(1)}, bf16[128,2048]{1,0:T(8,128)(2,1)S(1)}, u32[]{:S(2)}, u32[]{:S(2)}) %collective-permute-start.13) | collective-permute-done | bytes 524320 | tf_op jit(solution)/shard_map/ppermute | solution.py:26
  40.7 0.4 back.1
  41.2 2.5 %collective-permute-start.18 = (bf16[32,2048]{1,0:T(8,128)(2,1)S(1)}, bf16[32,2048]{1,0:T(8,128)(2,1)S(1)}, u32[]{:S(2)}, u32[]{:S(2)}) collective-permute-start(bf16[32,2048]{1,0:T(8,128)(2,1)S(1)} %get-tuple-element.58), channel_id=1, source_target_pairs={{0,24},{4,28},{8,16},{12,20},{16,8},{20,12},{24,0},{28,4},{1,25},{... | collective-permute-start | bytes 393224 | tf_op jit(solution)/shard_map/ppermute | solution.py:26
  43.7 0.5 collective-permute-start.19
  44.2 0.5 collective-permute-start.20
  44.7 1.5 %collective-permute-start.14 = (bf16[32,2048]{1,0:T(8,128)(2,1)S(1)}, bf16[32,2048]{1,0:T(8,128)(2,1)S(1)}, u32[]{:S(2)}, u32[]{:S(2)}) collective-permute-start(bf16[32,2048]{1,0:T(8,128)(2,1)S(1)} %get-tuple-element.53), channel_id=1, source_target_pairs={{0,8},{4,12},{8,0},{12,4},{16,24},{20,28},{24,16},{28,20},{1,9},{5... | collective-permute-start | bytes 393224 | tf_op jit(solution)/shard_map/ppermute | solution.py:26
  46.2 1.5 %collective-permute-start.15 = (bf16[32,2048]{1,0:T(8,128)(2,1)S(1)}, bf16[32,2048]{1,0:T(8,128)(2,1)S(1)}, u32[]{:S(2)}, u32[]{:S(2)}) collective-permute-start(bf16[32,2048]{1,0:T(8,128)(2,1)S(1)} %get-tuple-element.54), channel_id=1, source_target_pairs={{0,16},{4,20},{8,24},{12,28},{16,0},{20,4},{24,8},{28,12},{1,17},{... | collective-permute-start | bytes 393224 | tf_op jit(solution)/shard_map/ppermute | solution.py:26
  47.8 0.2 collective-permute-done.18.refs_0_
  48.0 3.0 %collective-permute-start.16 = (bf16[32,2048]{1,0:T(8,128)(2,1)S(1)}, bf16[32,2048]{1,0:T(8,128)(2,1)S(1)}, u32[]{:S(2)}, u32[]{:S(2)}) collective-permute-start(bf16[32,2048]{1,0:T(8,128)(2,1)S(1)} %get-tuple-element.55), channel_id=1, source_target_pairs={{0,24},{4,28},{8,16},{12,20},{16,8},{20,12},{24,0},{28,4},{1,25},{... | collective-permute-start | bytes 393224 | tf_op jit(solution)/shard_map/ppermute | solution.py:26
  51.0 0.0 collective-permute-done.19.refs_1_
  51.0 0.4 collective-permute-done.20.refs_2_
  51.4 0.1 plane.3
  51.5 2.2 %collective-permute-start.22 = (bf16[16,2048]{1,0:T(8,128)(2,1)S(1)}, bf16[16,2048]{1,0:T(8,128)(2,1)S(1)}, u32[]{:S(2)}, u32[]{:S(2)}) collective-permute-start(bf16[16,2048]{1,0:T(8,128)(2,1)S(1)} %get-tuple-element.62), channel_id=1, source_target_pairs={{0,3},{1,2},{2,1},{3,0},{4,7},{5,6},{6,5},{7,4},{8,11},{9,10},{10,... | collective-permute-start | bytes 196616 | tf_op jit(solution)/shard_map/ppermute | solution.py:26
  53.6 0.0 collective-permute-start.21
  53.6 0.6 collective-permute-done.14.refs_0_
  54.2 0.2 collective-permute-done.15.refs_1_
  54.4 1.7 %collective-permute-done.16.refs_2_ = bf16[32,2048]{1,0:T(8,128)(2,1)S(1)} collective-permute-done((bf16[32,2048]{1,0:T(8,128)(2,1)S(1)}, bf16[32,2048]{1,0:T(8,128)(2,1)S(1)}, u32[]{:S(2)}, u32[]{:S(2)}) %collective-permute-start.16) | collective-permute-done | bytes 131104 | tf_op jit(solution)/shard_map/ppermute | solution.py:26
  56.1 0.1 plane.2
  56.2 0.1 collective-permute-start.17
  56.3 1.3 %collective-permute-done.22 = bf16[16,2048]{1,0:T(8,128)(2,1)S(1)} collective-permute-done((bf16[16,2048]{1,0:T(8,128)(2,1)S(1)}, bf16[16,2048]{1,0:T(8,128)(2,1)S(1)}, u32[]{:S(2)}, u32[]{:S(2)}) %collective-permute-start.22) | collective-permute-done | bytes 65568 | tf_op jit(solution)/shard_map/ppermute | solution.py:26
  57.6 2.0 %collective-permute-done.21 = bf16[16,2048]{1,0:T(8,128)(2,1)S(1)} collective-permute-done((bf16[16,2048]{1,0:T(8,128)(2,1)S(1)}, bf16[16,2048]{1,0:T(8,128)(2,1)S(1)}, u32[]{:S(2)}, u32[]{:S(2)}) %collective-permute-start.21) | collective-permute-done | bytes 65568 | tf_op jit(solution)/shard_map/ppermute | solution.py:26
  59.6 1.0 %collective-permute-done.17 = bf16[16,2048]{1,0:T(8,128)(2,1)S(1)} collective-permute-done((bf16[16,2048]{1,0:T(8,128)(2,1)S(1)}, bf16[16,2048]{1,0:T(8,128)(2,1)S(1)}, u32[]{:S(2)}, u32[]{:S(2)}) %collective-permute-start.17) | collective-permute-done | bytes 65568 | tf_op jit(solution)/shard_map/ppermute | solution.py:26
  60.5 0.7 %convert_add_fusion = f32[16,2048]{1,0:T(8,128)} fusion(bf16[16,2048]{1,0:T(8,128)(2,1)S(1)} %collective-permute-done.22, bf16[16,2048]{1,0:T(8,128)(2,1)S(1)} %collective-permute-done.21, f32[16,2048]{1,0:T(8,128)S(1)} %get-tuple-element.56, bf16[16,2048]{1,0:T(8,128)(2,1)S(1)} %collective-permute-done.17), kind=kLoop, calls=%fused_computation | loop fusion | flops 196608 | bytes 458752 | tf_op jit(solution)/shard_map/add | solution.py:224
  (10 shorter events, 0.1 us)
Async XLA Ops:
  0.0 28.1 %copy-start = (bf16[1,128,512]{2,1,0:T(8,128)(2,1)S(1)}, bf16[1,128,512]{2,1,0:T(8,128)(2,1)}, u32[]{:S(2)}) copy-start(bf16[1,128,512]{2,1,0:T(8,128)(2,1)} %param.7) | copy-start | bytes 393220
  0.0 8.7 %collective-permute-start = (bf16[16,2048]{1,0:T(8,128)(2,1)}, bf16[16,2048]{1,0:T(8,128)(2,1)S(1)}, u32[]{:S(2)}, u32[]{:S(2)}) collective-permute-start(bf16[16,2048]{1,0:T(8,128)(2,1)} %param.6), channel_id=1, source_target_pairs={{0,1},{1,0},{2,3},{3,2},{4,5},{5,4},{6,7},{7,6},{8,9},{9,8},{10,11... | collective-permute-start | bytes 196616 | tf_op jit(solution)/shard_map/ppermute | solution.py:26
  3.0 7.5 %collective-permute-start.1 = (bf16[16,2048]{1,0:T(8,128)(2,1)}, bf16[16,2048]{1,0:T(8,128)(2,1)S(1)}, u32[]{:S(2)}, u32[]{:S(2)}) collective-permute-start(bf16[16,2048]{1,0:T(8,128)(2,1)} %param.6), channel_id=1, source_target_pairs={{0,2},{1,3},{2,0},{3,1},{4,6},{5,7},{6,4},{7,5},{8,10},{9,11},{10,... | collective-permute-start | bytes 196616 | tf_op jit(solution)/shard_map/ppermute | solution.py:26
  5.6 6.3 %collective-permute-start.2 = (bf16[16,2048]{1,0:T(8,128)(2,1)}, bf16[16,2048]{1,0:T(8,128)(2,1)S(1)}, u32[]{:S(2)}, u32[]{:S(2)}) collective-permute-start(bf16[16,2048]{1,0:T(8,128)(2,1)} %param.6), channel_id=1, source_target_pairs={{0,3},{1,2},{2,1},{3,0},{4,7},{5,6},{6,5},{7,4},{8,11},{9,10},{10,... | collective-permute-start | bytes 196616 | tf_op jit(solution)/shard_map/ppermute | solution.py:26
  5.6 6.3 %collective-permute-start.3 = (bf16[128,512]{1,0:T(8,128)(2,1)}, bf16[128,512]{1,0:T(8,128)(2,1)S(1)}, u32[]{:S(2)}, u32[]{:S(2)}) collective-permute-start(bf16[128,512]{1,0:T(8,128)(2,1)} %bitcast.15), channel_id=1, source_target_pairs={{0,4},{4,0},{8,12},{12,8},{16,20},{20,16},{24,28},{28,24},{1,5},{5... | collective-permute-start | bytes 393224 | tf_op jit(solution)/shard_map/ppermute | solution.py:26
  11.9 8.4 %copy-start.2 = (bf16[128,512]{1,0:T(8,128)(2,1)}, bf16[128,512]{1,0:T(8,128)(2,1)S(1)}, u32[]{:S(2)}) copy-start(bf16[128,512]{1,0:T(8,128)(2,1)S(1)} %collective-permute-done.3.oper_other) | copy-start | bytes 393220
  12.0 13.5 %collective-permute-start.7 = (bf16[64,2048]{1,0:T(8,128)(2,1)S(1)}, bf16[64,2048]{1,0:T(8,128)(2,1)S(1)}, u32[]{:S(2)}, u32[]{:S(2)}) collective-permute-start(bf16[64,2048]{1,0:T(8,128)(2,1)S(1)} %constant_dynamic-update-slice_fusion.refs_0_), channel_id=1, source_target_pairs={{0,8},{4,12},{8,0},{12,4},{16,24},{20,28},{24,16},{28,20},{1,9},{5... | collective-permute-start | bytes 786440 | tf_op jit(solution)/shard_map/ppermute | solution.py:26
  13.5 12.4 %collective-permute-start.9 = (bf16[64,2048]{1,0:T(8,128)(2,1)S(1)}, bf16[64,2048]{1,0:T(8,128)(2,1)S(1)}, u32[]{:S(2)}, u32[]{:S(2)}) collective-permute-start(bf16[64,2048]{1,0:T(8,128)(2,1)S(1)} %constant_dynamic-update-slice_fusion.refs_0_), channel_id=1, source_target_pairs={{0,16},{4,20},{8,24},{12,28},{16,0},{20,4},{24,8},{28,12},{1,17},{... | collective-permute-start | bytes 786440 | tf_op jit(solution)/shard_map/ppermute | solution.py:26
  15.0 11.0 %collective-permute-start.11 = (bf16[64,2048]{1,0:T(8,128)(2,1)S(1)}, bf16[64,2048]{1,0:T(8,128)(2,1)S(1)}, u32[]{:S(2)}, u32[]{:S(2)}) collective-permute-start(bf16[64,2048]{1,0:T(8,128)(2,1)S(1)} %constant_dynamic-update-slice_fusion.refs_0_), channel_id=1, source_target_pairs={{0,24},{4,28},{8,16},{12,20},{16,8},{20,12},{24,0},{28,4},{1,25},{... | collective-permute-start | bytes 786440 | tf_op jit(solution)/shard_map/ppermute | solution.py:26
  15.5 9.8 %collective-permute-start.5 = (f32[8,2560]{1,0:T(8,128)S(1)}, f32[8,2560]{1,0:T(8,128)S(1)}, u32[]{:S(2)}, u32[]{:S(2)}) collective-permute-start(f32[8,2560]{1,0:T(8,128)S(1)} %get-tuple-element.68), channel_id=1, source_target_pairs={{1,2},{2,1},{5,6},{6,5},{9,10},{10,9},{13,14},{14,13},{17,18},{18,... | collective-permute-start | bytes 245768 | tf_op jit(solution)/shard_map/ppermute | solution.py:186
  16.2 9.2 %collective-permute-start.6 = (f32[8,2560]{1,0:T(8,128)S(1)}, f32[8,2560]{1,0:T(8,128)S(1)}, u32[]{:S(2)}, u32[]{:S(2)}) collective-permute-start(f32[8,2560]{1,0:T(8,128)S(1)} %get-tuple-element.67), channel_id=1, source_target_pairs={{0,1},{1,0},{2,3},{3,2},{4,5},{5,4},{6,7},{7,6},{8,9},{9,8},{10,11... | collective-permute-start | bytes 245768 | tf_op jit(solution)/shard_map/ppermute | solution.py:187
  20.3 7.8 %copy-start.1 = (s32[2]{0:T(128)S(1)}, s32[2]{0:T(128)}, u32[]{:S(2)}) copy-start(s32[2]{0:T(128)} %pad_add_fusion.where) | copy-start | bytes 28
  25.4 1.6 %collective-permute-start.4 = (bf16[64,2048]{1,0:T(8,128)(2,1)S(1)}, bf16[64,2048]{1,0:T(8,128)(2,1)S(1)}, u32[]{:S(2)}, u32[]{:S(2)}) collective-permute-start(bf16[64,2048]{1,0:T(8,128)(2,1)S(1)} %constant_dynamic-update-slice_fusion.refs_0_), channel_id=1, source_target_pairs={{0,4},{4,0},{8,12},{12,8},{16,20},{20,16},{24,28},{28,24},{1,5},{5... | collective-permute-start | bytes 786440 | tf_op jit(solution)/shard_map/ppermute | solution.py:26
  25.5 1.9 %collective-permute-start.8 = (bf16[64,2048]{1,0:T(8,128)(2,1)S(1)}, bf16[64,2048]{1,0:T(8,128)(2,1)S(1)}, u32[]{:S(2)}, u32[]{:S(2)}) collective-permute-start(bf16[64,2048]{1,0:T(8,128)(2,1)S(1)} %collective-permute-done.7.refs_2_), channel_id=1, source_target_pairs={{0,4},{4,0},{8,12},{12,8},{16,20},{20,16},{24,28},{28,24},{1,5},{5... | collective-permute-start | bytes 786440 | tf_op jit(solution)/shard_map/ppermute | solution.py:26
  26.0 1.8 %collective-permute-start.10 = (bf16[64,2048]{1,0:T(8,128)(2,1)S(1)}, bf16[64,2048]{1,0:T(8,128)(2,1)S(1)}, u32[]{:S(2)}, u32[]{:S(2)}) collective-permute-start(bf16[64,2048]{1,0:T(8,128)(2,1)S(1)} %collective-permute-done.9.refs_4_), channel_id=1, source_target_pairs={{0,4},{4,0},{8,12},{12,8},{16,20},{20,16},{24,28},{28,24},{1,5},{5... | collective-permute-start | bytes 786440 | tf_op jit(solution)/shard_map/ppermute | solution.py:26
  26.1 2.0 %collective-permute-start.12 = (bf16[64,2048]{1,0:T(8,128)(2,1)S(1)}, bf16[64,2048]{1,0:T(8,128)(2,1)S(1)}, u32[]{:S(2)}, u32[]{:S(2)}) collective-permute-start(bf16[64,2048]{1,0:T(8,128)(2,1)S(1)} %collective-permute-done.11.refs_6_), channel_id=1, source_target_pairs={{0,4},{4,0},{8,12},{12,8},{16,20},{20,16},{24,28},{28,24},{1,5},{5... | collective-permute-start | bytes 786440 | tf_op jit(solution)/shard_map/ppermute | solution.py:26
  38.8 2.0 %collective-permute-start.13 = (bf16[128,2048]{1,0:T(8,128)(2,1)S(1)}, bf16[128,2048]{1,0:T(8,128)(2,1)S(1)}, u32[]{:S(2)}, u32[]{:S(2)}) collective-permute-start(bf16[128,2048]{1,0:T(8,128)(2,1)S(1)} %solve.1.part), channel_id=1, source_target_pairs={{0,4},{4,0},{8,12},{12,8},{16,20},{20,16},{24,28},{28,24},{1,5},{5... | collective-permute-start | bytes 1572872 | tf_op jit(solution)/shard_map/ppermute | solution.py:26
  41.2 6.8 %collective-permute-start.18 = (bf16[32,2048]{1,0:T(8,128)(2,1)S(1)}, bf16[32,2048]{1,0:T(8,128)(2,1)S(1)}, u32[]{:S(2)}, u32[]{:S(2)}) collective-permute-start(bf16[32,2048]{1,0:T(8,128)(2,1)S(1)} %get-tuple-element.58), channel_id=1, source_target_pairs={{0,24},{4,28},{8,16},{12,20},{16,8},{20,12},{24,0},{28,4},{1,25},{... | collective-permute-start | bytes 393224 | tf_op jit(solution)/shard_map/ppermute | solution.py:26
  43.7 7.3 %collective-permute-start.19 = (bf16[32,2048]{1,0:T(8,128)(2,1)S(1)}, bf16[32,2048]{1,0:T(8,128)(2,1)S(1)}, u32[]{:S(2)}, u32[]{:S(2)}) collective-permute-start(bf16[32,2048]{1,0:T(8,128)(2,1)S(1)} %get-tuple-element.59), channel_id=1, source_target_pairs={{0,16},{4,20},{8,24},{12,28},{16,0},{20,4},{24,8},{28,12},{1,17},{... | collective-permute-start | bytes 393224 | tf_op jit(solution)/shard_map/ppermute | solution.py:26
  44.2 7.2 %collective-permute-start.20 = (bf16[32,2048]{1,0:T(8,128)(2,1)S(1)}, bf16[32,2048]{1,0:T(8,128)(2,1)S(1)}, u32[]{:S(2)}, u32[]{:S(2)}) collective-permute-start(bf16[32,2048]{1,0:T(8,128)(2,1)S(1)} %get-tuple-element.60), channel_id=1, source_target_pairs={{0,8},{4,12},{8,0},{12,4},{16,24},{20,28},{24,16},{28,20},{1,9},{5... | collective-permute-start | bytes 393224 | tf_op jit(solution)/shard_map/ppermute | solution.py:26
  44.7 9.5 %collective-permute-start.14 = (bf16[32,2048]{1,0:T(8,128)(2,1)S(1)}, bf16[32,2048]{1,0:T(8,128)(2,1)S(1)}, u32[]{:S(2)}, u32[]{:S(2)}) collective-permute-start(bf16[32,2048]{1,0:T(8,128)(2,1)S(1)} %get-tuple-element.53), channel_id=1, source_target_pairs={{0,8},{4,12},{8,0},{12,4},{16,24},{20,28},{24,16},{28,20},{1,9},{5... | collective-permute-start | bytes 393224 | tf_op jit(solution)/shard_map/ppermute | solution.py:26
  46.2 8.1 %collective-permute-start.15 = (bf16[32,2048]{1,0:T(8,128)(2,1)S(1)}, bf16[32,2048]{1,0:T(8,128)(2,1)S(1)}, u32[]{:S(2)}, u32[]{:S(2)}) collective-permute-start(bf16[32,2048]{1,0:T(8,128)(2,1)S(1)} %get-tuple-element.54), channel_id=1, source_target_pairs={{0,16},{4,20},{8,24},{12,28},{16,0},{20,4},{24,8},{28,12},{1,17},{... | collective-permute-start | bytes 393224 | tf_op jit(solution)/shard_map/ppermute | solution.py:26
  48.0 8.1 %collective-permute-start.16 = (bf16[32,2048]{1,0:T(8,128)(2,1)S(1)}, bf16[32,2048]{1,0:T(8,128)(2,1)S(1)}, u32[]{:S(2)}, u32[]{:S(2)}) collective-permute-start(bf16[32,2048]{1,0:T(8,128)(2,1)S(1)} %get-tuple-element.55), channel_id=1, source_target_pairs={{0,24},{4,28},{8,16},{12,20},{16,8},{20,12},{24,0},{28,4},{1,25},{... | collective-permute-start | bytes 393224 | tf_op jit(solution)/shard_map/ppermute | solution.py:26
  51.5 6.1 %collective-permute-start.22 = (bf16[16,2048]{1,0:T(8,128)(2,1)S(1)}, bf16[16,2048]{1,0:T(8,128)(2,1)S(1)}, u32[]{:S(2)}, u32[]{:S(2)}) collective-permute-start(bf16[16,2048]{1,0:T(8,128)(2,1)S(1)} %get-tuple-element.62), channel_id=1, source_target_pairs={{0,3},{1,2},{2,1},{3,0},{4,7},{5,6},{6,5},{7,4},{8,11},{9,10},{10,... | collective-permute-start | bytes 196616 | tf_op jit(solution)/shard_map/ppermute | solution.py:26
  53.6 5.9 %collective-permute-start.21 = (bf16[16,2048]{1,0:T(8,128)(2,1)S(1)}, bf16[16,2048]{1,0:T(8,128)(2,1)S(1)}, u32[]{:S(2)}, u32[]{:S(2)}) collective-permute-start(bf16[16,2048]{1,0:T(8,128)(2,1)S(1)} %get-tuple-element.61), channel_id=1, source_target_pairs={{0,2},{1,3},{2,0},{3,1},{4,6},{5,7},{6,4},{7,5},{8,10},{9,11},{10,... | collective-permute-start | bytes 196616 | tf_op jit(solution)/shard_map/ppermute | solution.py:26
  56.2 4.3 %collective-permute-start.17 = (bf16[16,2048]{1,0:T(8,128)(2,1)S(1)}, bf16[16,2048]{1,0:T(8,128)(2,1)S(1)}, u32[]{:S(2)}, u32[]{:S(2)}) collective-permute-start(bf16[16,2048]{1,0:T(8,128)(2,1)S(1)} %get-tuple-element.57), channel_id=1, source_target_pairs={{0,1},{1,0},{2,3},{3,2},{4,5},{5,4},{6,7},{7,6},{8,9},{9,8},{10,11... | collective-permute-start | bytes 196616 | tf_op jit(solution)/shard_map/ppermute | solution.py:26

commit v5 on v4

--- a/solution.py
+++ b/solution.py
@@ -29,7 +29,7 @@
 def solve_kernel(n_blocks, n_slab, where, factor, *refs):
     blocks = refs[:n_blocks]
     oper, oper_up, oper_down, src, src_up, src_down, rec, lateral, moved = refs[n_blocks : n_blocks + 9]
-    out, inverse, field, field_lo = refs[n_blocks + 9 :]
+    out, inverse, field, field_lo, middle = refs[n_blocks + 9 :]
     slab = where[1]
     depth, width = src.shape
     tall = depth + 2 * HALO
@@ -59,15 +59,18 @@
             beside = pltpu.roll(before, 1, 0) + pltpu.roll(before, tall - 1, 0)
             after = (source(cols) + 0.5 * beside + side) * inverse[:, cols]
             field[new, :, cols] = after
-            field_lo[new, :, cols] = after.astype(jnp.bfloat16)
+            if sweep < SWEEPS - 2:
+                field_lo[new, :, cols] = after.astype(jnp.bfloat16)
+            else:
+                middle[:, cols] = after[HALO : HALO + depth].astype(jnp.bfloat16)
     old = (SWEEPS - 2) % 2
     mine = slice(HALO, HALO + depth)
     for n in range(0, width, TILE):
         cols = slice(n, n + TILE)
-        side = jnp.dot(field_lo[old], lateral[:, cols], preferred_element_type=jnp.float32)
+        side = jnp.dot(middle[...], lateral[:, cols], preferred_element_type=jnp.float32)
         before = field[old, :, cols]
         beside = pltpu.roll(before, 1, 0) + pltpu.roll(before, tall - 1, 0)
-        after = (src[:, cols] + 0.5 * beside[mine] + side[mine]) * inverse[mine, cols]
+        after = (src[:, cols] + 0.5 * beside[mine] + side) * inverse[mine, cols]
         out[:, cols] = (after * rec[:, cols]).astype(jnp.bfloat16)
 
 
@@ -140,7 +143,7 @@
             far[m - 1][:, cols] = rows[CUT * tile :]
 
 
-def plane_kernel(n_chips, tile, begin, n_keep, keep, *refs):
+def plane_kernel(n_chips, tile, begin, keep, *refs):
     gets, outs = refs[: n_chips - 1], refs[n_chips - 1 :]
     rows = gets[0].shape[0]
     for n in range(0, keep.shape[1], TILE):
@@ -189,7 +192,7 @@
     tile = fine_model.shape[0]
     order = [(2 * m + b, j) for m in range(n_chips) for b in range(2) for j in range(n_slab)]
     lateral, src, rec, moved, turned = stage(where, order, n_freq, n_slab, tile, oper, oper_other, lateral, src, rec)
-    far, near, plane[1] = lax.optimization_barrier((far, near, plane[1]))
+    near, far, plane[1] = lax.optimization_barrier((near, far, plane[1]))
     above = jnp.where(odd, near, far)
     below = jnp.where(odd, far, near)
     blocks = []
@@ -205,6 +208,7 @@
             pltpu.VMEM((tall, width), f32),
             pltpu.VMEM((2, tall, width), f32),
             pltpu.VMEM((2, tall, width), bf16),
+            pltpu.VMEM((depth, width), bf16),
         ],
         compiler_params=pltpu.CompilerParams(vmem_limit_bytes=12 * MIB),
         cost_estimate=cost(2 * (SWEEPS - 1) * tall * width * width, 2 * width * width),
@@ -230,7 +234,7 @@
     out_shape = [jax.ShapeDtypeStruct((tile, width), jnp.float32)] * n_keep
     out_shape += [jax.ShapeDtypeStruct((tile, width), jnp.bfloat16)] * (count - n_keep)
     return pl.pallas_call(
-        functools.partial(plane_kernel, len(gets) + 1, tile, begin * tile, n_keep),
+        functools.partial(plane_kernel, len(gets) + 1, tile, begin * tile),
         out_shape=out_shape,
         in_specs=[VMEM] * (len(gets) + 1),
         out_specs=[VMEM] * count,

time: 61.5 us -> 61 us (level)
  starting transfers between devices: 26.4 us -> 23.3 us
  waiting for transfers between devices: 13.9 us -> 16.6 us
    ppermute x1, starting transfers between devices: 3.43 us -> 0.07 us  [shards(): lax.ppermute(jnp.where(odd, edges, edges_last), 'slab', [(i, i ^ 1) for i...]
    ppermute x21, waiting for transfers between devices: 13.9 us -> 16.6 us  [xor_permute(): return lax.ppermute(value, axis, [(i, i ^ mask) for i in range(size)])]
  transfers between devices with their start and end apart: 23 -> 23, of which waited for: 15 -> 12; matrix products, arithmetic and copies ran while one was open for 5% -> 5% of each run, Pallas kernels for 8% -> 9%
where the time goes in v5:
time: 61 us; the launch traced here: 60.7 us
  starting transfers between devices  23.3 us (38%)
  waiting for transfers between devices  16.6 us (27%)
  Pallas kernels  16.1 us (26%)
  other arithmetic  2.1 us (3%)
  local copies, waits for them, and re-layouts  1.78 us (3%)
  between operations  0.85 us (1%)
    ppermute x21, starting transfers between devices, xor_permute(): return lax.ppermute(value, axis, [(i, i ^ mask) for i in range(size)])  22.5 us
    ppermute x21, waiting for transfers between devices, xor_permute(): return lax.ppermute(value, axis, [(i, i ^ mask) for i in range(size)])  16.6 us
    pallas_call x1, Pallas kernels, shards(): pl.pallas_call(functools.partial(solve_kernel, len(blocks), n_slab), out_...  10.5 us
    pallas_call x1, Pallas kernels, stage(): pl.pallas_call(functools.partial(stage_kernel, order, n_freq, n_slab, til...  5.06 us
  transfers between devices with their start and end apart: 23, of which 12 were waited for; matrix products, arithmetic and copies ran while one was open for 5% of the time, Pallas kernels for 9%

profile of v5, /device:TPU:0, one launch (start us, length us, event | category | flops | bytes accessed | tf_op | source)
XLA Modules:
  0.0 60.7 jit_solution(5972105299939710286)
XLA Ops:
  0.0 0.0 copy-start
  0.0 3.0 %collective-permute-start = (bf16[16,2048]{1,0:T(8,128)(2,1)}, bf16[16,2048]{1,0:T(8,128)(2,1)S(1)}, u32[]{:S(2)}, u32[]{:S(2)}) collective-permute-start(bf16[16,2048]{1,0:T(8,128)(2,1)} %param.6), channel_id=1, source_target_pairs={{0,1},{1,0},{2,3},{3,2},{4,5},{5,4},{6,7},{7,6},{8,9},{9,8},{10,11... | collective-permute-start | bytes 196616 | tf_op jit(solution)/shard_map/ppermute | solution.py:26
  3.0 2.6 %collective-permute-start.1 = (bf16[16,2048]{1,0:T(8,128)(2,1)}, bf16[16,2048]{1,0:T(8,128)(2,1)S(1)}, u32[]{:S(2)}, u32[]{:S(2)}) collective-permute-start(bf16[16,2048]{1,0:T(8,128)(2,1)} %param.6), channel_id=1, source_target_pairs={{0,2},{1,3},{2,0},{3,1},{4,6},{5,7},{6,4},{7,5},{8,10},{9,11},{10,... | collective-permute-start | bytes 196616 | tf_op jit(solution)/shard_map/ppermute | solution.py:26
  5.6 0.0 collective-permute-start.2
  5.6 0.0 collective-permute-start.3
  5.6 0.7 %bitcast_convert_fusion = (f32[8,512]{1,0:T(8,128)S(1)}, f32[8,512]{1,0:T(8,128)S(1)}) fusion(bf16[1,128,512]{2,1,0:T(8,128)(2,1)} %param.7), kind=kLoop, calls=%fused_computation.13 | loop fusion | flops 8192 | bytes 49152 | tf_op jit(solution)/shard_map/convert_element_type | solution.py:179
  6.3 0.9 %slice_bitcast_fusion = (f32[8,2048]{1,0:T(8,128)S(1)}, f32[8,2048]{1,0:T(8,128)S(1)}) fusion(f32[1,128,2048]{2,1,0:T(8,128)} %param.10), kind=kLoop, calls=%fused_computation.3 | loop fusion | bytes 262144 | tf_op jit(solution)/shard_map/slice | solution.py:179
  7.2 0.8 %constant_dynamic-update-slice_fusion.3 = bf16[64,2048]{1,0:T(8,128)(2,1)S(1)} fusion(bf16[16,2048]{1,0:T(8,128)(2,1)} %param.6), kind=kLoop, calls=%fused_computation.12 | loop fusion | bytes 131072
  8.7 0.0 collective-permute-done
  8.8 1.8 %collective-permute-done.1 = bf16[16,2048]{1,0:T(8,128)(2,1)S(1)} collective-permute-done((bf16[16,2048]{1,0:T(8,128)(2,1)}, bf16[16,2048]{1,0:T(8,128)(2,1)S(1)}, u32[]{:S(2)}, u32[]{:S(2)}) %collective-permute-start.1) | collective-permute-done | bytes 65568 | tf_op jit(solution)/shard_map/ppermute | solution.py:26
  10.5 1.4 %collective-permute-done.2 = bf16[16,2048]{1,0:T(8,128)(2,1)S(1)} collective-permute-done((bf16[16,2048]{1,0:T(8,128)(2,1)}, bf16[16,2048]{1,0:T(8,128)(2,1)S(1)}, u32[]{:S(2)}, u32[]{:S(2)}) %collective-permute-start.2) | collective-permute-done | bytes 65568 | tf_op jit(solution)/shard_map/ppermute | solution.py:26
  11.9 0.0 collective-permute-done.3.oper_other
  11.9 0.0 copy-start.2
  12.0 1.6 %collective-permute-start.7 = (bf16[64,2048]{1,0:T(8,128)(2,1)S(1)}, bf16[64,2048]{1,0:T(8,128)(2,1)S(1)}, u32[]{:S(2)}, u32[]{:S(2)}) collective-permute-start(bf16[64,2048]{1,0:T(8,128)(2,1)S(1)} %constant_dynamic-update-slice_fusion.refs_0_), channel_id=1, source_target_pairs={{0,8},{4,12},{8,0},{12,4},{16,24},{20,28},{24,16},{28,20},{1,9},{5... | collective-permute-start | bytes 786440 | tf_op jit(solution)/shard_map/ppermute | solution.py:26
  13.5 1.5 %collective-permute-start.9 = (bf16[64,2048]{1,0:T(8,128)(2,1)S(1)}, bf16[64,2048]{1,0:T(8,128)(2,1)S(1)}, u32[]{:S(2)}, u32[]{:S(2)}) collective-permute-start(bf16[64,2048]{1,0:T(8,128)(2,1)S(1)} %constant_dynamic-update-slice_fusion.refs_0_), channel_id=1, source_target_pairs={{0,16},{4,20},{8,24},{12,28},{16,0},{20,4},{24,8},{28,12},{1,17},{... | collective-permute-start | bytes 786440 | tf_op jit(solution)/shard_map/ppermute | solution.py:26
  15.0 0.5 collective-permute-start.11
  15.5 0.1 collective-permute-start.5
  15.6 0.7 %collective-permute-start.6 = (f32[8,2560]{1,0:T(8,128)S(1)}, f32[8,2560]{1,0:T(8,128)S(1)}, u32[]{:S(2)}, u32[]{:S(2)}) collective-permute-start(f32[8,2560]{1,0:T(8,128)S(1)} %get-tuple-element.67), channel_id=1, source_target_pairs={{1,2},{2,1},{5,6},{6,5},{9,10},{10,9},{13,14},{14,13},{17,18},{18,... | collective-permute-start | bytes 245768 | tf_op jit(solution)/shard_map/ppermute | solution.py:189
  16.3 0.7 %pad_add_fusion.where = s32[2]{0:T(128)} fusion(s32[1]{0:T(128)} %bitcast.1, s32[1]{0:T(128)} %bitcast), kind=kLoop, calls=%fused_computation.15 | loop fusion | flops 2 | bytes 16 | tf_op jit(solution)/shard_map/stack | solution.py:173
  16.9 0.0 copy-done.2
  16.9 0.0 copy-start.1
  16.9 5.1 %stage.1 = (bf16[2048,2048]{1,0:T(8,128)(2,1)S(1)}, f32[128,2048]{1,0:T(8,128)S(1)}, f32[128,2048]{1,0:T(8,128)S(1)}, bf16[512,512]{1,0:T(8,128)(2,1)S(1)}, bf16[256,256]{1,0:T(8,128)(2,1)S(1)}) custom-call(s32[2]{0:T(128)} %pad_add_fusion.where, bf16[128,512]{1,0:T(8,128)(2,1)} %bitcast.16, bf16[128,512]{1,0:T(8,128)(2,1)} %copy-done.2, ...), custom_call_target="tpu_custom_call" | custom-call | bytes 22282240 | tf_op jit(solution)/shard_map/stage/pallas_call | solution.py:117
  22.0 0.0 collective-permute-done.5
  22.0 0.1 collective-permute-start.4
  22.1 0.0 collective-permute-done.6
  22.1 0.0 collective-permute-done.7.refs_2_
  22.1 0.5 collective-permute-start.8
  22.6 2.7 %collective-permute-done.9.refs_4_ = bf16[64,2048]{1,0:T(8,128)(2,1)S(1)} collective-permute-done((bf16[64,2048]{1,0:T(8,128)(2,1)S(1)}, bf16[64,2048]{1,0:T(8,128)(2,1)S(1)}, u32[]{:S(2)}, u32[]{:S(2)}) %collective-permute-start.9) | collective-permute-done | bytes 262176 | tf_op jit(solution)/shard_map/ppermute | solution.py:26
  25.3 0.0 collective-permute-start.10
  25.3 0.0 collective-permute-done.11.refs_6_
  25.3 0.5 collective-permute-start.12
  25.9 0.0 collective-permute-done.4.refs_1_
  25.9 0.0 collective-permute-done.8.refs_3_
  25.9 0.9 %collective-permute-done.10.refs_5_ = bf16[64,2048]{1,0:T(8,128)(2,1)S(1)} collective-permute-done((bf16[64,2048]{1,0:T(8,128)(2,1)S(1)}, bf16[64,2048]{1,0:T(8,128)(2,1)S(1)}, u32[]{:S(2)}, u32[]{:S(2)}) %collective-permute-start.10) | collective-permute-done | bytes 262176 | tf_op jit(solution)/shard_map/ppermute | solution.py:26
  26.8 0.4 collective-permute-done.12.refs_7_
  27.2 0.0 copy-done
  27.2 0.0 copy-done.1
  27.2 10.5 %solve.1.part = bf16[128,2048]{1,0:T(8,128)(2,1)S(1)} custom-call(s32[2]{0:T(128)S(1)} %copy-done.1, f32[1]{0:T(128)S(6)} %copy.10.factor, bf16[64,2048]{1,0:T(8,128)(2,1)S(1)} %constant_dynamic-update-slice_fusion.refs_0_, bf16[64,2048]{1,0:T(8,128)(2,1)S(1)} %collective-permute-done.4.refs_1_, bf16[64,2048]{1,0:T(8,128)(2,1)S(1)} %collective-permute-done.7.refs_2_, ...), custom_call_target="tpu_custom_call" | custom-call | flops 8455716864 | bytes 8388608 | tf_op jit(solution)/shard_map/solve/pallas_call | solution.py:202
  37.7 0.2 collective-permute-start.13
  37.9 1.8 %collective-permute-done.13.part_other = bf16[128,2048]{1,0:T(8,128)(2,1)S(1)} collective-permute-done((bf16[128,2048]{1,0:T(8,128)(2,1)S(1)}, bf16[128,2048]{1,0:T(8,128)(2,1)S(1)}, u32[]{:S(2)}, u32[]{:S(2)}) %collective-permute-start.13) | collective-permute-done | bytes 524320 | tf_op jit(solution)/shard_map/ppermute | solution.py:26
  39.7 0.4 back.1
  40.1 1.6 %collective-permute-start.18 = (bf16[32,2048]{1,0:T(8,128)(2,1)S(1)}, bf16[32,2048]{1,0:T(8,128)(2,1)S(1)}, u32[]{:S(2)}, u32[]{:S(2)}) collective-permute-start(bf16[32,2048]{1,0:T(8,128)(2,1)S(1)} %get-tuple-element.58), channel_id=1, source_target_pairs={{0,24},{4,28},{8,16},{12,20},{16,8},{20,12},{24,0},{28,4},{1,25},{... | collective-permute-start | bytes 393224 | tf_op jit(solution)/shard_map/ppermute | solution.py:26
  41.7 0.8 %collective-permute-start.19 = (bf16[32,2048]{1,0:T(8,128)(2,1)S(1)}, bf16[32,2048]{1,0:T(8,128)(2,1)S(1)}, u32[]{:S(2)}, u32[]{:S(2)}) collective-permute-start(bf16[32,2048]{1,0:T(8,128)(2,1)S(1)} %get-tuple-element.59), channel_id=1, source_target_pairs={{0,16},{4,20},{8,24},{12,28},{16,0},{20,4},{24,8},{28,12},{1,17},{... | collective-permute-start | bytes 393224 | tf_op jit(solution)/shard_map/ppermute | solution.py:26
  42.5 1.2 %collective-permute-start.20 = (bf16[32,2048]{1,0:T(8,128)(2,1)S(1)}, bf16[32,2048]{1,0:T(8,128)(2,1)S(1)}, u32[]{:S(2)}, u32[]{:S(2)}) collective-permute-start(bf16[32,2048]{1,0:T(8,128)(2,1)S(1)} %get-tuple-element.60), channel_id=1, source_target_pairs={{0,8},{4,12},{8,0},{12,4},{16,24},{20,28},{24,16},{28,20},{1,9},{5... | collective-permute-start | bytes 393224 | tf_op jit(solution)/shard_map/ppermute | solution.py:26
  43.7 0.9 %collective-permute-start.14 = (bf16[32,2048]{1,0:T(8,128)(2,1)S(1)}, bf16[32,2048]{1,0:T(8,128)(2,1)S(1)}, u32[]{:S(2)}, u32[]{:S(2)}) collective-permute-start(bf16[32,2048]{1,0:T(8,128)(2,1)S(1)} %get-tuple-element.53), channel_id=1, source_target_pairs={{0,8},{4,12},{8,0},{12,4},{16,24},{20,28},{24,16},{28,20},{1,9},{5... | collective-permute-start | bytes 393224 | tf_op jit(solution)/shard_map/ppermute | solution.py:26
  44.5 1.2 %collective-permute-start.15 = (bf16[32,2048]{1,0:T(8,128)(2,1)S(1)}, bf16[32,2048]{1,0:T(8,128)(2,1)S(1)}, u32[]{:S(2)}, u32[]{:S(2)}) collective-permute-start(bf16[32,2048]{1,0:T(8,128)(2,1)S(1)} %get-tuple-element.54), channel_id=1, source_target_pairs={{0,16},{4,20},{8,24},{12,28},{16,0},{20,4},{24,8},{28,12},{1,17},{... | collective-permute-start | bytes 393224 | tf_op jit(solution)/shard_map/ppermute | solution.py:26
  45.8 1.7 %collective-permute-done.18.refs_0_ = bf16[32,2048]{1,0:T(8,128)(2,1)S(1)} collective-permute-done((bf16[32,2048]{1,0:T(8,128)(2,1)S(1)}, bf16[32,2048]{1,0:T(8,128)(2,1)S(1)}, u32[]{:S(2)}, u32[]{:S(2)}) %collective-permute-start.18) | collective-permute-done | bytes 131104 | tf_op jit(solution)/shard_map/ppermute | solution.py:26
  47.5 1.5 %collective-permute-start.16 = (bf16[32,2048]{1,0:T(8,128)(2,1)S(1)}, bf16[32,2048]{1,0:T(8,128)(2,1)S(1)}, u32[]{:S(2)}, u32[]{:S(2)}) collective-permute-start(bf16[32,2048]{1,0:T(8,128)(2,1)S(1)} %get-tuple-element.55), channel_id=1, source_target_pairs={{0,24},{4,28},{8,16},{12,20},{16,8},{20,12},{24,0},{28,4},{1,25},{... | collective-permute-start | bytes 393224 | tf_op jit(solution)/shard_map/ppermute | solution.py:26
  49.0 0.6 collective-permute-done.19.refs_1_
  49.5 0.8 %collective-permute-done.20.refs_2_ = bf16[32,2048]{1,0:T(8,128)(2,1)S(1)} collective-permute-done((bf16[32,2048]{1,0:T(8,128)(2,1)S(1)}, bf16[32,2048]{1,0:T(8,128)(2,1)S(1)}, u32[]{:S(2)}, u32[]{:S(2)}) %collective-permute-start.20) | collective-permute-done | bytes 131104 | tf_op jit(solution)/shard_map/ppermute | solution.py:26
  50.3 0.1 plane.3
  50.4 3.1 %collective-permute-start.22 = (bf16[16,2048]{1,0:T(8,128)(2,1)S(1)}, bf16[16,2048]{1,0:T(8,128)(2,1)S(1)}, u32[]{:S(2)}, u32[]{:S(2)}) collective-permute-start(bf16[16,2048]{1,0:T(8,128)(2,1)S(1)} %get-tuple-element.62), channel_id=1, source_target_pairs={{0,3},{1,2},{2,1},{3,0},{4,7},{5,6},{6,5},{7,4},{8,11},{9,10},{10,... | collective-permute-start | bytes 196616 | tf_op jit(solution)/shard_map/ppermute | solution.py:26
  53.5 0.1 collective-permute-start.21
  53.6 0.0 collective-permute-done.14.refs_0_
  53.6 0.0 collective-permute-done.15.refs_1_
  53.6 1.5 %collective-permute-done.16.refs_2_ = bf16[32,2048]{1,0:T(8,128)(2,1)S(1)} collective-permute-done((bf16[32,2048]{1,0:T(8,128)(2,1)S(1)}, bf16[32,2048]{1,0:T(8,128)(2,1)S(1)}, u32[]{:S(2)}, u32[]{:S(2)}) %collective-permute-start.16) | collective-permute-done | bytes 131104 | tf_op jit(solution)/shard_map/ppermute | solution.py:26
  55.1 0.1 plane.2
  55.1 1.7 %collective-permute-start.17 = (bf16[16,2048]{1,0:T(8,128)(2,1)S(1)}, bf16[16,2048]{1,0:T(8,128)(2,1)S(1)}, u32[]{:S(2)}, u32[]{:S(2)}) collective-permute-start(bf16[16,2048]{1,0:T(8,128)(2,1)S(1)} %get-tuple-element.57), channel_id=1, source_target_pairs={{0,1},{1,0},{2,3},{3,2},{4,5},{5,4},{6,7},{7,6},{8,9},{9,8},{10,11... | collective-permute-start | bytes 196616 | tf_op jit(solution)/shard_map/ppermute | solution.py:26
  56.9 0.0 collective-permute-done.22
  56.9 2.5 %collective-permute-done.21 = bf16[16,2048]{1,0:T(8,128)(2,1)S(1)} collective-permute-done((bf16[16,2048]{1,0:T(8,128)(2,1)S(1)}, bf16[16,2048]{1,0:T(8,128)(2,1)S(1)}, u32[]{:S(2)}, u32[]{:S(2)}) %collective-permute-start.21) | collective-permute-done | bytes 65568 | tf_op jit(solution)/shard_map/ppermute | solution.py:26
  59.4 0.6 %collective-permute-done.17 = bf16[16,2048]{1,0:T(8,128)(2,1)S(1)} collective-permute-done((bf16[16,2048]{1,0:T(8,128)(2,1)S(1)}, bf16[16,2048]{1,0:T(8,128)(2,1)S(1)}, u32[]{:S(2)}, u32[]{:S(2)}) %collective-permute-start.17) | collective-permute-done | bytes 65568 | tf_op jit(solution)/shard_map/ppermute | solution.py:26
  60.0 0.7 %convert_add_fusion = f32[16,2048]{1,0:T(8,128)} fusion(bf16[16,2048]{1,0:T(8,128)(2,1)S(1)} %collective-permute-done.22, bf16[16,2048]{1,0:T(8,128)(2,1)S(1)} %collective-permute-done.21, f32[16,2048]{1,0:T(8,128)S(1)} %get-tuple-element.56, bf16[16,2048]{1,0:T(8,128)(2,1)S(1)} %collective-permute-done.17), kind=kLoop, calls=%fused_computation | loop fusion | flops 196608 | bytes 458752 | tf_op jit(solution)/shard_map/add | solution.py:228
  (10 shorter events, 0.1 us)
Async XLA Ops:
  0.0 27.2 %copy-start = (bf16[1,128,512]{2,1,0:T(8,128)(2,1)S(1)}, bf16[1,128,512]{2,1,0:T(8,128)(2,1)}, u32[]{:S(2)}) copy-start(bf16[1,128,512]{2,1,0:T(8,128)(2,1)} %param.7) | copy-start | bytes 393220
  0.0 8.7 %collective-permute-start = (bf16[16,2048]{1,0:T(8,128)(2,1)}, bf16[16,2048]{1,0:T(8,128)(2,1)S(1)}, u32[]{:S(2)}, u32[]{:S(2)}) collective-permute-start(bf16[16,2048]{1,0:T(8,128)(2,1)} %param.6), channel_id=1, source_target_pairs={{0,1},{1,0},{2,3},{3,2},{4,5},{5,4},{6,7},{7,6},{8,9},{9,8},{10,11... | collective-permute-start | bytes 196616 | tf_op jit(solution)/shard_map/ppermute | solution.py:26
  3.0 7.5 %collective-permute-start.1 = (bf16[16,2048]{1,0:T(8,128)(2,1)}, bf16[16,2048]{1,0:T(8,128)(2,1)S(1)}, u32[]{:S(2)}, u32[]{:S(2)}) collective-permute-start(bf16[16,2048]{1,0:T(8,128)(2,1)} %param.6), channel_id=1, source_target_pairs={{0,2},{1,3},{2,0},{3,1},{4,6},{5,7},{6,4},{7,5},{8,10},{9,11},{10,... | collective-permute-start | bytes 196616 | tf_op jit(solution)/shard_map/ppermute | solution.py:26
  5.6 6.3 %collective-permute-start.2 = (bf16[16,2048]{1,0:T(8,128)(2,1)}, bf16[16,2048]{1,0:T(8,128)(2,1)S(1)}, u32[]{:S(2)}, u32[]{:S(2)}) collective-permute-start(bf16[16,2048]{1,0:T(8,128)(2,1)} %param.6), channel_id=1, source_target_pairs={{0,3},{1,2},{2,1},{3,0},{4,7},{5,6},{6,5},{7,4},{8,11},{9,10},{10,... | collective-permute-start | bytes 196616 | tf_op jit(solution)/shard_map/ppermute | solution.py:26
  5.6 6.3 %collective-permute-start.3 = (bf16[128,512]{1,0:T(8,128)(2,1)}, bf16[128,512]{1,0:T(8,128)(2,1)S(1)}, u32[]{:S(2)}, u32[]{:S(2)}) collective-permute-start(bf16[128,512]{1,0:T(8,128)(2,1)} %bitcast.15), channel_id=1, source_target_pairs={{0,4},{4,0},{8,12},{12,8},{16,20},{20,16},{24,28},{28,24},{1,5},{5... | collective-permute-start | bytes 393224 | tf_op jit(solution)/shard_map/ppermute | solution.py:26
  11.9 5.0 %copy-start.2 = (bf16[128,512]{1,0:T(8,128)(2,1)}, bf16[128,512]{1,0:T(8,128)(2,1)S(1)}, u32[]{:S(2)}) copy-start(bf16[128,512]{1,0:T(8,128)(2,1)S(1)} %collective-permute-done.3.oper_other) | copy-start | bytes 393220
  12.0 10.2 %collective-permute-start.7 = (bf16[64,2048]{1,0:T(8,128)(2,1)S(1)}, bf16[64,2048]{1,0:T(8,128)(2,1)S(1)}, u32[]{:S(2)}, u32[]{:S(2)}) collective-permute-start(bf16[64,2048]{1,0:T(8,128)(2,1)S(1)} %constant_dynamic-update-slice_fusion.refs_0_), channel_id=1, source_target_pairs={{0,8},{4,12},{8,0},{12,4},{16,24},{20,28},{24,16},{28,20},{1,9},{5... | collective-permute-start | bytes 786440 | tf_op jit(solution)/shard_map/ppermute | solution.py:26
  13.5 11.7 %collective-permute-start.9 = (bf16[64,2048]{1,0:T(8,128)(2,1)S(1)}, bf16[64,2048]{1,0:T(8,128)(2,1)S(1)}, u32[]{:S(2)}, u32[]{:S(2)}) collective-permute-start(bf16[64,2048]{1,0:T(8,128)(2,1)S(1)} %constant_dynamic-update-slice_fusion.refs_0_), channel_id=1, source_target_pairs={{0,16},{4,20},{8,24},{12,28},{16,0},{20,4},{24,8},{28,12},{1,17},{... | collective-permute-start | bytes 786440 | tf_op jit(solution)/shard_map/ppermute | solution.py:26
  15.0 10.2 %collective-permute-start.11 = (bf16[64,2048]{1,0:T(8,128)(2,1)S(1)}, bf16[64,2048]{1,0:T(8,128)(2,1)S(1)}, u32[]{:S(2)}, u32[]{:S(2)}) collective-permute-start(bf16[64,2048]{1,0:T(8,128)(2,1)S(1)} %constant_dynamic-update-slice_fusion.refs_0_), channel_id=1, source_target_pairs={{0,24},{4,28},{8,16},{12,20},{16,8},{20,12},{24,0},{28,4},{1,25},{... | collective-permute-start | bytes 786440 | tf_op jit(solution)/shard_map/ppermute | solution.py:26
  15.5 6.5 %collective-permute-start.5 = (f32[8,2560]{1,0:T(8,128)S(1)}, f32[8,2560]{1,0:T(8,128)S(1)}, u32[]{:S(2)}, u32[]{:S(2)}) collective-permute-start(f32[8,2560]{1,0:T(8,128)S(1)} %get-tuple-element.68), channel_id=1, source_target_pairs={{0,1},{1,0},{2,3},{3,2},{4,5},{5,4},{6,7},{7,6},{8,9},{9,8},{10,11... | collective-permute-start | bytes 245768 | tf_op jit(solution)/shard_map/ppermute | solution.py:190
  15.6 6.5 %collective-permute-start.6 = (f32[8,2560]{1,0:T(8,128)S(1)}, f32[8,2560]{1,0:T(8,128)S(1)}, u32[]{:S(2)}, u32[]{:S(2)}) collective-permute-start(f32[8,2560]{1,0:T(8,128)S(1)} %get-tuple-element.67), channel_id=1, source_target_pairs={{1,2},{2,1},{5,6},{6,5},{9,10},{10,9},{13,14},{14,13},{17,18},{18,... | collective-permute-start | bytes 245768 | tf_op jit(solution)/shard_map/ppermute | solution.py:189
  16.9 10.2 %copy-start.1 = (s32[2]{0:T(128)S(1)}, s32[2]{0:T(128)}, u32[]{:S(2)}) copy-start(s32[2]{0:T(128)} %pad_add_fusion.where) | copy-start | bytes 28
  22.0 3.8 %collective-permute-start.4 = (bf16[64,2048]{1,0:T(8,128)(2,1)S(1)}, bf16[64,2048]{1,0:T(8,128)(2,1)S(1)}, u32[]{:S(2)}, u32[]{:S(2)}) collective-permute-start(bf16[64,2048]{1,0:T(8,128)(2,1)S(1)} %constant_dynamic-update-slice_fusion.refs_0_), channel_id=1, source_target_pairs={{0,4},{4,0},{8,12},{12,8},{16,20},{20,16},{24,28},{28,24},{1,5},{5... | collective-permute-start | bytes 786440 | tf_op jit(solution)/shard_map/ppermute | solution.py:26
  22.1 3.7 %collective-permute-start.8 = (bf16[64,2048]{1,0:T(8,128)(2,1)S(1)}, bf16[64,2048]{1,0:T(8,128)(2,1)S(1)}, u32[]{:S(2)}, u32[]{:S(2)}) collective-permute-start(bf16[64,2048]{1,0:T(8,128)(2,1)S(1)} %collective-permute-done.7.refs_2_), channel_id=1, source_target_pairs={{0,4},{4,0},{8,12},{12,8},{16,20},{20,16},{24,28},{28,24},{1,5},{5... | collective-permute-start | bytes 786440 | tf_op jit(solution)/shard_map/ppermute | solution.py:26
  25.3 1.5 %collective-permute-start.10 = (bf16[64,2048]{1,0:T(8,128)(2,1)S(1)}, bf16[64,2048]{1,0:T(8,128)(2,1)S(1)}, u32[]{:S(2)}, u32[]{:S(2)}) collective-permute-start(bf16[64,2048]{1,0:T(8,128)(2,1)S(1)} %collective-permute-done.9.refs_4_), channel_id=1, source_target_pairs={{0,4},{4,0},{8,12},{12,8},{16,20},{20,16},{24,28},{28,24},{1,5},{5... | collective-permute-start | bytes 786440 | tf_op jit(solution)/shard_map/ppermute | solution.py:26
  25.3 1.9 %collective-permute-start.12 = (bf16[64,2048]{1,0:T(8,128)(2,1)S(1)}, bf16[64,2048]{1,0:T(8,128)(2,1)S(1)}, u32[]{:S(2)}, u32[]{:S(2)}) collective-permute-start(bf16[64,2048]{1,0:T(8,128)(2,1)S(1)} %collective-permute-done.11.refs_6_), channel_id=1, source_target_pairs={{0,4},{4,0},{8,12},{12,8},{16,20},{20,16},{24,28},{28,24},{1,5},{5... | collective-permute-start | bytes 786440 | tf_op jit(solution)/shard_map/ppermute | solution.py:26
  37.7 2.0 %collective-permute-start.13 = (bf16[128,2048]{1,0:T(8,128)(2,1)S(1)}, bf16[128,2048]{1,0:T(8,128)(2,1)S(1)}, u32[]{:S(2)}, u32[]{:S(2)}) collective-permute-start(bf16[128,2048]{1,0:T(8,128)(2,1)S(1)} %solve.1.part), channel_id=1, source_target_pairs={{0,4},{4,0},{8,12},{12,8},{16,20},{20,16},{24,28},{28,24},{1,5},{5... | collective-permute-start | bytes 1572872 | tf_op jit(solution)/shard_map/ppermute | solution.py:26
  40.1 7.3 %collective-permute-start.18 = (bf16[32,2048]{1,0:T(8,128)(2,1)S(1)}, bf16[32,2048]{1,0:T(8,128)(2,1)S(1)}, u32[]{:S(2)}, u32[]{:S(2)}) collective-permute-start(bf16[32,2048]{1,0:T(8,128)(2,1)S(1)} %get-tuple-element.58), channel_id=1, source_target_pairs={{0,24},{4,28},{8,16},{12,20},{16,8},{20,12},{24,0},{28,4},{1,25},{... | collective-permute-start | bytes 393224 | tf_op jit(solution)/shard_map/ppermute | solution.py:26
  41.7 7.8 %collective-permute-start.19 = (bf16[32,2048]{1,0:T(8,128)(2,1)S(1)}, bf16[32,2048]{1,0:T(8,128)(2,1)S(1)}, u32[]{:S(2)}, u32[]{:S(2)}) collective-permute-start(bf16[32,2048]{1,0:T(8,128)(2,1)S(1)} %get-tuple-element.59), channel_id=1, source_target_pairs={{0,16},{4,20},{8,24},{12,28},{16,0},{20,4},{24,8},{28,12},{1,17},{... | collective-permute-start | bytes 393224 | tf_op jit(solution)/shard_map/ppermute | solution.py:26
  42.5 7.8 %collective-permute-start.20 = (bf16[32,2048]{1,0:T(8,128)(2,1)S(1)}, bf16[32,2048]{1,0:T(8,128)(2,1)S(1)}, u32[]{:S(2)}, u32[]{:S(2)}) collective-permute-start(bf16[32,2048]{1,0:T(8,128)(2,1)S(1)} %get-tuple-element.60), channel_id=1, source_target_pairs={{0,8},{4,12},{8,0},{12,4},{16,24},{20,28},{24,16},{28,20},{1,9},{5... | collective-permute-start | bytes 393224 | tf_op jit(solution)/shard_map/ppermute | solution.py:26
  43.7 9.9 %collective-permute-start.14 = (bf16[32,2048]{1,0:T(8,128)(2,1)S(1)}, bf16[32,2048]{1,0:T(8,128)(2,1)S(1)}, u32[]{:S(2)}, u32[]{:S(2)}) collective-permute-start(bf16[32,2048]{1,0:T(8,128)(2,1)S(1)} %get-tuple-element.53), channel_id=1, source_target_pairs={{0,8},{4,12},{8,0},{12,4},{16,24},{20,28},{24,16},{28,20},{1,9},{5... | collective-permute-start | bytes 393224 | tf_op jit(solution)/shard_map/ppermute | solution.py:26
  44.5 9.1 %collective-permute-start.15 = (bf16[32,2048]{1,0:T(8,128)(2,1)S(1)}, bf16[32,2048]{1,0:T(8,128)(2,1)S(1)}, u32[]{:S(2)}, u32[]{:S(2)}) collective-permute-start(bf16[32,2048]{1,0:T(8,128)(2,1)S(1)} %get-tuple-element.54), channel_id=1, source_target_pairs={{0,16},{4,20},{8,24},{12,28},{16,0},{20,4},{24,8},{28,12},{1,17},{... | collective-permute-start | bytes 393224 | tf_op jit(solution)/shard_map/ppermute | solution.py:26
  47.5 7.6 %collective-permute-start.16 = (bf16[32,2048]{1,0:T(8,128)(2,1)S(1)}, bf16[32,2048]{1,0:T(8,128)(2,1)S(1)}, u32[]{:S(2)}, u32[]{:S(2)}) collective-permute-start(bf16[32,2048]{1,0:T(8,128)(2,1)S(1)} %get-tuple-element.55), channel_id=1, source_target_pairs={{0,24},{4,28},{8,16},{12,20},{16,8},{20,12},{24,0},{28,4},{1,25},{... | collective-permute-start | bytes 393224 | tf_op jit(solution)/shard_map/ppermute | solution.py:26
  50.4 6.5 %collective-permute-start.22 = (bf16[16,2048]{1,0:T(8,128)(2,1)S(1)}, bf16[16,2048]{1,0:T(8,128)(2,1)S(1)}, u32[]{:S(2)}, u32[]{:S(2)}) collective-permute-start(bf16[16,2048]{1,0:T(8,128)(2,1)S(1)} %get-tuple-element.62), channel_id=1, source_target_pairs={{0,3},{1,2},{2,1},{3,0},{4,7},{5,6},{6,5},{7,4},{8,11},{9,10},{10,... | collective-permute-start | bytes 196616 | tf_op jit(solution)/shard_map/ppermute | solution.py:26
  53.5 5.9 %collective-permute-start.21 = (bf16[16,2048]{1,0:T(8,128)(2,1)S(1)}, bf16[16,2048]{1,0:T(8,128)(2,1)S(1)}, u32[]{:S(2)}, u32[]{:S(2)}) collective-permute-start(bf16[16,2048]{1,0:T(8,128)(2,1)S(1)} %get-tuple-element.61), channel_id=1, source_target_pairs={{0,2},{1,3},{2,0},{3,1},{4,6},{5,7},{6,4},{7,5},{8,10},{9,11},{10,... | collective-permute-start | bytes 196616 | tf_op jit(solution)/shard_map/ppermute | solution.py:26
  55.1 4.9 %collective-permute-start.17 = (bf16[16,2048]{1,0:T(8,128)(2,1)S(1)}, bf16[16,2048]{1,0:T(8,128)(2,1)S(1)}, u32[]{:S(2)}, u32[]{:S(2)}) collective-permute-start(bf16[16,2048]{1,0:T(8,128)(2,1)S(1)} %get-tuple-element.57), channel_id=1, source_target_pairs={{0,1},{1,0},{2,3},{3,2},{4,5},{5,4},{6,7},{7,6},{8,9},{9,8},{10,11... | collective-permute-start | bytes 196616 | tf_op jit(solution)/shard_map/ppermute | solution.py:26

commit v6 on v5

--- a/solution.py
+++ b/solution.py
@@ -13,7 +13,7 @@
 Z_ORDER = (1, 2, 3)
 XY_ORDER = (3, 2, 1)
 XYB_ORDER = (3, 2, 1)
-ZB_ORDER = (1, 2, 3)
+ZB_ORDER = (1, 3, 2)
 XYB2_ORDER = (1, 2, 3)
 TILE = 256
 MIB = 1 << 20

time: 61 us -> 60.6 us (level)
  waiting for transfers between devices: 16.6 us -> 15.3 us
  starting transfers between devices: 23.3 us -> 24.2 us
    ppermute x21, waiting for transfers between devices: 16.6 us -> 15.3 us  [xor_permute(): return lax.ppermute(value, axis, [(i, i ^ mask) for i in range(size)])]
    ppermute x21, starting transfers between devices: 22.5 us -> 23.4 us  [xor_permute(): return lax.ppermute(value, axis, [(i, i ^ mask) for i in range(size)])]
  transfers between devices with their start and end apart: 23 -> 23, of which waited for: 12 -> 13; matrix products, arithmetic and copies ran while one was open for 5% -> 5% of each run, Pallas kernels for 9% -> 9%
where the time goes in v6:
time: 60.6 us; the launch traced here: 60.3 us
  starting transfers between devices  24.2 us (40%)
  Pallas kernels  16.1 us (27%)
  waiting for transfers between devices  15.3 us (25%)
  other arithmetic  2.1 us (3%)
  local copies, waits for them, and re-layouts  1.78 us (3%)
  between operations  0.85 us (1%)
    ppermute x21, starting transfers between devices, xor_permute(): return lax.ppermute(value, axis, [(i, i ^ mask) for i in range(size)])  23.4 us
    ppermute x21, waiting for transfers between devices, xor_permute(): return lax.ppermute(value, axis, [(i, i ^ mask) for i in range(size)])  15.3 us
    pallas_call x1, Pallas kernels, shards(): pl.pallas_call(functools.partial(solve_kernel, len(blocks), n_slab), out_...  10.5 us
    pallas_call x1, Pallas kernels, stage(): pl.pallas_call(functools.partial(stage_kernel, order, n_freq, n_slab, til...  5.06 us
  transfers between devices with their start and end apart: 23, of which 13 were waited for; matrix products, arithmetic and copies ran while one was open for 5% of the time, Pallas kernels for 9%

profile of v6, /device:TPU:0, one launch (start us, length us, event | category | flops | bytes accessed | tf_op | source)
XLA Modules:
  0.0 60.3 jit_solution(5628247022427497959)
XLA Ops:
  0.0 0.0 copy-start
  0.0 3.0 %collective-permute-start = (bf16[16,2048]{1,0:T(8,128)(2,1)}, bf16[16,2048]{1,0:T(8,128)(2,1)S(1)}, u32[]{:S(2)}, u32[]{:S(2)}) collective-permute-start(bf16[16,2048]{1,0:T(8,128)(2,1)} %param.6), channel_id=1, source_target_pairs={{0,1},{1,0},{2,3},{3,2},{4,5},{5,4},{6,7},{7,6},{8,9},{9,8},{10,11... | collective-permute-start | bytes 196616 | tf_op jit(solution)/shard_map/ppermute | solution.py:26
  3.0 2.6 %collective-permute-start.1 = (bf16[16,2048]{1,0:T(8,128)(2,1)}, bf16[16,2048]{1,0:T(8,128)(2,1)S(1)}, u32[]{:S(2)}, u32[]{:S(2)}) collective-permute-start(bf16[16,2048]{1,0:T(8,128)(2,1)} %param.6), channel_id=1, source_target_pairs={{0,2},{1,3},{2,0},{3,1},{4,6},{5,7},{6,4},{7,5},{8,10},{9,11},{10,... | collective-permute-start | bytes 196616 | tf_op jit(solution)/shard_map/ppermute | solution.py:26
  5.6 0.0 collective-permute-start.2
  5.6 0.0 collective-permute-start.3
  5.6 0.7 %bitcast_convert_fusion = (f32[8,512]{1,0:T(8,128)S(1)}, f32[8,512]{1,0:T(8,128)S(1)}) fusion(bf16[1,128,512]{2,1,0:T(8,128)(2,1)} %param.7), kind=kLoop, calls=%fused_computation.13 | loop fusion | flops 8192 | bytes 49152 | tf_op jit(solution)/shard_map/convert_element_type | solution.py:179
  6.3 0.9 %slice_bitcast_fusion = (f32[8,2048]{1,0:T(8,128)S(1)}, f32[8,2048]{1,0:T(8,128)S(1)}) fusion(f32[1,128,2048]{2,1,0:T(8,128)} %param.10), kind=kLoop, calls=%fused_computation.3 | loop fusion | bytes 262144 | tf_op jit(solution)/shard_map/slice | solution.py:179
  7.2 0.8 %constant_dynamic-update-slice_fusion.3 = bf16[64,2048]{1,0:T(8,128)(2,1)S(1)} fusion(bf16[16,2048]{1,0:T(8,128)(2,1)} %param.6), kind=kLoop, calls=%fused_computation.12 | loop fusion | bytes 131072
  8.7 0.0 collective-permute-done
  8.8 1.8 %collective-permute-done.1 = bf16[16,2048]{1,0:T(8,128)(2,1)S(1)} collective-permute-done((bf16[16,2048]{1,0:T(8,128)(2,1)}, bf16[16,2048]{1,0:T(8,128)(2,1)S(1)}, u32[]{:S(2)}, u32[]{:S(2)}) %collective-permute-start.1) | collective-permute-done | bytes 65568 | tf_op jit(solution)/shard_map/ppermute | solution.py:26
  10.5 1.4 %collective-permute-done.2 = bf16[16,2048]{1,0:T(8,128)(2,1)S(1)} collective-permute-done((bf16[16,2048]{1,0:T(8,128)(2,1)}, bf16[16,2048]{1,0:T(8,128)(2,1)S(1)}, u32[]{:S(2)}, u32[]{:S(2)}) %collective-permute-start.2) | collective-permute-done | bytes 65568 | tf_op jit(solution)/shard_map/ppermute | solution.py:26
  11.9 0.0 collective-permute-done.3.oper_other
  11.9 0.0 copy-start.2
  12.0 1.6 %collective-permute-start.7 = (bf16[64,2048]{1,0:T(8,128)(2,1)S(1)}, bf16[64,2048]{1,0:T(8,128)(2,1)S(1)}, u32[]{:S(2)}, u32[]{:S(2)}) collective-permute-start(bf16[64,2048]{1,0:T(8,128)(2,1)S(1)} %constant_dynamic-update-slice_fusion.refs_0_), channel_id=1, source_target_pairs={{0,8},{4,12},{8,0},{12,4},{16,24},{20,28},{24,16},{28,20},{1,9},{5... | collective-permute-start | bytes 786440 | tf_op jit(solution)/shard_map/ppermute | solution.py:26
  13.5 1.5 %collective-permute-start.9 = (bf16[64,2048]{1,0:T(8,128)(2,1)S(1)}, bf16[64,2048]{1,0:T(8,128)(2,1)S(1)}, u32[]{:S(2)}, u32[]{:S(2)}) collective-permute-start(bf16[64,2048]{1,0:T(8,128)(2,1)S(1)} %constant_dynamic-update-slice_fusion.refs_0_), channel_id=1, source_target_pairs={{0,16},{4,20},{8,24},{12,28},{16,0},{20,4},{24,8},{28,12},{1,17},{... | collective-permute-start | bytes 786440 | tf_op jit(solution)/shard_map/ppermute | solution.py:26
  15.0 0.5 collective-permute-start.11
  15.5 0.1 collective-permute-start.5
  15.6 0.7 %collective-permute-start.6 = (f32[8,2560]{1,0:T(8,128)S(1)}, f32[8,2560]{1,0:T(8,128)S(1)}, u32[]{:S(2)}, u32[]{:S(2)}) collective-permute-start(f32[8,2560]{1,0:T(8,128)S(1)} %get-tuple-element.67), channel_id=1, source_target_pairs={{1,2},{2,1},{5,6},{6,5},{9,10},{10,9},{13,14},{14,13},{17,18},{18,... | collective-permute-start | bytes 245768 | tf_op jit(solution)/shard_map/ppermute | solution.py:189
  16.3 0.7 %pad_add_fusion.where = s32[2]{0:T(128)} fusion(s32[1]{0:T(128)} %bitcast.1, s32[1]{0:T(128)} %bitcast), kind=kLoop, calls=%fused_computation.15 | loop fusion | flops 2 | bytes 16 | tf_op jit(solution)/shard_map/stack | solution.py:173
  16.9 0.0 copy-done.2
  16.9 0.0 copy-start.1
  16.9 5.1 %stage.1 = (bf16[2048,2048]{1,0:T(8,128)(2,1)S(1)}, f32[128,2048]{1,0:T(8,128)S(1)}, f32[128,2048]{1,0:T(8,128)S(1)}, bf16[512,512]{1,0:T(8,128)(2,1)S(1)}, bf16[256,256]{1,0:T(8,128)(2,1)S(1)}) custom-call(s32[2]{0:T(128)} %pad_add_fusion.where, bf16[128,512]{1,0:T(8,128)(2,1)} %bitcast.16, bf16[128,512]{1,0:T(8,128)(2,1)} %copy-done.2, ...), custom_call_target="tpu_custom_call" | custom-call | bytes 22282240 | tf_op jit(solution)/shard_map/stage/pallas_call | solution.py:117
  22.0 0.0 collective-permute-done.5
  22.0 0.1 collective-permute-start.4
  22.1 0.0 collective-permute-done.6
  22.1 0.0 collective-permute-done.7.refs_2_
  22.1 0.5 collective-permute-start.8
  22.6 2.7 %collective-permute-done.9.refs_4_ = bf16[64,2048]{1,0:T(8,128)(2,1)S(1)} collective-permute-done((bf16[64,2048]{1,0:T(8,128)(2,1)S(1)}, bf16[64,2048]{1,0:T(8,128)(2,1)S(1)}, u32[]{:S(2)}, u32[]{:S(2)}) %collective-permute-start.9) | collective-permute-done | bytes 262176 | tf_op jit(solution)/shard_map/ppermute | solution.py:26
  25.3 0.0 collective-permute-start.10
  25.3 0.0 collective-permute-done.11.refs_6_
  25.3 0.5 collective-permute-start.12
  25.9 0.0 collective-permute-done.4.refs_1_
  25.9 0.0 collective-permute-done.8.refs_3_
  25.9 0.9 %collective-permute-done.10.refs_5_ = bf16[64,2048]{1,0:T(8,128)(2,1)S(1)} collective-permute-done((bf16[64,2048]{1,0:T(8,128)(2,1)S(1)}, bf16[64,2048]{1,0:T(8,128)(2,1)S(1)}, u32[]{:S(2)}, u32[]{:S(2)}) %collective-permute-start.10) | collective-permute-done | bytes 262176 | tf_op jit(solution)/shard_map/ppermute | solution.py:26
  26.8 0.4 collective-permute-done.12.refs_7_
  27.2 0.0 copy-done
  27.2 0.0 copy-done.1
  27.2 10.5 %solve.1.part = bf16[128,2048]{1,0:T(8,128)(2,1)S(1)} custom-call(s32[2]{0:T(128)S(1)} %copy-done.1, f32[1]{0:T(128)S(6)} %copy.10.factor, bf16[64,2048]{1,0:T(8,128)(2,1)S(1)} %constant_dynamic-update-slice_fusion.refs_0_, bf16[64,2048]{1,0:T(8,128)(2,1)S(1)} %collective-permute-done.4.refs_1_, bf16[64,2048]{1,0:T(8,128)(2,1)S(1)} %collective-permute-done.7.refs_2_, ...), custom_call_target="tpu_custom_call" | custom-call | flops 8455716864 | bytes 8388608 | tf_op jit(solution)/shard_map/solve/pallas_call | solution.py:202
  37.7 0.2 collective-permute-start.13
  37.9 1.8 %collective-permute-done.13.part_other = bf16[128,2048]{1,0:T(8,128)(2,1)S(1)} collective-permute-done((bf16[128,2048]{1,0:T(8,128)(2,1)S(1)}, bf16[128,2048]{1,0:T(8,128)(2,1)S(1)}, u32[]{:S(2)}, u32[]{:S(2)}) %collective-permute-start.13) | collective-permute-done | bytes 524320 | tf_op jit(solution)/shard_map/ppermute | solution.py:26
  39.7 0.4 back.1
  40.1 1.6 %collective-permute-start.18 = (bf16[32,2048]{1,0:T(8,128)(2,1)S(1)}, bf16[32,2048]{1,0:T(8,128)(2,1)S(1)}, u32[]{:S(2)}, u32[]{:S(2)}) collective-permute-start(bf16[32,2048]{1,0:T(8,128)(2,1)S(1)} %get-tuple-element.58), channel_id=1, source_target_pairs={{0,24},{4,28},{8,16},{12,20},{16,8},{20,12},{24,0},{28,4},{1,25},{... | collective-permute-start | bytes 393224 | tf_op jit(solution)/shard_map/ppermute | solution.py:26
  41.7 0.8 %collective-permute-start.19 = (bf16[32,2048]{1,0:T(8,128)(2,1)S(1)}, bf16[32,2048]{1,0:T(8,128)(2,1)S(1)}, u32[]{:S(2)}, u32[]{:S(2)}) collective-permute-start(bf16[32,2048]{1,0:T(8,128)(2,1)S(1)} %get-tuple-element.59), channel_id=1, source_target_pairs={{0,16},{4,20},{8,24},{12,28},{16,0},{20,4},{24,8},{28,12},{1,17},{... | collective-permute-start | bytes 393224 | tf_op jit(solution)/shard_map/ppermute | solution.py:26
  42.5 1.2 %collective-permute-start.20 = (bf16[32,2048]{1,0:T(8,128)(2,1)S(1)}, bf16[32,2048]{1,0:T(8,128)(2,1)S(1)}, u32[]{:S(2)}, u32[]{:S(2)}) collective-permute-start(bf16[32,2048]{1,0:T(8,128)(2,1)S(1)} %get-tuple-element.60), channel_id=1, source_target_pairs={{0,8},{4,12},{8,0},{12,4},{16,24},{20,28},{24,16},{28,20},{1,9},{5... | collective-permute-start | bytes 393224 | tf_op jit(solution)/shard_map/ppermute | solution.py:26
  43.7 0.9 %collective-permute-start.14 = (bf16[32,2048]{1,0:T(8,128)(2,1)S(1)}, bf16[32,2048]{1,0:T(8,128)(2,1)S(1)}, u32[]{:S(2)}, u32[]{:S(2)}) collective-permute-start(bf16[32,2048]{1,0:T(8,128)(2,1)S(1)} %get-tuple-element.53), channel_id=1, source_target_pairs={{0,8},{4,12},{8,0},{12,4},{16,24},{20,28},{24,16},{28,20},{1,9},{5... | collective-permute-start | bytes 393224 | tf_op jit(solution)/shard_map/ppermute | solution.py:26
  44.5 1.2 %collective-permute-start.15 = (bf16[32,2048]{1,0:T(8,128)(2,1)S(1)}, bf16[32,2048]{1,0:T(8,128)(2,1)S(1)}, u32[]{:S(2)}, u32[]{:S(2)}) collective-permute-start(bf16[32,2048]{1,0:T(8,128)(2,1)S(1)} %get-tuple-element.54), channel_id=1, source_target_pairs={{0,16},{4,20},{8,24},{12,28},{16,0},{20,4},{24,8},{28,12},{1,17},{... | collective-permute-start | bytes 393224 | tf_op jit(solution)/shard_map/ppermute | solution.py:26
  45.8 1.7 %collective-permute-done.18.refs_0_ = bf16[32,2048]{1,0:T(8,128)(2,1)S(1)} collective-permute-done((bf16[32,2048]{1,0:T(8,128)(2,1)S(1)}, bf16[32,2048]{1,0:T(8,128)(2,1)S(1)}, u32[]{:S(2)}, u32[]{:S(2)}) %collective-permute-start.18) | collective-permute-done | bytes 131104 | tf_op jit(solution)/shard_map/ppermute | solution.py:26
  47.5 1.5 %collective-permute-start.16 = (bf16[32,2048]{1,0:T(8,128)(2,1)S(1)}, bf16[32,2048]{1,0:T(8,128)(2,1)S(1)}, u32[]{:S(2)}, u32[]{:S(2)}) collective-permute-start(bf16[32,2048]{1,0:T(8,128)(2,1)S(1)} %get-tuple-element.55), channel_id=1, source_target_pairs={{0,24},{4,28},{8,16},{12,20},{16,8},{20,12},{24,0},{28,4},{1,25},{... | collective-permute-start | bytes 393224 | tf_op jit(solution)/shard_map/ppermute | solution.py:26
  49.0 0.6 collective-permute-done.19.refs_1_
  49.5 0.8 %collective-permute-done.20.refs_2_ = bf16[32,2048]{1,0:T(8,128)(2,1)S(1)} collective-permute-done((bf16[32,2048]{1,0:T(8,128)(2,1)S(1)}, bf16[32,2048]{1,0:T(8,128)(2,1)S(1)}, u32[]{:S(2)}, u32[]{:S(2)}) %collective-permute-start.20) | collective-permute-done | bytes 131104 | tf_op jit(solution)/shard_map/ppermute | solution.py:26
  50.3 0.1 plane.3
  50.4 2.3 %collective-permute-start.22 = (bf16[16,2048]{1,0:T(8,128)(2,1)S(1)}, bf16[16,2048]{1,0:T(8,128)(2,1)S(1)}, u32[]{:S(2)}, u32[]{:S(2)}) collective-permute-start(bf16[16,2048]{1,0:T(8,128)(2,1)S(1)} %get-tuple-element.62), channel_id=1, source_target_pairs={{0,2},{1,3},{2,0},{3,1},{4,6},{5,7},{6,4},{7,5},{8,10},{9,11},{10,... | collective-permute-start | bytes 196616 | tf_op jit(solution)/shard_map/ppermute | solution.py:26
  52.7 1.8 %collective-permute-start.21 = (bf16[16,2048]{1,0:T(8,128)(2,1)S(1)}, bf16[16,2048]{1,0:T(8,128)(2,1)S(1)}, u32[]{:S(2)}, u32[]{:S(2)}) collective-permute-start(bf16[16,2048]{1,0:T(8,128)(2,1)S(1)} %get-tuple-element.61), channel_id=1, source_target_pairs={{0,3},{1,2},{2,1},{3,0},{4,7},{5,6},{6,5},{7,4},{8,11},{9,10},{10,... | collective-permute-start | bytes 196616 | tf_op jit(solution)/shard_map/ppermute | solution.py:26
  54.5 0.0 collective-permute-done.14.refs_0_
  54.5 0.0 collective-permute-done.15.refs_1_
  54.5 0.6 collective-permute-done.16.refs_2_
  55.1 0.1 plane.2
  55.1 1.7 %collective-permute-start.17 = (bf16[16,2048]{1,0:T(8,128)(2,1)S(1)}, bf16[16,2048]{1,0:T(8,128)(2,1)S(1)}, u32[]{:S(2)}, u32[]{:S(2)}) collective-permute-start(bf16[16,2048]{1,0:T(8,128)(2,1)S(1)} %get-tuple-element.57), channel_id=1, source_target_pairs={{0,1},{1,0},{2,3},{3,2},{4,5},{5,4},{6,7},{7,6},{8,9},{9,8},{10,11... | collective-permute-start | bytes 196616 | tf_op jit(solution)/shard_map/ppermute | solution.py:26
  56.9 0.9 %collective-permute-done.22 = bf16[16,2048]{1,0:T(8,128)(2,1)S(1)} collective-permute-done((bf16[16,2048]{1,0:T(8,128)(2,1)S(1)}, bf16[16,2048]{1,0:T(8,128)(2,1)S(1)}, u32[]{:S(2)}, u32[]{:S(2)}) %collective-permute-start.22) | collective-permute-done | bytes 65568 | tf_op jit(solution)/shard_map/ppermute | solution.py:26
  57.8 1.3 %collective-permute-done.21 = bf16[16,2048]{1,0:T(8,128)(2,1)S(1)} collective-permute-done((bf16[16,2048]{1,0:T(8,128)(2,1)S(1)}, bf16[16,2048]{1,0:T(8,128)(2,1)S(1)}, u32[]{:S(2)}, u32[]{:S(2)}) %collective-permute-start.21) | collective-permute-done | bytes 65568 | tf_op jit(solution)/shard_map/ppermute | solution.py:26
  59.1 0.5 collective-permute-done.17
  59.7 0.7 %convert_add_fusion = f32[16,2048]{1,0:T(8,128)} fusion(bf16[16,2048]{1,0:T(8,128)(2,1)S(1)} %collective-permute-done.22, bf16[16,2048]{1,0:T(8,128)(2,1)S(1)} %collective-permute-done.21, f32[16,2048]{1,0:T(8,128)S(1)} %get-tuple-element.56, bf16[16,2048]{1,0:T(8,128)(2,1)S(1)} %collective-permute-done.17), kind=kLoop, calls=%fused_computation | loop fusion | flops 196608 | bytes 458752 | tf_op jit(solution)/shard_map/add | solution.py:228
  (10 shorter events, 0.1 us)
Async XLA Ops:
  0.0 27.2 %copy-start = (bf16[1,128,512]{2,1,0:T(8,128)(2,1)S(1)}, bf16[1,128,512]{2,1,0:T(8,128)(2,1)}, u32[]{:S(2)}) copy-start(bf16[1,128,512]{2,1,0:T(8,128)(2,1)} %param.7) | copy-start | bytes 393220
  0.0 8.7 %collective-permute-start = (bf16[16,2048]{1,0:T(8,128)(2,1)}, bf16[16,2048]{1,0:T(8,128)(2,1)S(1)}, u32[]{:S(2)}, u32[]{:S(2)}) collective-permute-start(bf16[16,2048]{1,0:T(8,128)(2,1)} %param.6), channel_id=1, source_target_pairs={{0,1},{1,0},{2,3},{3,2},{4,5},{5,4},{6,7},{7,6},{8,9},{9,8},{10,11... | collective-permute-start | bytes 196616 | tf_op jit(solution)/shard_map/ppermute | solution.py:26
  3.0 7.5 %collective-permute-start.1 = (bf16[16,2048]{1,0:T(8,128)(2,1)}, bf16[16,2048]{1,0:T(8,128)(2,1)S(1)}, u32[]{:S(2)}, u32[]{:S(2)}) collective-permute-start(bf16[16,2048]{1,0:T(8,128)(2,1)} %param.6), channel_id=1, source_target_pairs={{0,2},{1,3},{2,0},{3,1},{4,6},{5,7},{6,4},{7,5},{8,10},{9,11},{10,... | collective-permute-start | bytes 196616 | tf_op jit(solution)/shard_map/ppermute | solution.py:26
  5.6 6.3 %collective-permute-start.2 = (bf16[16,2048]{1,0:T(8,128)(2,1)}, bf16[16,2048]{1,0:T(8,128)(2,1)S(1)}, u32[]{:S(2)}, u32[]{:S(2)}) collective-permute-start(bf16[16,2048]{1,0:T(8,128)(2,1)} %param.6), channel_id=1, source_target_pairs={{0,3},{1,2},{2,1},{3,0},{4,7},{5,6},{6,5},{7,4},{8,11},{9,10},{10,... | collective-permute-start | bytes 196616 | tf_op jit(solution)/shard_map/ppermute | solution.py:26
  5.6 6.3 %collective-permute-start.3 = (bf16[128,512]{1,0:T(8,128)(2,1)}, bf16[128,512]{1,0:T(8,128)(2,1)S(1)}, u32[]{:S(2)}, u32[]{:S(2)}) collective-permute-start(bf16[128,512]{1,0:T(8,128)(2,1)} %bitcast.15), channel_id=1, source_target_pairs={{0,4},{4,0},{8,12},{12,8},{16,20},{20,16},{24,28},{28,24},{1,5},{5... | collective-permute-start | bytes 393224 | tf_op jit(solution)/shard_map/ppermute | solution.py:26
  11.9 5.0 %copy-start.2 = (bf16[128,512]{1,0:T(8,128)(2,1)}, bf16[128,512]{1,0:T(8,128)(2,1)S(1)}, u32[]{:S(2)}) copy-start(bf16[128,512]{1,0:T(8,128)(2,1)S(1)} %collective-permute-done.3.oper_other) | copy-start | bytes 393220
  12.0 10.2 %collective-permute-start.7 = (bf16[64,2048]{1,0:T(8,128)(2,1)S(1)}, bf16[64,2048]{1,0:T(8,128)(2,1)S(1)}, u32[]{:S(2)}, u32[]{:S(2)}) collective-permute-start(bf16[64,2048]{1,0:T(8,128)(2,1)S(1)} %constant_dynamic-update-slice_fusion.refs_0_), channel_id=1, source_target_pairs={{0,8},{4,12},{8,0},{12,4},{16,24},{20,28},{24,16},{28,20},{1,9},{5... | collective-permute-start | bytes 786440 | tf_op jit(solution)/shard_map/ppermute | solution.py:26
  13.5 11.7 %collective-permute-start.9 = (bf16[64,2048]{1,0:T(8,128)(2,1)S(1)}, bf16[64,2048]{1,0:T(8,128)(2,1)S(1)}, u32[]{:S(2)}, u32[]{:S(2)}) collective-permute-start(bf16[64,2048]{1,0:T(8,128)(2,1)S(1)} %constant_dynamic-update-slice_fusion.refs_0_), channel_id=1, source_target_pairs={{0,16},{4,20},{8,24},{12,28},{16,0},{20,4},{24,8},{28,12},{1,17},{... | collective-permute-start | bytes 786440 | tf_op jit(solution)/shard_map/ppermute | solution.py:26
  15.0 10.2 %collective-permute-start.11 = (bf16[64,2048]{1,0:T(8,128)(2,1)S(1)}, bf16[64,2048]{1,0:T(8,128)(2,1)S(1)}, u32[]{:S(2)}, u32[]{:S(2)}) collective-permute-start(bf16[64,2048]{1,0:T(8,128)(2,1)S(1)} %constant_dynamic-update-slice_fusion.refs_0_), channel_id=1, source_target_pairs={{0,24},{4,28},{8,16},{12,20},{16,8},{20,12},{24,0},{28,4},{1,25},{... | collective-permute-start | bytes 786440 | tf_op jit(solution)/shard_map/ppermute | solution.py:26
  15.5 6.5 %collective-permute-start.5 = (f32[8,2560]{1,0:T(8,128)S(1)}, f32[8,2560]{1,0:T(8,128)S(1)}, u32[]{:S(2)}, u32[]{:S(2)}) collective-permute-start(f32[8,2560]{1,0:T(8,128)S(1)} %get-tuple-element.68), channel_id=1, source_target_pairs={{0,1},{1,0},{2,3},{3,2},{4,5},{5,4},{6,7},{7,6},{8,9},{9,8},{10,11... | collective-permute-start | bytes 245768 | tf_op jit(solution)/shard_map/ppermute | solution.py:190
  15.6 6.5 %collective-permute-start.6 = (f32[8,2560]{1,0:T(8,128)S(1)}, f32[8,2560]{1,0:T(8,128)S(1)}, u32[]{:S(2)}, u32[]{:S(2)}) collective-permute-start(f32[8,2560]{1,0:T(8,128)S(1)} %get-tuple-element.67), channel_id=1, source_target_pairs={{1,2},{2,1},{5,6},{6,5},{9,10},{10,9},{13,14},{14,13},{17,18},{18,... | collective-permute-start | bytes 245768 | tf_op jit(solution)/shard_map/ppermute | solution.py:189
  16.9 10.2 %copy-start.1 = (s32[2]{0:T(128)S(1)}, s32[2]{0:T(128)}, u32[]{:S(2)}) copy-start(s32[2]{0:T(128)} %pad_add_fusion.where) | copy-start | bytes 28
  22.0 3.8 %collective-permute-start.4 = (bf16[64,2048]{1,0:T(8,128)(2,1)S(1)}, bf16[64,2048]{1,0:T(8,128)(2,1)S(1)}, u32[]{:S(2)}, u32[]{:S(2)}) collective-permute-start(bf16[64,2048]{1,0:T(8,128)(2,1)S(1)} %constant_dynamic-update-slice_fusion.refs_0_), channel_id=1, source_target_pairs={{0,4},{4,0},{8,12},{12,8},{16,20},{20,16},{24,28},{28,24},{1,5},{5... | collective-permute-start | bytes 786440 | tf_op jit(solution)/shard_map/ppermute | solution.py:26
  22.1 3.7 %collective-permute-start.8 = (bf16[64,2048]{1,0:T(8,128)(2,1)S(1)}, bf16[64,2048]{1,0:T(8,128)(2,1)S(1)}, u32[]{:S(2)}, u32[]{:S(2)}) collective-permute-start(bf16[64,2048]{1,0:T(8,128)(2,1)S(1)} %collective-permute-done.7.refs_2_), channel_id=1, source_target_pairs={{0,4},{4,0},{8,12},{12,8},{16,20},{20,16},{24,28},{28,24},{1,5},{5... | collective-permute-start | bytes 786440 | tf_op jit(solution)/shard_map/ppermute | solution.py:26
  25.3 1.5 %collective-permute-start.10 = (bf16[64,2048]{1,0:T(8,128)(2,1)S(1)}, bf16[64,2048]{1,0:T(8,128)(2,1)S(1)}, u32[]{:S(2)}, u32[]{:S(2)}) collective-permute-start(bf16[64,2048]{1,0:T(8,128)(2,1)S(1)} %collective-permute-done.9.refs_4_), channel_id=1, source_target_pairs={{0,4},{4,0},{8,12},{12,8},{16,20},{20,16},{24,28},{28,24},{1,5},{5... | collective-permute-start | bytes 786440 | tf_op jit(solution)/shard_map/ppermute | solution.py:26
  25.3 1.9 %collective-permute-start.12 = (bf16[64,2048]{1,0:T(8,128)(2,1)S(1)}, bf16[64,2048]{1,0:T(8,128)(2,1)S(1)}, u32[]{:S(2)}, u32[]{:S(2)}) collective-permute-start(bf16[64,2048]{1,0:T(8,128)(2,1)S(1)} %collective-permute-done.11.refs_6_), channel_id=1, source_target_pairs={{0,4},{4,0},{8,12},{12,8},{16,20},{20,16},{24,28},{28,24},{1,5},{5... | collective-permute-start | bytes 786440 | tf_op jit(solution)/shard_map/ppermute | solution.py:26
  37.7 2.0 %collective-permute-start.13 = (bf16[128,2048]{1,0:T(8,128)(2,1)S(1)}, bf16[128,2048]{1,0:T(8,128)(2,1)S(1)}, u32[]{:S(2)}, u32[]{:S(2)}) collective-permute-start(bf16[128,2048]{1,0:T(8,128)(2,1)S(1)} %solve.1.part), channel_id=1, source_target_pairs={{0,4},{4,0},{8,12},{12,8},{16,20},{20,16},{24,28},{28,24},{1,5},{5... | collective-permute-start | bytes 1572872 | tf_op jit(solution)/shard_map/ppermute | solution.py:26
  40.1 7.3 %collective-permute-start.18 = (bf16[32,2048]{1,0:T(8,128)(2,1)S(1)}, bf16[32,2048]{1,0:T(8,128)(2,1)S(1)}, u32[]{:S(2)}, u32[]{:S(2)}) collective-permute-start(bf16[32,2048]{1,0:T(8,128)(2,1)S(1)} %get-tuple-element.58), channel_id=1, source_target_pairs={{0,24},{4,28},{8,16},{12,20},{16,8},{20,12},{24,0},{28,4},{1,25},{... | collective-permute-start | bytes 393224 | tf_op jit(solution)/shard_map/ppermute | solution.py:26
  41.7 7.8 %collective-permute-start.19 = (bf16[32,2048]{1,0:T(8,128)(2,1)S(1)}, bf16[32,2048]{1,0:T(8,128)(2,1)S(1)}, u32[]{:S(2)}, u32[]{:S(2)}) collective-permute-start(bf16[32,2048]{1,0:T(8,128)(2,1)S(1)} %get-tuple-element.59), channel_id=1, source_target_pairs={{0,16},{4,20},{8,24},{12,28},{16,0},{20,4},{24,8},{28,12},{1,17},{... | collective-permute-start | bytes 393224 | tf_op jit(solution)/shard_map/ppermute | solution.py:26
  42.5 7.8 %collective-permute-start.20 = (bf16[32,2048]{1,0:T(8,128)(2,1)S(1)}, bf16[32,2048]{1,0:T(8,128)(2,1)S(1)}, u32[]{:S(2)}, u32[]{:S(2)}) collective-permute-start(bf16[32,2048]{1,0:T(8,128)(2,1)S(1)} %get-tuple-element.60), channel_id=1, source_target_pairs={{0,8},{4,12},{8,0},{12,4},{16,24},{20,28},{24,16},{28,20},{1,9},{5... | collective-permute-start | bytes 393224 | tf_op jit(solution)/shard_map/ppermute | solution.py:26
  43.7 10.8 %collective-permute-start.14 = (bf16[32,2048]{1,0:T(8,128)(2,1)S(1)}, bf16[32,2048]{1,0:T(8,128)(2,1)S(1)}, u32[]{:S(2)}, u32[]{:S(2)}) collective-permute-start(bf16[32,2048]{1,0:T(8,128)(2,1)S(1)} %get-tuple-element.53), channel_id=1, source_target_pairs={{0,8},{4,12},{8,0},{12,4},{16,24},{20,28},{24,16},{28,20},{1,9},{5... | collective-permute-start | bytes 393224 | tf_op jit(solution)/shard_map/ppermute | solution.py:26
  44.5 10.0 %collective-permute-start.15 = (bf16[32,2048]{1,0:T(8,128)(2,1)S(1)}, bf16[32,2048]{1,0:T(8,128)(2,1)S(1)}, u32[]{:S(2)}, u32[]{:S(2)}) collective-permute-start(bf16[32,2048]{1,0:T(8,128)(2,1)S(1)} %get-tuple-element.54), channel_id=1, source_target_pairs={{0,16},{4,20},{8,24},{12,28},{16,0},{20,4},{24,8},{28,12},{1,17},{... | collective-permute-start | bytes 393224 | tf_op jit(solution)/shard_map/ppermute | solution.py:26
  47.5 7.6 %collective-permute-start.16 = (bf16[32,2048]{1,0:T(8,128)(2,1)S(1)}, bf16[32,2048]{1,0:T(8,128)(2,1)S(1)}, u32[]{:S(2)}, u32[]{:S(2)}) collective-permute-start(bf16[32,2048]{1,0:T(8,128)(2,1)S(1)} %get-tuple-element.55), channel_id=1, source_target_pairs={{0,24},{4,28},{8,16},{12,20},{16,8},{20,12},{24,0},{28,4},{1,25},{... | collective-permute-start | bytes 393224 | tf_op jit(solution)/shard_map/ppermute | solution.py:26
  50.4 7.4 %collective-permute-start.22 = (bf16[16,2048]{1,0:T(8,128)(2,1)S(1)}, bf16[16,2048]{1,0:T(8,128)(2,1)S(1)}, u32[]{:S(2)}, u32[]{:S(2)}) collective-permute-start(bf16[16,2048]{1,0:T(8,128)(2,1)S(1)} %get-tuple-element.62), channel_id=1, source_target_pairs={{0,2},{1,3},{2,0},{3,1},{4,6},{5,7},{6,4},{7,5},{8,10},{9,11},{10,... | collective-permute-start | bytes 196616 | tf_op jit(solution)/shard_map/ppermute | solution.py:26
  52.7 6.4 %collective-permute-start.21 = (bf16[16,2048]{1,0:T(8,128)(2,1)S(1)}, bf16[16,2048]{1,0:T(8,128)(2,1)S(1)}, u32[]{:S(2)}, u32[]{:S(2)}) collective-permute-start(bf16[16,2048]{1,0:T(8,128)(2,1)S(1)} %get-tuple-element.61), channel_id=1, source_target_pairs={{0,3},{1,2},{2,1},{3,0},{4,7},{5,6},{6,5},{7,4},{8,11},{9,10},{10,... | collective-permute-start | bytes 196616 | tf_op jit(solution)/shard_map/ppermute | solution.py:26
  55.1 4.5 %collective-permute-start.17 = (bf16[16,2048]{1,0:T(8,128)(2,1)S(1)}, bf16[16,2048]{1,0:T(8,128)(2,1)S(1)}, u32[]{:S(2)}, u32[]{:S(2)}) collective-permute-start(bf16[16,2048]{1,0:T(8,128)(2,1)S(1)} %get-tuple-element.57), channel_id=1, source_target_pairs={{0,1},{1,0},{2,3},{3,2},{4,5},{5,4},{6,7},{7,6},{8,9},{9,8},{10,11... | collective-permute-start | bytes 196616 | tf_op jit(solution)/shard_map/ppermute | solution.py:26

commit v7 on v6

--- a/solution.py
+++ b/solution.py
@@ -37,8 +37,9 @@
     def source(cols):
         return jnp.concatenate([src_up[:, cols], src[:, cols], src_down[:, cols]], axis=0)
 
-    rows = jnp.concatenate([oper_up[...], oper[...].astype(jnp.float32), oper_down[...]], axis=0)
-    basis = jnp.dot(rows.astype(jnp.bfloat16), moved[...], preferred_element_type=jnp.float32).astype(jnp.bfloat16)
+    outer = jnp.concatenate([oper_up[...], oper_down[...]], axis=0).astype(jnp.bfloat16)
+    outer = jnp.dot(outer, moved[...], preferred_element_type=jnp.float32)
+    basis = jnp.concatenate([outer[:HALO], oper[...].astype(jnp.float32), outer[HALO:]], axis=0).astype(jnp.bfloat16)
     at = lax.broadcasted_iota(jnp.int32, (tall, TILE), 0) - HALO + slab * depth
     inside = jnp.logical_and(at >= 0, at < n_slab * depth)
     for n in range(0, width, TILE):
@@ -75,8 +76,8 @@
 
 
 def stage_kernel(order, n_freq, n_slab, tile, where, oper, oper_other, *refs):
-    count = (len(refs) - 4) // 2
-    moved, turned, sems, upright = refs[-4:]
+    count = (len(refs) - 5) // 2
+    moved, turned, basis, sems, upright = refs[-5:]
     copies = [pltpu.make_async_copy(refs[i], refs[count + i], sems.at[i]) for i in range(count)]
     for copy in copies:
         copy.start()
@@ -91,6 +92,7 @@
     for n in range(0, size, step):
         row = lax.broadcasted_iota(jnp.int32, (step, size), 0) + n
         moved[n : n + step, :] = jnp.where(row == held, 1.0, 0.0).astype(jnp.bfloat16)
+    basis[...] = jnp.dot(oper[...], moved[...], preferred_element_type=jnp.float32).astype(jnp.bfloat16)
     core, chip = lax.rem(freq, 2), lax.div(freq, 2)
     half = n_slab * tile
     depth = oper.shape[0]
@@ -112,7 +114,7 @@
 def stage(where, order, n_freq, n_slab, tile, oper, oper_other, *arrays):
     size, depth = oper.shape[1], oper.shape[0]
     results = [pltpu.VMEM(a.shape, a.dtype) for a in arrays]
-    results += [pltpu.VMEM((size, size), jnp.bfloat16), pltpu.VMEM((size // 2, 2 * depth), jnp.bfloat16)]
+    results += [pltpu.VMEM((size, size), jnp.bfloat16), pltpu.VMEM((size // 2, 2 * depth), jnp.bfloat16), pltpu.VMEM((depth, size), jnp.bfloat16)]
     held = sum(a.size * a.dtype.itemsize for a in arrays) + 2 * size * size + 2 * size * depth
     return pl.pallas_call(
         functools.partial(stage_kernel, order, n_freq, n_slab, tile),
@@ -191,7 +193,7 @@
 
     tile = fine_model.shape[0]
     order = [(2 * m + b, j) for m in range(n_chips) for b in range(2) for j in range(n_slab)]
-    lateral, src, rec, moved, turned = stage(where, order, n_freq, n_slab, tile, oper, oper_other, lateral, src, rec)
+    lateral, src, rec, moved, turned, basis = stage(where, order, n_freq, n_slab, tile, oper, oper_other, lateral, src, rec)
     near, far, plane[1] = lax.optimization_barrier((near, far, plane[1]))
     above = jnp.where(odd, near, far)
     below = jnp.where(odd, far, near)
@@ -214,7 +216,7 @@
         cost_estimate=cost(2 * (SWEEPS - 1) * tall * width * width, 2 * width * width),
         name="solve",
     )(
-        where, shift, *blocks, oper, above[:, width:], below[:, width:], src, above[:, :width], below[:, :width],
+        where, shift, *blocks, basis, above[:, width:], below[:, width:], src, above[:, :width], below[:, :width],
         rec, lateral, moved,
     )
     tile = n_fine // (n_freq * n_slab)

time: 60.6 us -> 60.6 us (level)
  no operation moved by 1% of the time
where the time goes in v7:
time: 60.6 us; the launch traced here: 60.3 us
  starting transfers between devices  24.3 us (40%)
  Pallas kernels  16.2 us (27%)
  waiting for transfers between devices  15.2 us (25%)
  other arithmetic  2.03 us (3%)
  local copies, waits for them, and re-layouts  1.77 us (3%)
  between operations  0.84 us (1%)
    ppermute x21, starting transfers between devices, xor_permute(): return lax.ppermute(value, axis, [(i, i ^ mask) for i in range(size)])  23.6 us
    ppermute x21, waiting for transfers between devices, xor_permute(): return lax.ppermute(value, axis, [(i, i ^ mask) for i in range(size)])  15.2 us
    pallas_call x1, Pallas kernels, shards(): pl.pallas_call(functools.partial(solve_kernel, len(blocks), n_slab), out_...  10.5 us
    pallas_call x1, Pallas kernels, stage(): pl.pallas_call(functools.partial(stage_kernel, order, n_freq, n_slab, til...  5.18 us
  transfers between devices with their start and end apart: 23, of which 13 were waited for; matrix products, arithmetic and copies ran while one was open for 5% of the time, Pallas kernels for 9%

profile of v7, /device:TPU:0, one launch (start us, length us, event | category | flops | bytes accessed | tf_op | source)
XLA Modules:
  0.0 60.3 jit_solution(14404408416191496234)
XLA Ops:
  0.0 3.0 %collective-permute-start = (bf16[16,2048]{1,0:T(8,128)(2,1)}, bf16[16,2048]{1,0:T(8,128)(2,1)S(1)}, u32[]{:S(2)}, u32[]{:S(2)}) collective-permute-start(bf16[16,2048]{1,0:T(8,128)(2,1)} %param.6), channel_id=1, source_target_pairs={{0,1},{1,0},{2,3},{3,2},{4,5},{5,4},{6,7},{7,6},{8,9},{9,8},{10,11... | collective-permute-start | bytes 196616 | tf_op jit(solution)/shard_map/ppermute | solution.py:26
  3.0 2.6 %collective-permute-start.1 = (bf16[16,2048]{1,0:T(8,128)(2,1)}, bf16[16,2048]{1,0:T(8,128)(2,1)S(1)}, u32[]{:S(2)}, u32[]{:S(2)}) collective-permute-start(bf16[16,2048]{1,0:T(8,128)(2,1)} %param.6), channel_id=1, source_target_pairs={{0,2},{1,3},{2,0},{3,1},{4,6},{5,7},{6,4},{7,5},{8,10},{9,11},{10,... | collective-permute-start | bytes 196616 | tf_op jit(solution)/shard_map/ppermute | solution.py:26
  5.6 0.0 collective-permute-start.2
  5.6 0.0 collective-permute-start.3
  5.6 0.7 %bitcast_convert_fusion = (f32[8,512]{1,0:T(8,128)S(1)}, f32[8,512]{1,0:T(8,128)S(1)}) fusion(bf16[1,128,512]{2,1,0:T(8,128)(2,1)} %param.7), kind=kLoop, calls=%fused_computation.13 | loop fusion | flops 8192 | bytes 49152 | tf_op jit(solution)/shard_map/convert_element_type | solution.py:181
  6.3 0.9 %slice_bitcast_fusion = (f32[8,2048]{1,0:T(8,128)S(1)}, f32[8,2048]{1,0:T(8,128)S(1)}) fusion(f32[1,128,2048]{2,1,0:T(8,128)} %param.10), kind=kLoop, calls=%fused_computation.3 | loop fusion | bytes 262144 | tf_op jit(solution)/shard_map/slice | solution.py:181
  7.2 0.8 %constant_dynamic-update-slice_fusion.3 = bf16[64,2048]{1,0:T(8,128)(2,1)S(1)} fusion(bf16[16,2048]{1,0:T(8,128)(2,1)} %param.6), kind=kLoop, calls=%fused_computation.12 | loop fusion | bytes 131072
  8.7 0.0 collective-permute-done
  8.8 1.8 %collective-permute-done.1 = bf16[16,2048]{1,0:T(8,128)(2,1)S(1)} collective-permute-done((bf16[16,2048]{1,0:T(8,128)(2,1)}, bf16[16,2048]{1,0:T(8,128)(2,1)S(1)}, u32[]{:S(2)}, u32[]{:S(2)}) %collective-permute-start.1) | collective-permute-done | bytes 65568 | tf_op jit(solution)/shard_map/ppermute | solution.py:26
  10.5 1.4 %collective-permute-done.2 = bf16[16,2048]{1,0:T(8,128)(2,1)S(1)} collective-permute-done((bf16[16,2048]{1,0:T(8,128)(2,1)}, bf16[16,2048]{1,0:T(8,128)(2,1)S(1)}, u32[]{:S(2)}, u32[]{:S(2)}) %collective-permute-start.2) | collective-permute-done | bytes 65568 | tf_op jit(solution)/shard_map/ppermute | solution.py:26
  11.9 0.0 collective-permute-done.3.oper_other
  11.9 0.0 copy-start.1
  12.0 1.6 %collective-permute-start.7 = (bf16[64,2048]{1,0:T(8,128)(2,1)S(1)}, bf16[64,2048]{1,0:T(8,128)(2,1)S(1)}, u32[]{:S(2)}, u32[]{:S(2)}) collective-permute-start(bf16[64,2048]{1,0:T(8,128)(2,1)S(1)} %constant_dynamic-update-slice_fusion.refs_0_), channel_id=1, source_target_pairs={{0,8},{4,12},{8,0},{12,4},{16,24},{20,28},{24,16},{28,20},{1,9},{5... | collective-permute-start | bytes 786440 | tf_op jit(solution)/shard_map/ppermute | solution.py:26
  13.5 1.5 %collective-permute-start.9 = (bf16[64,2048]{1,0:T(8,128)(2,1)S(1)}, bf16[64,2048]{1,0:T(8,128)(2,1)S(1)}, u32[]{:S(2)}, u32[]{:S(2)}) collective-permute-start(bf16[64,2048]{1,0:T(8,128)(2,1)S(1)} %constant_dynamic-update-slice_fusion.refs_0_), channel_id=1, source_target_pairs={{0,16},{4,20},{8,24},{12,28},{16,0},{20,4},{24,8},{28,12},{1,17},{... | collective-permute-start | bytes 786440 | tf_op jit(solution)/shard_map/ppermute | solution.py:26
  15.0 0.5 collective-permute-start.11
  15.5 0.1 collective-permute-start.5
  15.6 0.7 %collective-permute-start.6 = (f32[8,2560]{1,0:T(8,128)S(1)}, f32[8,2560]{1,0:T(8,128)S(1)}, u32[]{:S(2)}, u32[]{:S(2)}) collective-permute-start(f32[8,2560]{1,0:T(8,128)S(1)} %get-tuple-element.69), channel_id=1, source_target_pairs={{1,2},{2,1},{5,6},{6,5},{9,10},{10,9},{13,14},{14,13},{17,18},{18,... | collective-permute-start | bytes 245768 | tf_op jit(solution)/shard_map/ppermute | solution.py:191
  16.3 0.6 pad_add_fusion.where
  16.9 0.0 copy-done.1
  16.9 0.0 copy-start
  16.9 5.2 %stage.1 = (bf16[2048,2048]{1,0:T(8,128)(2,1)S(1)}, f32[128,2048]{1,0:T(8,128)S(1)}, f32[128,2048]{1,0:T(8,128)S(1)}, bf16[512,512]{1,0:T(8,128)(2,1)S(1)}, bf16...) custom-call(s32[2]{0:T(128)} %pad_add_fusion.where, bf16[128,512]{1,0:T(8,128)(2,1)} %bitcast.18, ...), custom_call_target="tpu_custom_call" | custom-call | bytes 22282240 | tf_op jit(solution)/shard_map/stage/pallas_call | solution.py:119
  22.1 0.0 collective-permute-done.5
  22.1 0.1 collective-permute-start.4
  22.2 0.0 collective-permute-done.6
  22.2 0.0 collective-permute-done.7.refs_2_
  22.2 0.5 collective-permute-start.8
  22.7 2.6 %collective-permute-done.9.refs_4_ = bf16[64,2048]{1,0:T(8,128)(2,1)S(1)} collective-permute-done((bf16[64,2048]{1,0:T(8,128)(2,1)S(1)}, bf16[64,2048]{1,0:T(8,128)(2,1)S(1)}, u32[]{:S(2)}, u32[]{:S(2)}) %collective-permute-start.9) | collective-permute-done | bytes 262176 | tf_op jit(solution)/shard_map/ppermute | solution.py:26
  25.3 0.0 collective-permute-start.10
  25.3 0.0 collective-permute-done.11.refs_6_
  25.3 0.5 collective-permute-start.12
  25.8 0.0 collective-permute-done.4.refs_1_
  25.9 0.0 collective-permute-done.8.refs_3_
  25.9 0.9 %collective-permute-done.10.refs_5_ = bf16[64,2048]{1,0:T(8,128)(2,1)S(1)} collective-permute-done((bf16[64,2048]{1,0:T(8,128)(2,1)S(1)}, bf16[64,2048]{1,0:T(8,128)(2,1)S(1)}, u32[]{:S(2)}, u32[]{:S(2)}) %collective-permute-start.10) | collective-permute-done | bytes 262176 | tf_op jit(solution)/shard_map/ppermute | solution.py:26
  26.8 0.4 collective-permute-done.12.refs_7_
  27.2 0.0 copy-done
  27.2 10.5 %solve.1.part = bf16[128,2048]{1,0:T(8,128)(2,1)S(1)} custom-call(s32[2]{0:T(128)S(1)} %copy-done, f32[1]{0:T(128)S(6)} %copy.10.factor, bf16[64,2048]{1,0:T(8,128)(2,1)S(1)} %constant_dynamic-update-slice_fusion.refs_0_, bf16[64,2048]{1,0:T(8,128)(2,1)S(1)} %collective-permute-done.4.refs_1_, bf16[64,2048]{1,0:T(8,128)(2,1)S(1)} %collective-permute-done.7.refs_2_, ...), custom_call_target="tpu_custom_call" | custom-call | flops 8455716864 | bytes 8388608 | tf_op jit(solution)/shard_map/solve/pallas_call | solution.py:204
  37.7 0.2 collective-permute-start.13
  37.9 1.8 %collective-permute-done.13.part_other = bf16[128,2048]{1,0:T(8,128)(2,1)S(1)} collective-permute-done((bf16[128,2048]{1,0:T(8,128)(2,1)S(1)}, bf16[128,2048]{1,0:T(8,128)(2,1)S(1)}, u32[]{:S(2)}, u32[]{:S(2)}) %collective-permute-start.13) | collective-permute-done | bytes 524320 | tf_op jit(solution)/shard_map/ppermute | solution.py:26
  39.6 0.4 back.1
  40.1 1.6 %collective-permute-start.18 = (bf16[32,2048]{1,0:T(8,128)(2,1)S(1)}, bf16[32,2048]{1,0:T(8,128)(2,1)S(1)}, u32[]{:S(2)}, u32[]{:S(2)}) collective-permute-start(bf16[32,2048]{1,0:T(8,128)(2,1)S(1)} %get-tuple-element.60), channel_id=1, source_target_pairs={{0,24},{4,28},{8,16},{12,20},{16,8},{20,12},{24,0},{28,4},{1,25},{... | collective-permute-start | bytes 393224 | tf_op jit(solution)/shard_map/ppermute | solution.py:26
  41.7 0.8 %collective-permute-start.19 = (bf16[32,2048]{1,0:T(8,128)(2,1)S(1)}, bf16[32,2048]{1,0:T(8,128)(2,1)S(1)}, u32[]{:S(2)}, u32[]{:S(2)}) collective-permute-start(bf16[32,2048]{1,0:T(8,128)(2,1)S(1)} %get-tuple-element.61), channel_id=1, source_target_pairs={{0,16},{4,20},{8,24},{12,28},{16,0},{20,4},{24,8},{28,12},{1,17},{... | collective-permute-start | bytes 393224 | tf_op jit(solution)/shard_map/ppermute | solution.py:26
  42.5 1.2 %collective-permute-start.20 = (bf16[32,2048]{1,0:T(8,128)(2,1)S(1)}, bf16[32,2048]{1,0:T(8,128)(2,1)S(1)}, u32[]{:S(2)}, u32[]{:S(2)}) collective-permute-start(bf16[32,2048]{1,0:T(8,128)(2,1)S(1)} %get-tuple-element.62), channel_id=1, source_target_pairs={{0,8},{4,12},{8,0},{12,4},{16,24},{20,28},{24,16},{28,20},{1,9},{5... | collective-permute-start | bytes 393224 | tf_op jit(solution)/shard_map/ppermute | solution.py:26
  43.6 0.9 %collective-permute-start.14 = (bf16[32,2048]{1,0:T(8,128)(2,1)S(1)}, bf16[32,2048]{1,0:T(8,128)(2,1)S(1)}, u32[]{:S(2)}, u32[]{:S(2)}) collective-permute-start(bf16[32,2048]{1,0:T(8,128)(2,1)S(1)} %get-tuple-element.55), channel_id=1, source_target_pairs={{0,8},{4,12},{8,0},{12,4},{16,24},{20,28},{24,16},{28,20},{1,9},{5... | collective-permute-start | bytes 393224 | tf_op jit(solution)/shard_map/ppermute | solution.py:26
  44.5 1.2 %collective-permute-start.15 = (bf16[32,2048]{1,0:T(8,128)(2,1)S(1)}, bf16[32,2048]{1,0:T(8,128)(2,1)S(1)}, u32[]{:S(2)}, u32[]{:S(2)}) collective-permute-start(bf16[32,2048]{1,0:T(8,128)(2,1)S(1)} %get-tuple-element.56), channel_id=1, source_target_pairs={{0,16},{4,20},{8,24},{12,28},{16,0},{20,4},{24,8},{28,12},{1,17},{... | collective-permute-start | bytes 393224 | tf_op jit(solution)/shard_map/ppermute | solution.py:26
  45.7 1.7 %collective-permute-done.18.refs_0_ = bf16[32,2048]{1,0:T(8,128)(2,1)S(1)} collective-permute-done((bf16[32,2048]{1,0:T(8,128)(2,1)S(1)}, bf16[32,2048]{1,0:T(8,128)(2,1)S(1)}, u32[]{:S(2)}, u32[]{:S(2)}) %collective-permute-start.18) | collective-permute-done | bytes 131104 | tf_op jit(solution)/shard_map/ppermute | solution.py:26
  47.4 1.5 %collective-permute-start.16 = (bf16[32,2048]{1,0:T(8,128)(2,1)S(1)}, bf16[32,2048]{1,0:T(8,128)(2,1)S(1)}, u32[]{:S(2)}, u32[]{:S(2)}) collective-permute-start(bf16[32,2048]{1,0:T(8,128)(2,1)S(1)} %get-tuple-element.57), channel_id=1, source_target_pairs={{0,24},{4,28},{8,16},{12,20},{16,8},{20,12},{24,0},{28,4},{1,25},{... | collective-permute-start | bytes 393224 | tf_op jit(solution)/shard_map/ppermute | solution.py:26
  49.0 0.5 collective-permute-done.19.refs_1_
  49.5 0.8 %collective-permute-done.20.refs_2_ = bf16[32,2048]{1,0:T(8,128)(2,1)S(1)} collective-permute-done((bf16[32,2048]{1,0:T(8,128)(2,1)S(1)}, bf16[32,2048]{1,0:T(8,128)(2,1)S(1)}, u32[]{:S(2)}, u32[]{:S(2)}) %collective-permute-start.20) | collective-permute-done | bytes 131104 | tf_op jit(solution)/shard_map/ppermute | solution.py:26
  50.3 0.1 plane.3
  50.4 2.4 %collective-permute-start.22 = (bf16[16,2048]{1,0:T(8,128)(2,1)S(1)}, bf16[16,2048]{1,0:T(8,128)(2,1)S(1)}, u32[]{:S(2)}, u32[]{:S(2)}) collective-permute-start(bf16[16,2048]{1,0:T(8,128)(2,1)S(1)} %get-tuple-element.64), channel_id=1, source_target_pairs={{0,2},{1,3},{2,0},{3,1},{4,6},{5,7},{6,4},{7,5},{8,10},{9,11},{10,... | collective-permute-start | bytes 196616 | tf_op jit(solution)/shard_map/ppermute | solution.py:26
  52.8 1.8 %collective-permute-start.21 = (bf16[16,2048]{1,0:T(8,128)(2,1)S(1)}, bf16[16,2048]{1,0:T(8,128)(2,1)S(1)}, u32[]{:S(2)}, u32[]{:S(2)}) collective-permute-start(bf16[16,2048]{1,0:T(8,128)(2,1)S(1)} %get-tuple-element.63), channel_id=1, source_target_pairs={{0,3},{1,2},{2,1},{3,0},{4,7},{5,6},{6,5},{7,4},{8,11},{9,10},{10,... | collective-permute-start | bytes 196616 | tf_op jit(solution)/shard_map/ppermute | solution.py:26
  54.5 0.0 collective-permute-done.14.refs_0_
  54.5 0.0 collective-permute-done.15.refs_1_
  54.5 0.5 collective-permute-done.16.refs_2_
  55.0 0.1 plane.2
  55.1 1.8 %collective-permute-start.17 = (bf16[16,2048]{1,0:T(8,128)(2,1)S(1)}, bf16[16,2048]{1,0:T(8,128)(2,1)S(1)}, u32[]{:S(2)}, u32[]{:S(2)}) collective-permute-start(bf16[16,2048]{1,0:T(8,128)(2,1)S(1)} %get-tuple-element.59), channel_id=1, source_target_pairs={{0,1},{1,0},{2,3},{3,2},{4,5},{5,4},{6,7},{7,6},{8,9},{9,8},{10,11... | collective-permute-start | bytes 196616 | tf_op jit(solution)/shard_map/ppermute | solution.py:26
  56.9 0.8 %collective-permute-done.22 = bf16[16,2048]{1,0:T(8,128)(2,1)S(1)} collective-permute-done((bf16[16,2048]{1,0:T(8,128)(2,1)S(1)}, bf16[16,2048]{1,0:T(8,128)(2,1)S(1)}, u32[]{:S(2)}, u32[]{:S(2)}) %collective-permute-start.22) | collective-permute-done | bytes 65568 | tf_op jit(solution)/shard_map/ppermute | solution.py:26
  57.7 1.4 %collective-permute-done.21 = bf16[16,2048]{1,0:T(8,128)(2,1)S(1)} collective-permute-done((bf16[16,2048]{1,0:T(8,128)(2,1)S(1)}, bf16[16,2048]{1,0:T(8,128)(2,1)S(1)}, u32[]{:S(2)}, u32[]{:S(2)}) %collective-permute-start.21) | collective-permute-done | bytes 65568 | tf_op jit(solution)/shard_map/ppermute | solution.py:26
  59.2 0.5 collective-permute-done.17
  59.7 0.7 %convert_add_fusion = f32[16,2048]{1,0:T(8,128)} fusion(bf16[16,2048]{1,0:T(8,128)(2,1)S(1)} %collective-permute-done.22, bf16[16,2048]{1,0:T(8,128)(2,1)S(1)} %collective-permute-done.21, f32[16,2048]{1,0:T(8,128)S(1)} %get-tuple-element.58, bf16[16,2048]{1,0:T(8,128)(2,1)S(1)} %collective-permute-done.17), kind=kLoop, calls=%fused_computation | loop fusion | flops 196608 | bytes 458752 | tf_op jit(solution)/shard_map/add | solution.py:230
  (10 shorter events, 0.1 us)
Async XLA Ops:
  0.0 8.7 %collective-permute-start = (bf16[16,2048]{1,0:T(8,128)(2,1)}, bf16[16,2048]{1,0:T(8,128)(2,1)S(1)}, u32[]{:S(2)}, u32[]{:S(2)}) collective-permute-start(bf16[16,2048]{1,0:T(8,128)(2,1)} %param.6), channel_id=1, source_target_pairs={{0,1},{1,0},{2,3},{3,2},{4,5},{5,4},{6,7},{7,6},{8,9},{9,8},{10,11... | collective-permute-start | bytes 196616 | tf_op jit(solution)/shard_map/ppermute | solution.py:26
  3.0 7.5 %collective-permute-start.1 = (bf16[16,2048]{1,0:T(8,128)(2,1)}, bf16[16,2048]{1,0:T(8,128)(2,1)S(1)}, u32[]{:S(2)}, u32[]{:S(2)}) collective-permute-start(bf16[16,2048]{1,0:T(8,128)(2,1)} %param.6), channel_id=1, source_target_pairs={{0,2},{1,3},{2,0},{3,1},{4,6},{5,7},{6,4},{7,5},{8,10},{9,11},{10,... | collective-permute-start | bytes 196616 | tf_op jit(solution)/shard_map/ppermute | solution.py:26
  5.6 6.3 %collective-permute-start.2 = (bf16[16,2048]{1,0:T(8,128)(2,1)}, bf16[16,2048]{1,0:T(8,128)(2,1)S(1)}, u32[]{:S(2)}, u32[]{:S(2)}) collective-permute-start(bf16[16,2048]{1,0:T(8,128)(2,1)} %param.6), channel_id=1, source_target_pairs={{0,3},{1,2},{2,1},{3,0},{4,7},{5,6},{6,5},{7,4},{8,11},{9,10},{10,... | collective-permute-start | bytes 196616 | tf_op jit(solution)/shard_map/ppermute | solution.py:26
  5.6 6.3 %collective-permute-start.3 = (bf16[128,512]{1,0:T(8,128)(2,1)}, bf16[128,512]{1,0:T(8,128)(2,1)S(1)}, u32[]{:S(2)}, u32[]{:S(2)}) collective-permute-start(bf16[128,512]{1,0:T(8,128)(2,1)} %bitcast.17), channel_id=1, source_target_pairs={{0,4},{4,0},{8,12},{12,8},{16,20},{20,16},{24,28},{28,24},{1,5},{5... | collective-permute-start | bytes 393224 | tf_op jit(solution)/shard_map/ppermute | solution.py:26
  11.9 4.9 %copy-start.1 = (bf16[128,512]{1,0:T(8,128)(2,1)}, bf16[128,512]{1,0:T(8,128)(2,1)S(1)}, u32[]{:S(2)}) copy-start(bf16[128,512]{1,0:T(8,128)(2,1)S(1)} %collective-permute-done.3.oper_other) | copy-start | bytes 393220
  12.0 10.2 %collective-permute-start.7 = (bf16[64,2048]{1,0:T(8,128)(2,1)S(1)}, bf16[64,2048]{1,0:T(8,128)(2,1)S(1)}, u32[]{:S(2)}, u32[]{:S(2)}) collective-permute-start(bf16[64,2048]{1,0:T(8,128)(2,1)S(1)} %constant_dynamic-update-slice_fusion.refs_0_), channel_id=1, source_target_pairs={{0,8},{4,12},{8,0},{12,4},{16,24},{20,28},{24,16},{28,20},{1,9},{5... | collective-permute-start | bytes 786440 | tf_op jit(solution)/shard_map/ppermute | solution.py:26
  13.5 11.7 %collective-permute-start.9 = (bf16[64,2048]{1,0:T(8,128)(2,1)S(1)}, bf16[64,2048]{1,0:T(8,128)(2,1)S(1)}, u32[]{:S(2)}, u32[]{:S(2)}) collective-permute-start(bf16[64,2048]{1,0:T(8,128)(2,1)S(1)} %constant_dynamic-update-slice_fusion.refs_0_), channel_id=1, source_target_pairs={{0,16},{4,20},{8,24},{12,28},{16,0},{20,4},{24,8},{28,12},{1,17},{... | collective-permute-start | bytes 786440 | tf_op jit(solution)/shard_map/ppermute | solution.py:26
  15.0 10.2 %collective-permute-start.11 = (bf16[64,2048]{1,0:T(8,128)(2,1)S(1)}, bf16[64,2048]{1,0:T(8,128)(2,1)S(1)}, u32[]{:S(2)}, u32[]{:S(2)}) collective-permute-start(bf16[64,2048]{1,0:T(8,128)(2,1)S(1)} %constant_dynamic-update-slice_fusion.refs_0_), channel_id=1, source_target_pairs={{0,24},{4,28},{8,16},{12,20},{16,8},{20,12},{24,0},{28,4},{1,25},{... | collective-permute-start | bytes 786440 | tf_op jit(solution)/shard_map/ppermute | solution.py:26
  15.5 6.5 %collective-permute-start.5 = (f32[8,2560]{1,0:T(8,128)S(1)}, f32[8,2560]{1,0:T(8,128)S(1)}, u32[]{:S(2)}, u32[]{:S(2)}) collective-permute-start(f32[8,2560]{1,0:T(8,128)S(1)} %get-tuple-element.70), channel_id=1, source_target_pairs={{0,1},{1,0},{2,3},{3,2},{4,5},{5,4},{6,7},{7,6},{8,9},{9,8},{10,11... | collective-permute-start | bytes 245768 | tf_op jit(solution)/shard_map/ppermute | solution.py:192
  15.6 6.5 %collective-permute-start.6 = (f32[8,2560]{1,0:T(8,128)S(1)}, f32[8,2560]{1,0:T(8,128)S(1)}, u32[]{:S(2)}, u32[]{:S(2)}) collective-permute-start(f32[8,2560]{1,0:T(8,128)S(1)} %get-tuple-element.69), channel_id=1, source_target_pairs={{1,2},{2,1},{5,6},{6,5},{9,10},{10,9},{13,14},{14,13},{17,18},{18,... | collective-permute-start | bytes 245768 | tf_op jit(solution)/shard_map/ppermute | solution.py:191
  16.9 10.3 %copy-start = (s32[2]{0:T(128)S(1)}, s32[2]{0:T(128)}, u32[]{:S(2)}) copy-start(s32[2]{0:T(128)} %pad_add_fusion.where) | copy-start | bytes 28
  22.1 3.8 %collective-permute-start.4 = (bf16[64,2048]{1,0:T(8,128)(2,1)S(1)}, bf16[64,2048]{1,0:T(8,128)(2,1)S(1)}, u32[]{:S(2)}, u32[]{:S(2)}) collective-permute-start(bf16[64,2048]{1,0:T(8,128)(2,1)S(1)} %constant_dynamic-update-slice_fusion.refs_0_), channel_id=1, source_target_pairs={{0,4},{4,0},{8,12},{12,8},{16,20},{20,16},{24,28},{28,24},{1,5},{5... | collective-permute-start | bytes 786440 | tf_op jit(solution)/shard_map/ppermute | solution.py:26
  22.2 3.7 %collective-permute-start.8 = (bf16[64,2048]{1,0:T(8,128)(2,1)S(1)}, bf16[64,2048]{1,0:T(8,128)(2,1)S(1)}, u32[]{:S(2)}, u32[]{:S(2)}) collective-permute-start(bf16[64,2048]{1,0:T(8,128)(2,1)S(1)} %collective-permute-done.7.refs_2_), channel_id=1, source_target_pairs={{0,4},{4,0},{8,12},{12,8},{16,20},{20,16},{24,28},{28,24},{1,5},{5... | collective-permute-start | bytes 786440 | tf_op jit(solution)/shard_map/ppermute | solution.py:26
  25.3 1.5 %collective-permute-start.10 = (bf16[64,2048]{1,0:T(8,128)(2,1)S(1)}, bf16[64,2048]{1,0:T(8,128)(2,1)S(1)}, u32[]{:S(2)}, u32[]{:S(2)}) collective-permute-start(bf16[64,2048]{1,0:T(8,128)(2,1)S(1)} %collective-permute-done.9.refs_4_), channel_id=1, source_target_pairs={{0,4},{4,0},{8,12},{12,8},{16,20},{20,16},{24,28},{28,24},{1,5},{5... | collective-permute-start | bytes 786440 | tf_op jit(solution)/shard_map/ppermute | solution.py:26
  25.3 1.9 %collective-permute-start.12 = (bf16[64,2048]{1,0:T(8,128)(2,1)S(1)}, bf16[64,2048]{1,0:T(8,128)(2,1)S(1)}, u32[]{:S(2)}, u32[]{:S(2)}) collective-permute-start(bf16[64,2048]{1,0:T(8,128)(2,1)S(1)} %collective-permute-done.11.refs_6_), channel_id=1, source_target_pairs={{0,4},{4,0},{8,12},{12,8},{16,20},{20,16},{24,28},{28,24},{1,5},{5... | collective-permute-start | bytes 786440 | tf_op jit(solution)/shard_map/ppermute | solution.py:26
  37.7 2.0 %collective-permute-start.13 = (bf16[128,2048]{1,0:T(8,128)(2,1)S(1)}, bf16[128,2048]{1,0:T(8,128)(2,1)S(1)}, u32[]{:S(2)}, u32[]{:S(2)}) collective-permute-start(bf16[128,2048]{1,0:T(8,128)(2,1)S(1)} %solve.1.part), channel_id=1, source_target_pairs={{0,4},{4,0},{8,12},{12,8},{16,20},{20,16},{24,28},{28,24},{1,5},{5... | collective-permute-start | bytes 1572872 | tf_op jit(solution)/shard_map/ppermute | solution.py:26
  40.1 7.3 %collective-permute-start.18 = (bf16[32,2048]{1,0:T(8,128)(2,1)S(1)}, bf16[32,2048]{1,0:T(8,128)(2,1)S(1)}, u32[]{:S(2)}, u32[]{:S(2)}) collective-permute-start(bf16[32,2048]{1,0:T(8,128)(2,1)S(1)} %get-tuple-element.60), channel_id=1, source_target_pairs={{0,24},{4,28},{8,16},{12,20},{16,8},{20,12},{24,0},{28,4},{1,25},{... | collective-permute-start | bytes 393224 | tf_op jit(solution)/shard_map/ppermute | solution.py:26
  41.7 7.8 %collective-permute-start.19 = (bf16[32,2048]{1,0:T(8,128)(2,1)S(1)}, bf16[32,2048]{1,0:T(8,128)(2,1)S(1)}, u32[]{:S(2)}, u32[]{:S(2)}) collective-permute-start(bf16[32,2048]{1,0:T(8,128)(2,1)S(1)} %get-tuple-element.61), channel_id=1, source_target_pairs={{0,16},{4,20},{8,24},{12,28},{16,0},{20,4},{24,8},{28,12},{1,17},{... | collective-permute-start | bytes 393224 | tf_op jit(solution)/shard_map/ppermute | solution.py:26
  42.5 7.8 %collective-permute-start.20 = (bf16[32,2048]{1,0:T(8,128)(2,1)S(1)}, bf16[32,2048]{1,0:T(8,128)(2,1)S(1)}, u32[]{:S(2)}, u32[]{:S(2)}) collective-permute-start(bf16[32,2048]{1,0:T(8,128)(2,1)S(1)} %get-tuple-element.62), channel_id=1, source_target_pairs={{0,8},{4,12},{8,0},{12,4},{16,24},{20,28},{24,16},{28,20},{1,9},{5... | collective-permute-start | bytes 393224 | tf_op jit(solution)/shard_map/ppermute | solution.py:26
  43.6 10.9 %collective-permute-start.14 = (bf16[32,2048]{1,0:T(8,128)(2,1)S(1)}, bf16[32,2048]{1,0:T(8,128)(2,1)S(1)}, u32[]{:S(2)}, u32[]{:S(2)}) collective-permute-start(bf16[32,2048]{1,0:T(8,128)(2,1)S(1)} %get-tuple-element.55), channel_id=1, source_target_pairs={{0,8},{4,12},{8,0},{12,4},{16,24},{20,28},{24,16},{28,20},{1,9},{5... | collective-permute-start | bytes 393224 | tf_op jit(solution)/shard_map/ppermute | solution.py:26
  44.5 10.0 %collective-permute-start.15 = (bf16[32,2048]{1,0:T(8,128)(2,1)S(1)}, bf16[32,2048]{1,0:T(8,128)(2,1)S(1)}, u32[]{:S(2)}, u32[]{:S(2)}) collective-permute-start(bf16[32,2048]{1,0:T(8,128)(2,1)S(1)} %get-tuple-element.56), channel_id=1, source_target_pairs={{0,16},{4,20},{8,24},{12,28},{16,0},{20,4},{24,8},{28,12},{1,17},{... | collective-permute-start | bytes 393224 | tf_op jit(solution)/shard_map/ppermute | solution.py:26
  47.4 7.6 %collective-permute-start.16 = (bf16[32,2048]{1,0:T(8,128)(2,1)S(1)}, bf16[32,2048]{1,0:T(8,128)(2,1)S(1)}, u32[]{:S(2)}, u32[]{:S(2)}) collective-permute-start(bf16[32,2048]{1,0:T(8,128)(2,1)S(1)} %get-tuple-element.57), channel_id=1, source_target_pairs={{0,24},{4,28},{8,16},{12,20},{16,8},{20,12},{24,0},{28,4},{1,25},{... | collective-permute-start | bytes 393224 | tf_op jit(solution)/shard_map/ppermute | solution.py:26
  50.4 7.4 %collective-permute-start.22 = (bf16[16,2048]{1,0:T(8,128)(2,1)S(1)}, bf16[16,2048]{1,0:T(8,128)(2,1)S(1)}, u32[]{:S(2)}, u32[]{:S(2)}) collective-permute-start(bf16[16,2048]{1,0:T(8,128)(2,1)S(1)} %get-tuple-element.64), channel_id=1, source_target_pairs={{0,2},{1,3},{2,0},{3,1},{4,6},{5,7},{6,4},{7,5},{8,10},{9,11},{10,... | collective-permute-start | bytes 196616 | tf_op jit(solution)/shard_map/ppermute | solution.py:26
  52.8 6.4 %collective-permute-start.21 = (bf16[16,2048]{1,0:T(8,128)(2,1)S(1)}, bf16[16,2048]{1,0:T(8,128)(2,1)S(1)}, u32[]{:S(2)}, u32[]{:S(2)}) collective-permute-start(bf16[16,2048]{1,0:T(8,128)(2,1)S(1)} %get-tuple-element.63), channel_id=1, source_target_pairs={{0,3},{1,2},{2,1},{3,0},{4,7},{5,6},{6,5},{7,4},{8,11},{9,10},{10,... | collective-permute-start | bytes 196616 | tf_op jit(solution)/shard_map/ppermute | solution.py:26
  55.1 4.6 %collective-permute-start.17 = (bf16[16,2048]{1,0:T(8,128)(2,1)S(1)}, bf16[16,2048]{1,0:T(8,128)(2,1)S(1)}, u32[]{:S(2)}, u32[]{:S(2)}) collective-permute-start(bf16[16,2048]{1,0:T(8,128)(2,1)S(1)} %get-tuple-element.59), channel_id=1, source_target_pairs={{0,1},{1,0},{2,3},{3,2},{4,5},{5,4},{6,7},{7,6},{8,9},{9,8},{10,11... | collective-permute-start | bytes 196616 | tf_op jit(solution)/shard_map/ppermute | solution.py:26
